TPU v7x, 128 devices: a whole 4x4x4 slice. The times are simulated.
128 devices in a mesh: dp: 16 (over y, z), frame: 8 (over x, core).
Axes of the slice: x: 4, y: 4, z: 4, core: 2. Of those that a mesh axis runs over, the one named last changes fastest.
Arguments:
- video: bfloat16 [32, 16, 12, 20, 1024], P('dp', 'frame'), may hold values from -6 to 6
- norm_gain: float32 [1024], replicated, may hold values from 0.5 to 1.5
- spatial_weight: bfloat16 [9, 1024, 1024], P(None, 'dp'), may hold values from -0.0625 to 0.0625
- spatial_bias: float32 [1024], replicated, may hold values from -3 to 3
- temporal_weight: bfloat16 [3, 1024, 1024], P(None, 'dp'), may hold values from -0.109375 to 0.109375
Outputs:
- result: bfloat16 [32, 16, 12, 20, 1024], P('dp', 'frame')
All inputs are finite; a program needn't handle non-finite values.
Results may differ from a plain program's by a relative error of at most 0.0033.
Values may be sent and summed in bfloat16 or wider, within the bound.
No kernel may reach another device: no remote copies, remote signals or barrier semaphores. Data moves between devices by JAX's collectives and lax.ppermute only.
A program may use at most 128 MiB of HBM per device.

v0:
```python
import jax
import jax.numpy as jnp
from jax import lax
from jax.sharding import PartitionSpec as P

epsilon = 1e-06


def extended_2(block, sides, width):
    for axis, dim in sides:
        count = lax.axis_size(axis)
        forward = [(i, i + 1) for i in range(count - 1)]
        backward = [(target, source) for source, target in forward]
        low = lax.ppermute(
            lax.slice_in_dim(block, block.shape[dim] - width, None, axis=dim), axis, forward
        )
        high = lax.ppermute(lax.slice_in_dim(block, 0, width, axis=dim), axis, backward)
        block = jnp.concatenate([low, block, high], axis=dim)
    return block


def spatial_conv(inputs, kernel):
    return lax.conv_general_dilated(
        inputs,
        kernel,
        (1, 1),
        ((1, 1), (1, 1)),
        dimension_numbers=("CNHW", "HWIO", "NHWC"),
        preferred_element_type=jnp.float32,
    )


def temporal_conv(inputs, kernel):
    return lax.conv_general_dilated(
        inputs,
        kernel,
        (1, 1),
        ((0, 0), (0, 0)),
        dimension_numbers=("CNHW", "HWIO", "NHWC"),
        preferred_element_type=jnp.float32,
    )


def shards(video, norm_gain, spatial_weight, spatial_bias, temporal_weight):
    batch_dev, frame_dev, height, width_cells, channels = video.shape
    widened = video.astype(jnp.float32)
    scaled = (
        widened
        * lax.rsqrt(jnp.mean(widened * widened, axis=-1, keepdims=True) + epsilon)
        * norm_gain
    )
    active = jax.nn.silu(scaled).astype(jnp.bfloat16)
    channel_first = jnp.transpose(
        active.reshape(batch_dev * frame_dev, height, width_cells, channels), (3, 0, 1, 2)
    )
    empty_space = jnp.zeros((batch_dev * frame_dev, height, width_cells, channels), jnp.float32)
    piece = lax.all_gather(spatial_weight, "dp", axis=1, tiled=True)
    inputs = channel_first
    spatial = empty_space + spatial_conv(
        inputs, piece.reshape(3, 3, piece.shape[1], piece.shape[2])
    )
    hidden = jax.nn.silu(spatial + spatial_bias).astype(jnp.bfloat16)
    hidden_first = jnp.transpose(
        hidden.reshape(batch_dev, frame_dev, height * width_cells, channels), (3, 0, 1, 2)
    )
    extended = extended_2(hidden_first, (("frame", 2),), 1)
    empty_time = jnp.zeros((batch_dev, frame_dev, height * width_cells, channels), jnp.float32)
    piece = lax.all_gather(temporal_weight, "dp", axis=1, tiled=True)
    inputs = extended
    temporal = empty_time + temporal_conv(
        inputs, piece.reshape(3, 1, piece.shape[1], piece.shape[2])
    )
    return (widened + temporal.reshape(video.shape)).astype(jnp.bfloat16)


def solution(mesh):
    in_specs = (
        P("dp", "frame", None, None, None),
        P(),
        P(None, "dp", None),
        P(),
        P(None, "dp", None),
    )
    out_specs = P("dp", "frame", None, None, None)
    return jax.shard_map(shards, mesh=mesh, in_specs=in_specs, out_specs=out_specs, check_vma=False)
```

profile of v0, /device:TPU:1, one launch (start us, length us, event | category | flops | bytes accessed | tf_op | source)
XLA Modules:
  0.0 240.5 jit_solution(3169280156081994170)
XLA Ops:
  6.5 0.0 copy-start
  6.5 0.0 copy-start.2
  6.5 0.0 all-gather.3.cloned.1.call-start
  6.5 0.7 all-gather.3.cloned.1.call-update
  7.3 0.0 all-gather.5.cloned.1.call-start
  7.3 0.7 all-gather.5.cloned.1.call-update
  8.0 3.7 %fusion.3 = f32[2,2,12,20]{1,3,2,0:T(8,128)S(1)} fusion(bf16[2,2,12,20,1024]{4,1,3,2,0:T(2,128)(2,1)} %param.5), kind=kLoop, calls=%fused_computation.9 | loop fusion | flops 2948160 | bytes 1969920 | tf_op jit(solution)/shard_map/reduce_sum | solution.py:49
  11.7 0.3 copy.36
  12.0 0.3 copy.37
  12.3 0.0 copy-done
  12.3 0.0 copy-done.2
  12.3 5.2 %fusion.13 = bf16[2,2,12,20,1024]{4,1,3,2,0:T(2,128)(2,1)S(1)} fusion(bf16[2,2,12,20,1024]{4,1,3,2,0:T(2,128)(2,1)S(1)} %copy-done, f32[1024]{0:T(1024)S(1)} %copy-done.2, f32[2,2,12,20]{1,3,2,0:T(8,128)S(1)} %copy.37), kind=kLoop, calls=%fused_computation.18 | loop fusion | flops 7864320 | bytes 3940096 | tf_op jit(solution)/shard_map/convert_element_type | solution.py:52
  17.5 2.9 %copy.38 = bf16[2,2,12,20,1024]{4,1,0,3,2:T(2,128)(2,1)} copy(bf16[2,2,12,20,1024]{4,1,3,2,0:T(2,128)(2,1)S(1)} %fusion.13) | data formatting | bytes 3932160 | tf_op jit(solution)/shard_map/convert_element_type | solution.py:52
  20.4 4.7 %reshape.25 = bf16[4,12,20,1024]{3,0,2,1:T(4,128)(2,1)S(1)} reshape(bf16[2,2,12,20,1024]{4,1,0,3,2:T(2,128)(2,1)} %copy.38) | data formatting | bytes 3932160 | tf_op jit(solution)/shard_map/reshape | solution.py:54
  25.1 1.1 pad
  26.2 0.8 slice.11
  27.0 0.0 copy-start.3
  27.0 0.0 copy-start.4
  27.0 3.4 %fusion.6 = bf16[12,4,8,5,1024]{4,1,3,2,0:T(4,128)(2,1)} fusion(bf16[12,4,7,2,1024]{4,1,3,2,0:T(4,128)(2,1)S(1)} %slice.11, bf16[12,4,8,3,1024]{4,1,3,2,0:T(4,128)(2,1)S(1)} %bitcast.30), kind=kLoop, calls=%fused_computation.12 | loop fusion | flops 11796480 | bytes 7667712 | tf_op jit(solution)/shard_map/conv_general_dilated | solution.py:23
  30.4 104.6 %all-gather.3.cloned.1.call-done = bf16[9,1024,1024]{2,1,0:T(8,128)(2,1)} async-done(((bf16[9,64,1024]{2,1,0:T(8,128)(2,1)}), bf16[9,1024,1024]{2,1,0:T(8,128)(2,1)}) %all-gather.3.cloned.1.call-update) | async-done | bytes 18874384 | tf_op jit(solution)/shard_map/all_gather | solution.py:57
  135.0 0.0 copy-done.3
  135.0 0.0 copy-done.4
  135.0 28.2 %multiply_convert_fusion = bf16[12,32,3,1024]{3,1,2,0:T(8,128)(2,1)S(1)} fusion(bf16[3,3,1024,1024]{3,2,1,0:T(8,128)(2,1)} %bitcast.34, bf16[12,4,8,5,1024]{4,1,3,2,0:T(4,128)(2,1)} %fusion.6, f32[1024]{0:T(1024)S(1)} %copy-done.3, pred[32,3]{0,1:T(4,128)(4,1)S(1)} %copy-done.4), kind=kOutput, calls=%fused_computation.7 | convolution fusion | flops 20543569920 | bytes 25170016 | tf_op jit(solution)/shard_map/conv_general_dilated | solution.py:23
  163.2 2.0 copy.40
  165.2 4.1 %reshape.36 = bf16[12,4,24,1024]{3,2,1,0:T(8,128)(2,1)} reshape(bf16[12,32,3,1024]{3,2,1,0:T(4,128)(2,1)S(1)} %copy.40) | data formatting | bytes 4718592 | tf_op jit(solution)/shard_map/convert_element_type | solution.py:62
  169.3 2.2 slice_bitcast_fusion
  171.5 2.8 %copy.41 = bf16[4,12,20,1024]{3,0,2,1:T(4,128)(2,1)} copy(bf16[4,12,20,1024]{3,2,0,1:T(8,128)(2,1)S(1)} %slice_bitcast_fusion) | data formatting | bytes 3932160 | tf_op jit(solution)/shard_map/convert_element_type | solution.py:62
  174.3 4.1 %reshape.27 = bf16[2,2,240,1024]{3,1,0,2:T(2,128)(2,1)S(1)} reshape(bf16[4,12,20,1024]{3,0,2,1:T(4,128)(2,1)} %copy.41) | data formatting | bytes 3932160 | tf_op jit(solution)/shard_map/reshape | solution.py:64
  178.4 2.8 %fusion.14 = (bf16[1024,2,1,240]{0,2,1,3:T(2,128)(2,1)S(1)}, bf16[1024,2,1,240]{0,2,1,3:T(2,128)(2,1)S(1)}) fusion(bf16[1024,2,2,240]{0,2,1,3:T(2,128)(2,1)S(1)} %bitcast.27), kind=kLoop, calls=%fused_computation.21 | loop fusion | bytes 3932160 | tf_op jit(solution)/shard_map/slice | solution.py:15
  181.2 0.5 copy.42
  181.8 3.6 %collective-permute-start = (bf16[1024,2,1,240]{0,3,2,1:T(8,128)(2,1)S(1)}, bf16[1024,2,1,240]{0,3,2,1:T(8,128)(2,1)S(1)}, u32[]{:S(2)}, u32[]{:S(2)}) collective-permute-start(bf16[1024,2,1,240]{0,3,2,1:T(8,128)(2,1)S(1)} %copy.42), channel_id=1, source_target_pairs={{0,1},{1,2},{2,3},{3,4},{4,5},{5,6},{6,7},{8,9},{9,10},{10,11},{11... | collective-permute-start | bytes 2949128 | tf_op jit(solution)/shard_map/ppermute | solution.py:14
  185.4 0.5 copy.43
  186.0 1.9 collective-permute-start.1
  187.9 8.5 %collective-permute-done = bf16[1024,2,1,240]{0,3,2,1:T(8,128)(2,1)S(1)} collective-permute-done((bf16[1024,2,1,240]{0,3,2,1:T(8,128)(2,1)S(1)}, bf16[1024,2,1,240]{0,3,2,1:T(8,128)(2,1)S(1)}, u32[]{:S(2)}, u32[]{:S(2)}) %collective-permute-start) | collective-permute-done | bytes 983072 | tf_op jit(solution)/shard_map/ppermute | solution.py:14
  196.4 1.5 copy.44
  197.9 3.4 %collective-permute-done.1 = bf16[1024,2,1,240]{0,3,2,1:T(8,128)(2,1)S(1)} collective-permute-done((bf16[1024,2,1,240]{0,3,2,1:T(8,128)(2,1)S(1)}, bf16[1024,2,1,240]{0,3,2,1:T(8,128)(2,1)S(1)}, u32[]{:S(2)}, u32[]{:S(2)}) %collective-permute-start.1) | collective-permute-done | bytes 983072 | tf_op jit(solution)/shard_map/ppermute | solution.py:17
  201.4 1.5 copy.45
  202.9 6.8 %maximum_bitcast_fusion = bf16[1024,4,2,240]{0,1,2,3:T(4,128)(2,1)S(1)} fusion(bf16[1024,2,1,240]{0,2,1,3:T(2,128)(2,1)S(1)} %copy.45, bf16[1024,2,2,240]{0,2,1,3:T(2,128)(2,1)S(1)} %bitcast.28, bf16[1024,2,1,240]{0,2,1,3:T(2,128)(2,1)S(1)} %copy.44), kind=kLoop, calls=%fused_computation.13 | loop fusion | flops 11796480 | bytes 7864320 | tf_op jit(solution)/shard_map/concatenate | solution.py:18
  209.7 3.2 %copy.46 = bf16[1024,4,2,240]{0,1,3,2:T(4,128)(2,1)} copy(bf16[1024,4,2,240]{0,1,2,3:T(4,128)(2,1)S(1)} %maximum_bitcast_fusion) | data formatting | bytes 7864320 | tf_op jit(solution)/shard_map/concatenate | solution.py:18
  213.0 0.0 all-gather.5.cloned.1.call-done
  213.0 13.9 %fusion.1 = f32[2,16,30,1024]{3,1,2,0:T(8,128)S(1)} fusion(bf16[3,1024,1024]{2,1,0:T(8,128)(2,1)} %all-gather.5.cloned.1.call-done, bf16[1024,4,16,30]{0,1,3,2:T(4,128)(2,1)} %bitcast.33), kind=kOutput, calls=%fused_computation.2 | convolution fusion | flops 6039797760 | bytes 14155776 | tf_op jit(solution)/shard_map/conv_general_dilated | solution.py:34
  226.8 0.0 copy-start.1
  226.8 3.0 %copy.48 = f32[2,16,30,1024]{3,0,2,1:T(2,128)S(1)} copy(f32[2,16,30,1024]{3,1,2,0:T(8,128)S(1)} %fusion.1) | data formatting | bytes 7864320 | tf_op jit(solution)/shard_map/conv_general_dilated | solution.py:34
  229.9 0.0 copy-done.1
  229.9 3.5 %fusion.5 = bf16[2,2,12,20,1024]{4,1,3,2,0:T(2,128)(2,1)} fusion(f32[2,2,12,20,1024]{4,1,3,2,0:T(2,128)S(1)} %bitcast.31, bf16[2,2,12,20,1024]{4,1,3,2,0:T(2,128)(2,1)S(1)} %copy-done.1), kind=kLoop, calls=%fused_computation.11 | loop fusion | flops 2949120 | bytes 7864320 | tf_op jit(solution)/shard_map/convert_element_type | solution.py:73
  (1 shorter events, 0.0 us)
Async XLA Ops:
  6.5 5.7 %copy-start = (bf16[2,2,12,20,1024]{4,1,3,2,0:T(2,128)(2,1)S(1)}, bf16[2,2,12,20,1024]{4,1,3,2,0:T(2,128)(2,1)}, u32[]{:S(2)}) copy-start(bf16[2,2,12,20,1024]{4,1,3,2,0:T(2,128)(2,1)} %param.5) | copy-start | bytes 5898244
  6.5 5.7 %copy-start.2 = (f32[1024]{0:T(1024)S(1)}, f32[1024]{0:T(1024)}, u32[]{:S(2)}) copy-start(f32[1024]{0:T(1024)} %param.6) | copy-start | bytes 12292
  6.5 128.4 %all-gather.3.cloned.1.call-start = ((), (), s32[]{:S(2)}) async-start(), calls=%async_computation | async-start | bytes 20054016 | tf_op jit(solution)/shard_map/all_gather | solution.py:57
  7.3 205.7 %all-gather.5.cloned.1.call-start = ((), (), s32[]{:S(2)}) async-start(), calls=%async_computation.1 | async-start | bytes 6684672 | tf_op jit(solution)/shard_map/all_gather | solution.py:68
  27.0 108.0 %copy-start.3 = (f32[1024]{0:T(1024)S(1)}, f32[1024]{0:T(1024)}, u32[]{:S(2)}) copy-start(f32[1024]{0:T(1024)} %param.8) | copy-start | bytes 12292
  27.0 107.9 %copy-start.4 = (pred[32,3]{0,1:T(4,128)(4,1)S(1)}, pred[32,3]{0,1:T(4,128)(4,1)}, u32[]{:S(2)}) copy-start(pred[32,3]{0,1:T(4,128)(4,1)} %constant.21) | copy-start | bytes 292
  181.8 14.6 %collective-permute-start = (bf16[1024,2,1,240]{0,3,2,1:T(8,128)(2,1)S(1)}, bf16[1024,2,1,240]{0,3,2,1:T(8,128)(2,1)S(1)}, u32[]{:S(2)}, u32[]{:S(2)}) collective-permute-start(bf16[1024,2,1,240]{0,3,2,1:T(8,128)(2,1)S(1)} %copy.42), channel_id=1, source_target_pairs={{0,1},{1,2},{2,3},{3,4},{4,5},{5,6},{6,7},{8,9},{9,10},{10,11},{11... | collective-permute-start | bytes 2949128 | tf_op jit(solution)/shard_map/ppermute | solution.py:14
  186.0 15.4 %collective-permute-start.1 = (bf16[1024,2,1,240]{0,3,2,1:T(8,128)(2,1)S(1)}, bf16[1024,2,1,240]{0,3,2,1:T(8,128)(2,1)S(1)}, u32[]{:S(2)}, u32[]{:S(2)}) collective-permute-start(bf16[1024,2,1,240]{0,3,2,1:T(8,128)(2,1)S(1)} %copy.43), channel_id=1, source_target_pairs={{1,0},{2,1},{3,2},{4,3},{5,4},{6,5},{7,6},{9,8},{10,9},{11,10},{12... | collective-permute-start | bytes 2949128 | tf_op jit(solution)/shard_map/ppermute | solution.py:17
  226.8 3.1 %copy-start.1 = (bf16[2,2,12,20,1024]{4,1,3,2,0:T(2,128)(2,1)S(1)}, bf16[2,2,12,20,1024]{4,1,3,2,0:T(2,128)(2,1)}, u32[]{:S(2)}) copy-start(bf16[2,2,12,20,1024]{4,1,3,2,0:T(2,128)(2,1)} %param.5) | copy-start | bytes 5898244
Sparse Core Ops, SparseCore 0:
  9.6 125.3 all-gather.2
  137.2 61.0 all-gather.4
where the time goes:
time: 243 us; the launch traced here: 240 us
  waiting for transfers between devices  118 us (49%)
  matrix products  42.1 us (17%)
  local copies, waits for them, and re-layouts  38.5 us (16%)
  other arithmetic  22.6 us (9%)
  between operations  13.8 us (6%)
  starting transfers between devices  5.58 us (2%)
    all_gather x1, waiting for transfers between devices, shards(): piece = lax.all_gather(spatial_weight, 'dp', axis=1, tiled=True)  105 us
    conv_general_dilated x1, matrix products, spatial_conv(): lax.conv_general_dilated(inputs, kernel, (1, 1), ((1, 1), (1, 1)), dimens...  28.2 us
    conv_general_dilated x1, matrix products, temporal_conv(): lax.conv_general_dilated(inputs, kernel, (1, 1), ((0, 0), (0, 0)), dimens...  13.9 us
    convert_element_type x4, local copies, waits for them, and re-layouts, shards(): hidden = jax.nn.silu(spatial + spatial_bias).astype(jnp.bfloat16)  11.1 us
    ppermute x1, waiting for transfers between devices, extended_2(): lax.ppermute(lax.slice_in_dim(block, block.shape[dim] - width, None, axis...  8.54 us
    concatenate x1, other arithmetic, extended_2(): block = jnp.concatenate([low, block, high], axis=dim)  6.84 us
    reshape x2, local copies, waits for them, and re-layouts, shards(): active.reshape(batch_dev * frame_dev, height, width_cells, channels)  5.79 us
    convert_element_type x1, other arithmetic, shards(): active = jax.nn.silu(scaled).astype(jnp.bfloat16)  5.21 us
  transfers between devices with their start and end apart: 4, of which 3 were waited for; matrix products, arithmetic and copies ran while one was open for 34% of the time, Pallas kernels for 0%

commit v1 on v0

v1 whole, which is shorter than its diff:
```python
import functools

import jax
import jax.numpy as jnp
from jax import lax
from jax.experimental import pallas as pl
from jax.experimental.pallas import tpu as pltpu
from jax.sharding import Mesh
from jax.sharding import PartitionSpec as P

EPSILON = 1e-06
F32, BF16 = jnp.float32, jnp.bfloat16
MIB = 2**20

ROWS, COLS, SLOTS = 12, 20, 8
LINE = COLS * SLOTS
POINTS = ROWS * LINE


def silu(v):
    return v / (1.0 + jnp.exp(-v))


def specs(*kinds):
    places = {"s": pltpu.SMEM, "v": pltpu.VMEM, "h": pl.ANY}
    return [pl.BlockSpec(memory_space=places[kind]) for kind in kinds]


def params(mib):
    return pltpu.CompilerParams(vmem_limit_bytes=mib * MIB)


def cost(flops, bytes_accessed):
    return pl.CostEstimate(flops=flops, bytes_accessed=bytes_accessed, transcendentals=0)


def pack_kernel(where, spatial, temporal, unit_a, unit_b):
    core = where[3]
    source = lax.broadcasted_iota(jnp.int32, (256, 128), 0)
    target = lax.broadcasted_iota(jnp.int32, (256, 128), 1)
    wanted = (target >> 5) * 64 + (target & 31) + core * 32
    pick = jnp.where(source == wanted, 1.0, 0.0).astype(BF16)
    for part in range(4):
        unit = (unit_a, unit_b)[part // 2]
        columns = spatial[:, :, part * 256 : (part + 1) * 256].reshape(576, 256)
        kept = jnp.dot(columns, pick, preferred_element_type=F32).astype(BF16)
        unit[0:576, (part % 2) * 128 : (part % 2 + 1) * 128] = kept
    for tap in range(3):
        rows = temporal[tap, pl.ds(pl.multiple_of(core * 32, 32), 32), :]
        for part in range(4):
            unit = (unit_a, unit_b)[part // 2]
            start = 576 + (part % 2) * 96 + tap * 32
            unit[start : start + 32, :] = rows[:, part * 256 : (part + 1) * 256]


def pack(where, spatial, temporal):
    unit = jax.ShapeDtypeStruct((768, 256), BF16)
    return pl.pallas_call(
        pack_kernel,
        out_shape=(unit, unit),
        in_specs=specs("s", "v", "v"),
        out_specs=specs("v", "v"),
        compiler_params=params(16),
        cost_estimate=cost(10**9, 3 * 10**6),
    )(where, spatial, temporal)


def arrange_kernel(where, own, other, gain, wide_a, core_a, wide_b, core_b, active):
    core = where[3]
    scale = gain[...]
    for relative, video in ((0, own), (1, other)):
        owner = core if relative == 0 else 1 - core
        for index in range(2):
            for frame in range(2):
                slot = (2 * owner + frame) * 2 + index

                def line(i, carry, video=video, index=index, frame=frame, slot=slot):
                    values = video[index, frame, i].astype(F32)
                    mean = jnp.mean(values * values, axis=-1, keepdims=True)
                    scaled = values * lax.rsqrt(mean + EPSILON) * scale
                    scaled = silu(scaled)
                    for part in range(8):
                        active[part, pl.ds(i * LINE + slot, COLS, stride=SLOTS), :] = scaled[
                            :, part * 128 : (part + 1) * 128
                        ]
                    return carry

                lax.fori_loop(0, ROWS, line, 0, unroll=2)

    low = lax.broadcasted_iota(jnp.int32, (LINE, 128), 1) < 64
    edge = jnp.zeros((SLOTS, 256), F32)

    def put(wide, narrow, block, i, value):
        narrow[block, i + 1] = value.astype(BF16)
        wide[block, i + 1] = jnp.concatenate([edge, value, edge], axis=0).astype(BF16)

    def spread(i, carry):
        lines = [active[part, pl.ds(i * LINE, LINE), :] for part in range(8)]
        turned = [pltpu.roll(value, 64, 1) for value in lines]
        for y in range(4):
            put(wide_b, core_b, y, i, jnp.concatenate([lines[2 * y], lines[2 * y + 1]], axis=1))
        for z in range(4):
            halves = []
            for y in (0, 2):
                first, second = y * 2 + z // 2, (y + 1) * 2 + z // 2
                if z % 2 == 0:
                    halves.append(jnp.where(low, lines[first], turned[second]))
                else:
                    halves.append(jnp.where(low, turned[first], lines[second]))
            put(wide_a, core_a, z, i, jnp.concatenate(halves, axis=1))
        return carry

    lax.fori_loop(0, ROWS, spread, 0)
    for block in range(4):
        for i in (0, ROWS + 1):
            for ref in (wide_a, core_a, wide_b, core_b):
                ref[block, i] = jnp.zeros(ref.shape[2:], BF16)


def arrange(where, own, other, gain):
    wide = jax.ShapeDtypeStruct((4, ROWS + 2, LINE + 16, 256), BF16)
    narrow = jax.ShapeDtypeStruct((4, ROWS + 2, LINE, 256), BF16)
    return pl.pallas_call(
        arrange_kernel,
        out_shape=(wide, narrow, wide, narrow),
        in_specs=specs("s", "v", "v", "v"),
        out_specs=specs("v", "v", "v", "v"),
        scratch_shapes=[pltpu.VMEM((8, POINTS, 128), F32)],
        compiler_params=params(52),
        cost_estimate=cost(10**9, 25 * 10**6),
    )(where, own, other, gain)


def stack_kernel(*refs):
    units, (sa, ta, sb, tb), sem = refs[:8], refs[8:12], refs[12]
    copies = []
    for index in range(8):
        spatial, temporal = ((sa, ta), (sb, tb))[index // 4]
        slot = index % 4
        copies.append((units[index].at[pl.ds(0, 576)], spatial.at[slot]))
        copies.append((units[index].at[pl.ds(576, 192)], temporal.at[slot]))
    started = []
    for number, (source, target) in enumerate(copies):
        copy = pltpu.make_async_copy(source, target, sem.at[number])
        copy.start()
        started.append(copy)
    for copy in started:
        copy.wait()


def stack(units):
    spatial = jax.ShapeDtypeStruct((4, 576, 256), BF16)
    temporal = jax.ShapeDtypeStruct((4, 192, 256), BF16)
    return pl.pallas_call(
        stack_kernel,
        out_shape=(spatial, temporal, spatial, temporal),
        in_specs=specs(*"hhhhhhhh"),
        out_specs=specs(*"hhhh"),
        scratch_shapes=[pltpu.SemaphoreType.DMA((16,))],
        compiler_params=params(8),
        cost_estimate=cost(0, 6 * 10**6),
    )(*units)


def conv_kernel(step, *refs):
    first, last = step == 0, step == 3
    refs = list(refs)
    where, *inputs = refs[:7]
    refs = refs[7:]
    wide_hbm, narrow_hbm, spatial_hbm = (inputs[0], inputs[2]), (inputs[1], inputs[3]), inputs[4:6]
    sums_hbm = None
    if not first:
        sums_hbm, refs = refs[:2], refs[2:]
    if last:
        bias, refs = refs[0], refs[1:]
        hidden, lower, upper = refs[:3]
        refs = refs[3:]
    else:
        out, refs = refs[:2], refs[2:]
    wide, narrow, pieces, kernel, sums, sem = refs[:6]
    sides = refs[6] if last else None
    y, z, core = where[0], where[1], where[3]
    turn = 2 * core - 1
    mine = (z, y)
    across = (y, z)
    waits = []
    for colour in range(2):
        block = (mine[colour] + turn * step + 4) & 3
        copies = [
            pltpu.make_async_copy(spatial_hbm[colour], pieces.at[colour], sem.at[colour, 0]),
            pltpu.make_async_copy(wide_hbm[colour].at[block], wide.at[colour], sem.at[colour, 1]),
            pltpu.make_async_copy(narrow_hbm[colour].at[block], narrow.at[colour], sem.at[colour, 2]),
        ]
        if not first:
            copies.append(pltpu.make_async_copy(sums_hbm[colour], sums.at[colour], sem.at[colour, 3]))
        for copy in copies:
            copy.start()
        waits.append(copies)
    outs = []
    for colour in range(2):
        for copy in waits[colour]:
            copy.wait()
        for slot in range(4):
            place = (across[colour] + turn * slot + 4) & 3
            for tap in range(9):
                kernel[pl.ds(pl.multiple_of(tap * 256 + place * 64, 64), 64), :] = pieces[
                    colour, slot, tap * 64 : (tap + 1) * 64, :
                ]

        lines = 4

        def part(group, carry, colour=colour):
            i = group * lines
            total = None
            for tap in range(9):
                dy, dx = tap // 3, tap % 3
                if dx == 1:
                    window = narrow[colour, pl.ds(i + dy, lines), :, :]
                else:
                    window = wide[colour, pl.ds(i + dy, lines), dx * 8 : dx * 8 + LINE, :]
                product = jnp.dot(
                    window.reshape(lines * LINE, 256),
                    kernel[tap * 256 : (tap + 1) * 256, :],
                    preferred_element_type=F32,
                )
                total = product if total is None else total + product
            rows = pl.ds(pl.multiple_of(i * LINE, lines * LINE), lines * LINE)
            if not first:
                total = total + sums[colour, rows, :]
            if last:
                total = silu(total + bias[:, colour * 256 : (colour + 1) * 256])
                hidden[rows, colour * 256 : (colour + 1) * 256] = total.astype(BF16)
                for half in range(2):
                    sides[colour * 2 + half, rows, :] = total[:, half * 128 : (half + 1) * 128]
            else:
                sums[colour, rows, :] = total
            return carry

        lax.fori_loop(0, ROWS // lines, part, 0)
        if last:
            for half in range(2):
                columns = slice(colour * 256 + half * 128, colour * 256 + (half + 1) * 128)
                for index in range(2):
                    for target, slot in ((lower, index), (upper, 6 + index)):
                        target[index, :, columns] = sides[
                            colour * 2 + half, pl.ds(slot, ROWS * COLS, stride=SLOTS), :
                        ].astype(BF16)
        else:
            copy = pltpu.make_async_copy(sums.at[colour], out[colour], sem.at[colour, 4])
            copy.start()
            outs.append(copy)
    for copy in outs:
        copy.wait()


def conv(step, where, active, spatial, sums=None, bias=None):
    operands = [where, *active, *spatial]
    kinds = "shhhhhh"
    if step > 0:
        operands += sums
        kinds += "hh"
    if step == 3:
        operands.append(bias)
        kinds += "v"
        side = jax.ShapeDtypeStruct((2, ROWS * COLS, 512), BF16)
        out_shape = (jax.ShapeDtypeStruct((POINTS, 512), BF16), side, side)
        out_specs = specs(*"vvv")
    else:
        total = jax.ShapeDtypeStruct((POINTS, 256), F32)
        out_shape, out_specs = (total, total), specs(*"hh")
    return pl.pallas_call(
        functools.partial(conv_kernel, step),
        out_shape=out_shape,
        in_specs=specs(*kinds),
        out_specs=out_specs,
        scratch_shapes=[
            pltpu.VMEM((2, ROWS + 2, LINE + 16, 256), BF16),
            pltpu.VMEM((2, ROWS + 2, LINE, 256), BF16),
            pltpu.VMEM((2, 4, 576, 256), BF16),
            pltpu.VMEM((2304, 256), BF16),
            pltpu.VMEM((2, POINTS, 256), F32),
            pltpu.SemaphoreType.DMA((2, 5)),
        ]
        + ([pltpu.VMEM((4, POINTS, 128), F32)] if step == 3 else []),
        compiler_params=params(40),
        cost_estimate=cost(2 * 2 * POINTS * 2304 * 256, 18 * 10**6),
    )(*operands)


def temporal_kernel(where, hidden, before, after, *refs):
    blocks, (mine, theirs, plain, kernel, pieces, shifted, total, sem) = refs[:8], refs[8:]
    y, z, core = where[0], where[1], where[3]
    turn = 2 * core - 1
    copies = []
    for number in range(8):
        copy = pltpu.make_async_copy(blocks[number], pieces.at[number], sem.at[number])
        copy.start()
        copies.append(copy)
    slot = lax.broadcasted_iota(jnp.int32, (LINE, 128), 0) & 7
    zero = jnp.zeros((SLOTS, 128), F32)
    for part in range(4):
        columns = slice(part * 128, (part + 1) * 128)

        def move(i, carry, part=part, columns=columns):
            rows = pl.ds(pl.multiple_of(i * LINE, LINE), LINE)
            values = hidden[rows, columns].astype(F32)
            plain[0, rows, :] = jnp.where(slot >= 2, pltpu.roll(values, 2, 0), 0.0)
            plain[1, rows, :] = jnp.where(slot < 6, pltpu.roll(values, LINE - 2, 0), 0.0)
            return carry

        lax.fori_loop(0, ROWS, move, 0)
        for index in range(2):
            plain[0, pl.ds(index, ROWS * COLS, stride=SLOTS), :] = before[index, :, columns].astype(F32)
            plain[1, pl.ds(6 + index, ROWS * COLS, stride=SLOTS), :] = after[index, :, columns].astype(F32)
        shifted[0, :, columns] = plain[0].astype(BF16)
        shifted[1, :, columns] = plain[1].astype(BF16)
    for copy in copies:
        copy.wait()
    for number in range(8):
        colour, step = number // 4, number % 4
        for unit in range(4):
            fixed, moving = (unit, step) if colour == 0 else (step, unit)
            row, column = (y + turn * fixed + 4) & 3, (z + turn * moving + 4) & 3
            place = pl.multiple_of((row * 4 + column) * 32, 32)
            for tap in range(3):
                for half in range(2):
                    start = half * 96 + tap * 32
                    kernel[tap, pl.ds(place, 32), (colour * 2 + half) * 256 : (colour * 2 + half + 1) * 256] = pieces[
                        number, unit, start : start + 32, :
                    ]

    for part in range(4):
        columns = slice(part * 256, (part + 1) * 256)

        def multiply(group, carry, part=part, columns=columns):
            rows = pl.ds(pl.multiple_of(group * 640, 640), 640)
            value = jnp.dot(hidden[rows, :], kernel[1, :, columns], preferred_element_type=F32)
            value = value + jnp.dot(shifted[0, rows, :], kernel[0, :, columns], preferred_element_type=F32)
            value = value + jnp.dot(shifted[1, rows, :], kernel[2, :, columns], preferred_element_type=F32)
            for half in range(2):
                total[part * 2 + half, rows, :] = value[:, half * 128 : (half + 1) * 128]
            return carry

        lax.fori_loop(0, 3, multiply, 0)

    for index in range(2):
        for frame in range(2):
            for target, owner in ((theirs, 1 - core), (mine, core)):
                start = (2 * owner + frame) * 2 + index

                def line(i, carry, target=target, start=start, index=index, frame=frame):
                    for part in range(8):
                        target[index, frame, i, :, part * 128 : (part + 1) * 128] = total[
                            part, pl.ds(i * LINE + start, COLS, stride=SLOTS), :
                        ].astype(target.dtype)
                    return carry

                lax.fori_loop(0, ROWS, line, 0)


def temporal(where, hidden, before, after, blocks):
    shape = (2, 2, ROWS, COLS, 1024)
    return pl.pallas_call(
        temporal_kernel,
        out_shape=(jax.ShapeDtypeStruct(shape, F32), jax.ShapeDtypeStruct(shape, BF16)),
        in_specs=specs("s", "v", "v", "v", *"hhhhhhhh"),
        out_specs=specs("v", "v"),
        scratch_shapes=[
            pltpu.VMEM((2, POINTS, 128), F32),
            pltpu.VMEM((3, 512, 1024), BF16),
            pltpu.VMEM((8, 4, 192, 256), BF16),
            pltpu.VMEM((2, POINTS, 512), BF16),
            pltpu.VMEM((8, POINTS, 128), F32),
            pltpu.SemaphoreType.DMA((8,)),
        ],
        compiler_params=params(52),
        cost_estimate=cost(2 * 3 * POINTS * 512 * 1024, 12 * 10**6),
    )(where, hidden, before, after, *blocks)


def finish_kernel(video, mine, received, result):
    result[...] = (video[...].astype(F32) + mine[...] + received[...].astype(F32)).astype(BF16)


def finish(video, mine, received):
    block = pl.BlockSpec((1, 1, ROWS, COLS, 1024), lambda i: (i // 2, i % 2, 0, 0, 0))
    return pl.pallas_call(
        finish_kernel,
        grid=(4,),
        out_shape=jax.ShapeDtypeStruct(video.shape, BF16),
        in_specs=[block] * 3,
        out_specs=block,
        compiler_params=params(24),
        cost_estimate=cost(3 * 10**6, 10 * 10**6),
    )(video, mine, received)


def ring(value, axis):
    count = lax.axis_size(axis)
    pairs = [(i * 2, (i + 1) % count * 2) for i in range(count)]
    pairs += [(i * 2 + 1, (i - 1) % count * 2 + 1) for i in range(count)]
    return lax.ppermute(value, (axis, "core"), pairs)


def shards(video, norm_gain, spatial_weight, spatial_bias, temporal_weight):
    where = jnp.stack([lax.axis_index(axis) for axis in ("y", "z", "x", "core")]).astype(jnp.int32)
    swap = [(0, 1), (1, 0)]
    other = lax.ppermute(video, "core", swap)
    unit_a, unit_b = pack(where, spatial_weight, temporal_weight)
    units_a, units_b = [unit_a], [unit_b]
    for _ in range(3):
        units_a.append(ring(units_a[-1], "y"))
        units_b.append(ring(units_b[-1], "z"))
    active = arrange(where, video, other, norm_gain.reshape(1, 1024))
    bias = spatial_bias.reshape(16, 2, 32)[:, where[3], :].reshape(1, 512)

    sa, ta, sb, tb = stack(units_a + units_b)
    spatial, later = [(sa, sb)], [(ta, tb)]
    for _ in range(3):
        spatial.append((ring(spatial[-1][0], "z"), ring(spatial[-1][1], "y")))
        later.append((ring(later[-1][0], "z"), ring(later[-1][1], "y")))

    sums = None
    for step in range(3):
        sums = conv(step, where, active, spatial[step], sums)
    hidden, lower, upper = conv(3, where, active, spatial[3], sums, bias)
    count = lax.axis_size("x")
    before = lax.ppermute(upper, "x", [(i, i + 1) for i in range(count - 1)])
    after = lax.ppermute(lower, "x", [(i + 1, i) for i in range(count - 1)])
    blocks = [pair[0] for pair in later] + [pair[1] for pair in later]
    mine, theirs = temporal(where, hidden, before, after, blocks)
    received = lax.ppermute(theirs, "core", swap)
    return finish(video, mine, received)


def solution(mesh):
    parts = Mesh(mesh.devices.reshape(4, 4, 4, 2), ("y", "z", "x", "core"))
    dp, frame = ("y", "z"), ("x", "core")
    in_specs = (
        P(dp, frame, None, None, None),
        P(),
        P(None, dp, None),
        P(),
        P(None, dp, None),
    )
    out_specs = P(dp, frame, None, None, None)
    return jax.shard_map(shards, mesh=parts, in_specs=in_specs, out_specs=out_specs, check_vma=False)
```

time: 243 us -> 196 us (0.81)
  waiting for transfers between devices: 118 us -> 40 us
  Pallas kernels: 0 us -> 77.1 us
  matrix products: 42.1 us -> 0 us
  starting transfers between devices: 5.58 us -> 47.4 us
  other arithmetic: 22.6 us -> 0.08 us
  between operations: 13.8 us -> 0.24 us
  local copies, waits for them, and re-layouts: 38.5 us -> 27.8 us
    all_gather x2 -> x0, waiting for transfers between devices: 105 us -> none  [the longest x1 105 us: shards(): piece = lax.all_gather(spatial_weight, 'dp', axis=1, tiled=True)]
    pallas_call x0 -> x9, Pallas kernels: none -> 77.1 us  [the longest x4 35.6 us: conv(): pl.pallas_call(functools.partial(conv_kernel, step), out_shape=out_shape,...]
    conv_general_dilated x2 -> x0, matrix products: 42.1 us -> none  [the longest x1 28.2 us: spatial_conv(): lax.conv_general_dilated(inputs, kernel, (1, 1), ((1, 1), (1, 1)), dimens...]
    ppermute x2 -> x22, starting transfers between devices: 5.53 us -> 47.4 us  [the longest x18 35.5 us: ring(): return lax.ppermute(value, (axis, 'core'), pairs)]
    ppermute x2 -> x22, waiting for transfers between devices: 12 us -> 40 us  [the longest x18 35.6 us: ring(): return lax.ppermute(value, (axis, 'core'), pairs)]
    unnamed x10 -> x35, local copies, waits for them, and re-layouts: 0.03 us -> 14.9 us
    convert_element_type x5 -> x0, local copies, waits for them, and re-layouts: 14 us -> none  [the longest x4 11.1 us: shards(): hidden = jax.nn.silu(spatial + spatial_bias).astype(jnp.bfloat16)]
    reshape x3 -> x1, local copies, waits for them, and re-layouts: 9.91 us -> 0.69 us  [shards(): bias = spatial_bias.reshape(16, 2, 32)[:, where[3], :].reshape(1, 512)]
  transfers between devices with their start and end apart: 4 -> 22, of which waited for: 3 -> 12; matrix products, arithmetic and copies ran while one was open for 34% -> 5% of each run, Pallas kernels for 0% -> 29%
where the time goes in v1:
time: 196 us; the launch traced here: 193 us
  Pallas kernels  77.1 us (39%)
  starting transfers between devices  47.4 us (24%)
  waiting for transfers between devices  40 us (20%)
  local copies, waits for them, and re-layouts  27.8 us (14%)
    ppermute x18, waiting for transfers between devices, ring(): return lax.ppermute(value, (axis, 'core'), pairs)  35.6 us
    pallas_call x4, Pallas kernels, conv(): pl.pallas_call(functools.partial(conv_kernel, step), out_shape=out_shape,...  35.6 us
    ppermute x18, starting transfers between devices, ring(): return lax.ppermute(value, (axis, 'core'), pairs)  35.5 us
    pallas_call x1, Pallas kernels, arrange(): pl.pallas_call(arrange_kernel, out_shape=(wide, narrow, wide, narrow), in...  19.8 us
    pallas_call x1, Pallas kernels, temporal(): pl.pallas_call(temporal_kernel, out_shape=(jax.ShapeDtypeStruct(shape, F3...  18.5 us
    unnamed x35, local copies, waits for them, and re-layouts  14.9 us
    ppermute x1, starting transfers between devices, shards(): received = lax.ppermute(theirs, 'core', swap)  6.36 us
  transfers between devices with their start and end apart: 22, of which 12 were waited for; matrix products, arithmetic and copies ran while one was open for 5% of the time, Pallas kernels for 29%

profile of v1, /device:TPU:1, one launch (start us, length us, event | category | flops | bytes accessed | tf_op | source)
XLA Modules:
  0.0 192.6 jit_solution(14271954220671902083)
XLA Ops:
  0.0 0.1 pad_add_fusion.where.refs_0_
  0.1 1.3 copy-done.9
  1.4 1.0 copy-done.10
  2.3 1.0 shard_map.56
  3.4 3.6 %collective-permute-start.1 = (bf16[768,256]{1,0:T(8,128)(2,1)S(1)}, bf16[768,256]{1,0:T(8,128)(2,1)S(1)}, u32[]{:S(2)}, u32[]{:S(2)}) collective-permute-start(bf16[768,256]{1,0:T(8,128)(2,1)S(1)} %get-tuple-element.30.refs_0_), channel_id=1, source_target_pairs={{0,32},{32,64},{64,96},{96,0},{1,97},{33,1},{65,33},{97,65},{2,34}... | collective-permute-start | bytes 1179656 | tf_op jit(solution)/shard_map/ppermute | solution.py:402
  7.0 3.8 %collective-permute-start.4 = (bf16[768,256]{1,0:T(8,128)(2,1)S(1)}, bf16[768,256]{1,0:T(8,128)(2,1)S(1)}, u32[]{:S(2)}, u32[]{:S(2)}) collective-permute-start(bf16[768,256]{1,0:T(8,128)(2,1)S(1)} %get-tuple-element.31.refs_4_), channel_id=1, source_target_pairs={{0,8},{8,16},{16,24},{24,0},{1,25},{9,1},{17,9},{25,17},{2,10},{10... | collective-permute-start | bytes 1179656 | tf_op jit(solution)/shard_map/ppermute | solution.py:402
  10.8 1.0 collective-permute-done.1.refs_1_
  11.7 3.4 %collective-permute-start.2 = (bf16[768,256]{1,0:T(8,128)(2,1)S(1)}, bf16[768,256]{1,0:T(8,128)(2,1)S(1)}, u32[]{:S(2)}, u32[]{:S(2)}) collective-permute-start(bf16[768,256]{1,0:T(8,128)(2,1)S(1)} %collective-permute-done.1.refs_1_), channel_id=1, source_target_pairs={{0,32},{32,64},{64,96},{96,0},{1,97},{33,1},{65,33},{97,65},{2,34}... | collective-permute-start | bytes 1179656 | tf_op jit(solution)/shard_map/ppermute | solution.py:402
  15.1 0.3 collective-permute-done.4.refs_5_
  15.5 3.1 %collective-permute-start.5 = (bf16[768,256]{1,0:T(8,128)(2,1)S(1)}, bf16[768,256]{1,0:T(8,128)(2,1)S(1)}, u32[]{:S(2)}, u32[]{:S(2)}) collective-permute-start(bf16[768,256]{1,0:T(8,128)(2,1)S(1)} %collective-permute-done.4.refs_5_), channel_id=1, source_target_pairs={{0,8},{8,16},{16,24},{24,0},{1,25},{9,1},{17,9},{25,17},{2,10},{10... | collective-permute-start | bytes 1179656 | tf_op jit(solution)/shard_map/ppermute | solution.py:402
  18.6 1.3 collective-permute-done.2.refs_2_
  19.9 3.4 %collective-permute-start.3 = (bf16[768,256]{1,0:T(8,128)(2,1)S(1)}, bf16[768,256]{1,0:T(8,128)(2,1)S(1)}, u32[]{:S(2)}, u32[]{:S(2)}) collective-permute-start(bf16[768,256]{1,0:T(8,128)(2,1)S(1)} %collective-permute-done.2.refs_2_), channel_id=1, source_target_pairs={{0,32},{32,64},{64,96},{96,0},{1,97},{33,1},{65,33},{97,65},{2,34}... | collective-permute-start | bytes 1179656 | tf_op jit(solution)/shard_map/ppermute | solution.py:402
  23.3 0.1 collective-permute-done.5.refs_6_
  23.3 3.1 %collective-permute-start.6 = (bf16[768,256]{1,0:T(8,128)(2,1)S(1)}, bf16[768,256]{1,0:T(8,128)(2,1)S(1)}, u32[]{:S(2)}, u32[]{:S(2)}) collective-permute-start(bf16[768,256]{1,0:T(8,128)(2,1)S(1)} %collective-permute-done.5.refs_6_), channel_id=1, source_target_pairs={{0,8},{8,16},{16,24},{24,0},{1,25},{9,1},{17,9},{25,17},{2,10},{10... | collective-permute-start | bytes 1179656 | tf_op jit(solution)/shard_map/ppermute | solution.py:402
  26.4 1.6 collective-permute-done.3.refs_3_
  28.0 3.2 %collective-permute-done.6.refs_7_ = bf16[768,256]{1,0:T(8,128)(2,1)S(1)} collective-permute-done((bf16[768,256]{1,0:T(8,128)(2,1)S(1)}, bf16[768,256]{1,0:T(8,128)(2,1)S(1)}, u32[]{:S(2)}, u32[]{:S(2)}) %collective-permute-start.6) | collective-permute-done | bytes 393248 | tf_op jit(solution)/shard_map/ppermute | solution.py:402
  31.2 1.2 shard_map.57
  32.4 0.5 collective-permute-start.10
  33.0 3.1 %collective-permute-start.7 = (bf16[4,576,256]{2,1,0:T(8,128)(2,1)S(1)}, bf16[4,576,256]{2,1,0:T(8,128)(2,1)}, u32[]{:S(2)}, u32[]{:S(2)}) collective-permute-start(bf16[4,576,256]{2,1,0:T(8,128)(2,1)S(1)} %get-tuple-element.32.refs_5_), channel_id=1, source_target_pairs={{0,8},{8,16},{16,24},{24,0},{1,25},{9,1},{17,9},{25,17},{2,10},{10... | collective-permute-start | bytes 3538952 | tf_op jit(solution)/shard_map/ppermute | solution.py:402
  36.1 1.1 collective-permute-start
  37.2 10.7 %collective-permute-done.10.refs_6_ = bf16[4,576,256]{2,1,0:T(8,128)(2,1)S(1)} collective-permute-done((bf16[4,576,256]{2,1,0:T(8,128)(2,1)S(1)}, bf16[4,576,256]{2,1,0:T(8,128)(2,1)S(1)}, u32[]{:S(2)}, u32[]{:S(2)}) %collective-permute-start.10) | collective-permute-done | bytes 1179680 | tf_op jit(solution)/shard_map/ppermute | solution.py:402
  47.9 1.7 collective-permute-start.11
  49.6 3.0 %collective-permute-start.8 = (bf16[4,576,256]{2,1,0:T(8,128)(2,1)}, bf16[4,576,256]{2,1,0:T(8,128)(2,1)}, u32[]{:S(2)}, u32[]{:S(2)}) collective-permute-start(bf16[4,576,256]{2,1,0:T(8,128)(2,1)} %collective-permute-done.7.refs_5_), channel_id=1, source_target_pairs={{0,8},{8,16},{16,24},{24,0},{1,25},{9,1},{17,9},{25,17},{2,10},{10... | collective-permute-start | bytes 3538952 | tf_op jit(solution)/shard_map/ppermute | solution.py:402
  52.6 0.0 collective-permute-start.15
  52.7 3.7 %copy.17.own.video = bf16[2,2,12,20,1024]{4,3,2,1,0:T(8,128)(2,1)} copy(bf16[2,2,12,20,1024]{4,1,3,2,0:T(2,128)(2,1)} %param.5) | data formatting | bytes 3932160 | tf_op args[0]
  56.3 0.7 reshape.7
  57.0 0.7 dynamic-slice_reduce_fusion
  57.8 0.1 reshape_squeeze.3.refs_9_
  57.9 12.5 %collective-permute-done.15.refs_1_ = bf16[4,192,256]{2,1,0:T(8,128)(2,1)} collective-permute-done((bf16[4,192,256]{2,1,0:T(8,128)(2,1)}, bf16[4,192,256]{2,1,0:T(8,128)(2,1)}, u32[]{:S(2)}, u32[]{:S(2)}) %collective-permute-start.15) | collective-permute-done | bytes 393248 | tf_op jit(solution)/shard_map/ppermute | solution.py:402
  70.3 3.4 %collective-permute-start.16 = (bf16[4,192,256]{2,1,0:T(8,128)(2,1)}, bf16[4,192,256]{2,1,0:T(8,128)(2,1)S(1)}, u32[]{:S(2)}, u32[]{:S(2)}) collective-permute-start(bf16[4,192,256]{2,1,0:T(8,128)(2,1)} %collective-permute-done.15.refs_1_), channel_id=1, source_target_pairs={{0,8},{8,16},{16,24},{24,0},{1,25},{9,1},{17,9},{25,17},{2,10},{10... | collective-permute-start | bytes 1179656 | tf_op jit(solution)/shard_map/ppermute | solution.py:402
  73.7 0.0 collective-permute-done.18.refs_5_
  73.7 0.0 collective-permute-start.19
  73.7 0.0 collective-permute-done
  73.7 3.6 %copy.15.other = bf16[2,2,12,20,1024]{4,3,2,1,0:T(8,128)(2,1)} copy(bf16[2,2,12,20,1024]{4,1,3,2,0:T(2,128)(2,1)} %collective-permute-done) | data formatting | bytes 3932160 | tf_op jit(solution)/shard_map/ppermute | solution.py:408
  77.3 19.8 %shard_map.55 = (bf16[4,14,176,256]{3,2,1,0:T(8,128)(2,1)}, bf16[4,14,160,256]{3,2,1,0:T(8,128)(2,1)}, bf16[4,14,176,256]{3,2,1,0:T(8,128)(2,1)}, bf16[4,14,160,256]{3,2,1,0:T(8,128)(2,1)}) custom-call(s32[4]{0:T(128)S(1)} %pad_add_fusion.where.refs_0_, bf16[2,2,12,20,1024]{4,3,2,1,0:T(8,128)(2,1)} %copy.17.own.video, ...), custom_call_target="tpu_custom_call" | custom-call | flops 1000000000 | bytes 25000000 | tf_op jit(solution)/shard_map/pallas_call | solution.py:123
  97.1 0.0 collective-permute-done.8.refs_5_
  97.2 0.3 collective-permute-start.9
  97.4 2.3 %copy-done = bf16[4,14,160,256]{3,2,1,0:T(8,128)(2,1)S(1)} copy-done((bf16[4,14,160,256]{3,2,1,0:T(8,128)(2,1)S(1)}, bf16[4,14,160,256]{3,2,1,0:T(8,128)(2,1)}, u32[]{:S(2)}) %copy-start) | copy-done | bytes 4587544
  99.7 8.6 %shard_map.58 = (f32[1920,256]{1,0:T(8,128)S(1)}, f32[1920,256]{1,0:T(8,128)S(1)}) custom-call(s32[4]{0:T(128)S(1)} %pad_add_fusion.where.refs_0_, bf16[4,14,176,256]{3,2,1,0:T(8,128)(2,1)} %get-tuple-element.26.refs_1_, bf16[4,14,160,256]{3,2,1,0:T(8,128)(2,1)S(1)} %copy-done, bf16[4,14,176,256]{3,2,1,0:T(8,128)(2,1)} %get-tuple-element.28.refs_3_, ...), custom_call_target="tpu_custom_call" | custom-call | flops 4529848320 | bytes 18000000 | tf_op jit(solution)/shard_map/pallas_call | solution.py:271
  108.3 9.0 %shard_map.59 = (f32[1920,256]{1,0:T(8,128)S(1)}, f32[1920,256]{1,0:T(8,128)S(1)}) custom-call(s32[4]{0:T(128)S(1)} %pad_add_fusion.where.refs_0_, bf16[4,14,176,256]{3,2,1,0:T(8,128)(2,1)} %get-tuple-element.26.refs_1_, bf16[4,14,160,256]{3,2,1,0:T(8,128)(2,1)} %get-tuple-element.27.refs_2_, bf16[4,14,176,256]{3,2,1,0:T(8,128)(2,1)} %get-tuple-element.28.refs_3_, ...), custom_call_target="tpu_custom_call" | custom-call | flops 4529848320 | bytes 18000000 | tf_op jit(solution)/shard_map/pallas_call | solution.py:271
  117.3 9.3 %shard_map.60 = (f32[1920,256]{1,0:T(8,128)S(1)}, f32[1920,256]{1,0:T(8,128)S(1)}) custom-call(s32[4]{0:T(128)S(1)} %pad_add_fusion.where.refs_0_, bf16[4,14,176,256]{3,2,1,0:T(8,128)(2,1)} %get-tuple-element.26.refs_1_, bf16[4,14,160,256]{3,2,1,0:T(8,128)(2,1)} %get-tuple-element.27.refs_2_, bf16[4,14,176,256]{3,2,1,0:T(8,128)(2,1)} %get-tuple-element.28.refs_3_, ...), custom_call_target="tpu_custom_call" | custom-call | flops 4529848320 | bytes 18000000 | tf_op jit(solution)/shard_map/pallas_call | solution.py:271
  126.7 1.0 copy-done.3
  127.7 1.0 copy-done.5
  128.7 1.3 copy-done.4
  130.0 1.3 copy-done.6
  131.3 8.7 %shard_map.61 = (bf16[1920,512]{1,0:T(8,128)(2,1)S(1)}, bf16[2,240,512]{2,1,0:T(8,128)(2,1)S(1)}, bf16[2,240,512]{2,1,0:T(8,128)(2,1)S(1)}) custom-call(s32[4]{0:T(128)S(1)} %pad_add_fusion.where.refs_0_, bf16[4,14,176,256]{3,2,1,0:T(8,128)(2,1)} %get-tuple-element.26.refs_1_, bf16[4,14,160,256]{3,2,1,0:T(8,128)(2,1)S(1)} %bitcast.6, ...), custom_call_target="tpu_custom_call" | custom-call | flops 4529848320 | bytes 18000000 | tf_op jit(solution)/shard_map/pallas_call | solution.py:271
  140.0 0.0 copy-start.8
  140.0 1.3 copy-done.8
  141.2 3.1 %collective-permute-start.13 = (bf16[2,240,512]{2,1,0:T(8,128)(2,1)S(1)}, bf16[2,240,512]{2,1,0:T(8,128)(2,1)S(1)}, u32[]{:S(2)}, u32[]{:S(2)}) collective-permute-start(bf16[2,240,512]{2,1,0:T(8,128)(2,1)S(1)} %get-tuple-element.41), channel_id=1, source_target_pairs={{0,2},{2,4},{4,6},{1,3},{3,5},{5,7},{8,10},{10,12},{12,14},{9,11},... | collective-permute-start | bytes 1474568 | tf_op jit(solution)/shard_map/ppermute | solution.py:428
  144.4 1.3 collective-permute-start.14
  145.7 0.1 collective-permute-start.17
  145.8 2.9 %collective-permute-start.20 = (bf16[4,192,256]{2,1,0:T(8,128)(2,1)}, bf16[4,192,256]{2,1,0:T(8,128)(2,1)S(1)}, u32[]{:S(2)}, u32[]{:S(2)}) collective-permute-start(bf16[4,192,256]{2,1,0:T(8,128)(2,1)} %collective-permute-done.19.refs_6_), channel_id=1, source_target_pairs={{0,32},{32,64},{64,96},{96,0},{1,97},{33,1},{65,33},{97,65},{2,34}... | collective-permute-start | bytes 1179656 | tf_op jit(solution)/shard_map/ppermute | solution.py:402
  148.7 3.7 %collective-permute-done.17.refs_3_ = bf16[4,192,256]{2,1,0:T(8,128)(2,1)S(1)} collective-permute-done((bf16[4,192,256]{2,1,0:T(8,128)(2,1)S(1)}, bf16[4,192,256]{2,1,0:T(8,128)(2,1)S(1)}, u32[]{:S(2)}, u32[]{:S(2)}) %collective-permute-start.17) | collective-permute-done | bytes 393248 | tf_op jit(solution)/shard_map/ppermute | solution.py:402
  152.4 1.3 collective-permute-done.20.refs_7_
  153.7 0.8 collective-permute-done.14.after
  154.5 0.2 copy-done.12
  154.7 0.7 copy-done.13
  155.3 18.5 %shard_map.62 = (f32[2,2,12,20,1024]{4,3,2,1,0:T(8,128)}, bf16[2,2,12,20,1024]{4,3,2,1,0:T(8,128)(2,1)}) custom-call(s32[4]{0:T(128)S(1)} %pad_add_fusion.where.refs_0_, bf16[1920,512]{1,0:T(8,128)(2,1)} %copy-done.8, bf16[2,240,512]{2,1,0:T(8,128)(2,1)} %copy-done.12, bf16[2,240,512]{2,1,0:T(8,128)(2,1)} %copy-done.13, ...), custom_call_target="tpu_custom_call" | custom-call | flops 6039797760 | bytes 12000000 | tf_op jit(solution)/shard_map/pallas_call | solution.py:363
  173.9 3.8 %copy.16 = bf16[2,2,12,20,1024]{4,1,3,2,0:T(2,128)(2,1)S(1)} copy(bf16[2,2,12,20,1024]{4,3,2,1,0:T(8,128)(2,1)} %get-tuple-element.46) | data formatting | bytes 3932160 | tf_op jit(solution)/shard_map/pallas_call | solution.py:363
  177.7 6.4 %collective-permute-start.21 = (bf16[2,2,12,20,1024]{4,1,3,2,0:T(2,128)(2,1)S(1)}, bf16[2,2,12,20,1024]{4,1,3,2,0:T(2,128)(2,1)S(1)}, u32[]{:S(2)}, u32[]{:S(2)}) collective-permute-start(bf16[2,2,12,20,1024]{4,1,3,2,0:T(2,128)(2,1)S(1)} %copy.16), channel_id=1, source_target_pairs={{0,1},{1,0},{2,3},{3,2},{4,5},{5,4},{6,7},{7,6},{8,9},{9,8},{10,11... | collective-permute-start | bytes 5898248 | tf_op jit(solution)/shard_map/ppermute | solution.py:432
  184.1 3.6 %collective-permute-done.21 = bf16[2,2,12,20,1024]{4,1,3,2,0:T(2,128)(2,1)S(1)} collective-permute-done((bf16[2,2,12,20,1024]{4,1,3,2,0:T(2,128)(2,1)S(1)}, bf16[2,2,12,20,1024]{4,1,3,2,0:T(2,128)(2,1)S(1)}, u32[]{:S(2)}, u32[]{:S(2)}) %collective-permute-start.21) | collective-permute-done | bytes 1966112 | tf_op jit(solution)/shard_map/ppermute | solution.py:432
  187.7 0.7 copy.18.received
  188.4 0.9 shard_map.63
  189.3 3.3 %copy.19 = bf16[2,2,12,20,1024]{4,1,3,2,0:T(2,128)(2,1)} copy(bf16[2,2,12,20,1024]{4,3,2,1,0:T(8,128)(2,1)S(1)} %shard_map.63) | data formatting | bytes 3932160 | tf_op jit(solution)/shard_map/pallas_call | solution.py:387
  (33 shorter events, 0.1 us)
Async XLA Ops:
  0.1 1.3 copy-start.9
  1.4 1.0 copy-start.10
  3.4 8.4 %collective-permute-start.1 = (bf16[768,256]{1,0:T(8,128)(2,1)S(1)}, bf16[768,256]{1,0:T(8,128)(2,1)S(1)}, u32[]{:S(2)}, u32[]{:S(2)}) collective-permute-start(bf16[768,256]{1,0:T(8,128)(2,1)S(1)} %get-tuple-element.30.refs_0_), channel_id=1, source_target_pairs={{0,32},{32,64},{64,96},{96,0},{1,97},{33,1},{65,33},{97,65},{2,34}... | collective-permute-start | bytes 1179656 | tf_op jit(solution)/shard_map/ppermute | solution.py:402
  7.0 8.5 %collective-permute-start.4 = (bf16[768,256]{1,0:T(8,128)(2,1)S(1)}, bf16[768,256]{1,0:T(8,128)(2,1)S(1)}, u32[]{:S(2)}, u32[]{:S(2)}) collective-permute-start(bf16[768,256]{1,0:T(8,128)(2,1)S(1)} %get-tuple-element.31.refs_4_), channel_id=1, source_target_pairs={{0,8},{8,16},{16,24},{24,0},{1,25},{9,1},{17,9},{25,17},{2,10},{10... | collective-permute-start | bytes 1179656 | tf_op jit(solution)/shard_map/ppermute | solution.py:402
  11.7 8.1 %collective-permute-start.2 = (bf16[768,256]{1,0:T(8,128)(2,1)S(1)}, bf16[768,256]{1,0:T(8,128)(2,1)S(1)}, u32[]{:S(2)}, u32[]{:S(2)}) collective-permute-start(bf16[768,256]{1,0:T(8,128)(2,1)S(1)} %collective-permute-done.1.refs_1_), channel_id=1, source_target_pairs={{0,32},{32,64},{64,96},{96,0},{1,97},{33,1},{65,33},{97,65},{2,34}... | collective-permute-start | bytes 1179656 | tf_op jit(solution)/shard_map/ppermute | solution.py:402
  15.5 7.8 %collective-permute-start.5 = (bf16[768,256]{1,0:T(8,128)(2,1)S(1)}, bf16[768,256]{1,0:T(8,128)(2,1)S(1)}, u32[]{:S(2)}, u32[]{:S(2)}) collective-permute-start(bf16[768,256]{1,0:T(8,128)(2,1)S(1)} %collective-permute-done.4.refs_5_), channel_id=1, source_target_pairs={{0,8},{8,16},{16,24},{24,0},{1,25},{9,1},{17,9},{25,17},{2,10},{10... | collective-permute-start | bytes 1179656 | tf_op jit(solution)/shard_map/ppermute | solution.py:402
  19.9 8.1 %collective-permute-start.3 = (bf16[768,256]{1,0:T(8,128)(2,1)S(1)}, bf16[768,256]{1,0:T(8,128)(2,1)S(1)}, u32[]{:S(2)}, u32[]{:S(2)}) collective-permute-start(bf16[768,256]{1,0:T(8,128)(2,1)S(1)} %collective-permute-done.2.refs_2_), channel_id=1, source_target_pairs={{0,32},{32,64},{64,96},{96,0},{1,97},{33,1},{65,33},{97,65},{2,34}... | collective-permute-start | bytes 1179656 | tf_op jit(solution)/shard_map/ppermute | solution.py:402
  23.3 7.8 %collective-permute-start.6 = (bf16[768,256]{1,0:T(8,128)(2,1)S(1)}, bf16[768,256]{1,0:T(8,128)(2,1)S(1)}, u32[]{:S(2)}, u32[]{:S(2)}) collective-permute-start(bf16[768,256]{1,0:T(8,128)(2,1)S(1)} %collective-permute-done.5.refs_6_), channel_id=1, source_target_pairs={{0,8},{8,16},{16,24},{24,0},{1,25},{9,1},{17,9},{25,17},{2,10},{10... | collective-permute-start | bytes 1179656 | tf_op jit(solution)/shard_map/ppermute | solution.py:402
  32.4 15.5 %collective-permute-start.10 = (bf16[4,576,256]{2,1,0:T(8,128)(2,1)S(1)}, bf16[4,576,256]{2,1,0:T(8,128)(2,1)S(1)}, u32[]{:S(2)}, u32[]{:S(2)}) collective-permute-start(bf16[4,576,256]{2,1,0:T(8,128)(2,1)S(1)} %get-tuple-element.33.refs_6_), channel_id=1, source_target_pairs={{0,32},{32,64},{64,96},{96,0},{1,97},{33,1},{65,33},{97,65},{2,34}... | collective-permute-start | bytes 3538952 | tf_op jit(solution)/shard_map/ppermute | solution.py:402
  33.0 16.7 %collective-permute-start.7 = (bf16[4,576,256]{2,1,0:T(8,128)(2,1)S(1)}, bf16[4,576,256]{2,1,0:T(8,128)(2,1)}, u32[]{:S(2)}, u32[]{:S(2)}) collective-permute-start(bf16[4,576,256]{2,1,0:T(8,128)(2,1)S(1)} %get-tuple-element.32.refs_5_), channel_id=1, source_target_pairs={{0,8},{8,16},{16,24},{24,0},{1,25},{9,1},{17,9},{25,17},{2,10},{10... | collective-permute-start | bytes 3538952 | tf_op jit(solution)/shard_map/ppermute | solution.py:402
  36.1 37.7 %collective-permute-start = (bf16[2,2,12,20,1024]{4,1,3,2,0:T(2,128)(2,1)}, bf16[2,2,12,20,1024]{4,1,3,2,0:T(2,128)(2,1)}, u32[]{:S(2)}, u32[]{:S(2)}) collective-permute-start(bf16[2,2,12,20,1024]{4,1,3,2,0:T(2,128)(2,1)} %param.5), channel_id=1, source_target_pairs={{0,1},{1,0},{2,3},{3,2},{4,5},{5,4},{6,7},{7,6},{8,9},{9,8},{10,11... | collective-permute-start | bytes 5898248 | tf_op jit(solution)/shard_map/ppermute | solution.py:408
  47.9 49.2 %collective-permute-start.11 = (bf16[4,576,256]{2,1,0:T(8,128)(2,1)S(1)}, bf16[4,576,256]{2,1,0:T(8,128)(2,1)}, u32[]{:S(2)}, u32[]{:S(2)}) collective-permute-start(bf16[4,576,256]{2,1,0:T(8,128)(2,1)S(1)} %collective-permute-done.10.refs_6_), channel_id=1, source_target_pairs={{0,32},{32,64},{64,96},{96,0},{1,97},{33,1},{65,33},{97,65},{2,34}... | collective-permute-start | bytes 3538952 | tf_op jit(solution)/shard_map/ppermute | solution.py:402
  49.6 47.5 %collective-permute-start.8 = (bf16[4,576,256]{2,1,0:T(8,128)(2,1)}, bf16[4,576,256]{2,1,0:T(8,128)(2,1)}, u32[]{:S(2)}, u32[]{:S(2)}) collective-permute-start(bf16[4,576,256]{2,1,0:T(8,128)(2,1)} %collective-permute-done.7.refs_5_), channel_id=1, source_target_pairs={{0,8},{8,16},{16,24},{24,0},{1,25},{9,1},{17,9},{25,17},{2,10},{10... | collective-permute-start | bytes 3538952 | tf_op jit(solution)/shard_map/ppermute | solution.py:402
  52.6 17.7 %collective-permute-start.15 = (bf16[4,192,256]{2,1,0:T(8,128)(2,1)}, bf16[4,192,256]{2,1,0:T(8,128)(2,1)}, u32[]{:S(2)}, u32[]{:S(2)}) collective-permute-start(bf16[4,192,256]{2,1,0:T(8,128)(2,1)} %get-tuple-element.43.refs_0_), channel_id=1, source_target_pairs={{0,8},{8,16},{16,24},{24,0},{1,25},{9,1},{17,9},{25,17},{2,10},{10... | collective-permute-start | bytes 1179656 | tf_op jit(solution)/shard_map/ppermute | solution.py:402
  52.7 3.7 %copy-start.11 = (f32[1024]{0:T(1024)S(1)}, f32[1024]{0:T(1024)}, u32[]{:S(2)}) copy-start(f32[1024]{0:T(1024)} %param.8) | copy-start | bytes 12292
  52.7 21.1 %collective-permute-start.18 = (bf16[4,192,256]{2,1,0:T(8,128)(2,1)}, bf16[4,192,256]{2,1,0:T(8,128)(2,1)}, u32[]{:S(2)}, u32[]{:S(2)}) collective-permute-start(bf16[4,192,256]{2,1,0:T(8,128)(2,1)} %get-tuple-element.44.refs_4_), channel_id=1, source_target_pairs={{0,32},{32,64},{64,96},{96,0},{1,97},{33,1},{65,33},{97,65},{2,34}... | collective-permute-start | bytes 1179656 | tf_op jit(solution)/shard_map/ppermute | solution.py:402
  57.8 19.5 %copy-start.7 = (f32[1024]{0:T(1024)S(1)}, f32[1024]{0:T(1024)}, u32[]{:S(2)}) copy-start(f32[1024]{0:T(1024)} %param.6) | copy-start | bytes 12292
  70.3 75.4 %collective-permute-start.16 = (bf16[4,192,256]{2,1,0:T(8,128)(2,1)}, bf16[4,192,256]{2,1,0:T(8,128)(2,1)S(1)}, u32[]{:S(2)}, u32[]{:S(2)}) collective-permute-start(bf16[4,192,256]{2,1,0:T(8,128)(2,1)} %collective-permute-done.15.refs_1_), channel_id=1, source_target_pairs={{0,8},{8,16},{16,24},{24,0},{1,25},{9,1},{17,9},{25,17},{2,10},{10... | collective-permute-start | bytes 1179656 | tf_op jit(solution)/shard_map/ppermute | solution.py:402
  73.7 72.1 %collective-permute-start.19 = (bf16[4,192,256]{2,1,0:T(8,128)(2,1)}, bf16[4,192,256]{2,1,0:T(8,128)(2,1)}, u32[]{:S(2)}, u32[]{:S(2)}) collective-permute-start(bf16[4,192,256]{2,1,0:T(8,128)(2,1)} %collective-permute-done.18.refs_5_), channel_id=1, source_target_pairs={{0,32},{32,64},{64,96},{96,0},{1,97},{33,1},{65,33},{97,65},{2,34}... | collective-permute-start | bytes 1179656 | tf_op jit(solution)/shard_map/ppermute | solution.py:402
  97.1 29.5 %collective-permute-start.12 = (bf16[4,576,256]{2,1,0:T(8,128)(2,1)}, bf16[4,576,256]{2,1,0:T(8,128)(2,1)S(1)}, u32[]{:S(2)}, u32[]{:S(2)}) collective-permute-start(bf16[4,576,256]{2,1,0:T(8,128)(2,1)} %collective-permute-done.11.refs_6_), channel_id=1, source_target_pairs={{0,32},{32,64},{64,96},{96,0},{1,97},{33,1},{65,33},{97,65},{2,34}... | collective-permute-start | bytes 3538952 | tf_op jit(solution)/shard_map/ppermute | solution.py:402
  97.2 30.5 %collective-permute-start.9 = (bf16[4,576,256]{2,1,0:T(8,128)(2,1)}, bf16[4,576,256]{2,1,0:T(8,128)(2,1)S(1)}, u32[]{:S(2)}, u32[]{:S(2)}) collective-permute-start(bf16[4,576,256]{2,1,0:T(8,128)(2,1)} %collective-permute-done.8.refs_5_), channel_id=1, source_target_pairs={{0,8},{8,16},{16,24},{24,0},{1,25},{9,1},{17,9},{25,17},{2,10},{10... | collective-permute-start | bytes 3538952 | tf_op jit(solution)/shard_map/ppermute | solution.py:402
  97.4 2.3 %copy-start = (bf16[4,14,160,256]{3,2,1,0:T(8,128)(2,1)S(1)}, bf16[4,14,160,256]{3,2,1,0:T(8,128)(2,1)}, u32[]{:S(2)}) copy-start(bf16[4,14,160,256]{3,2,1,0:T(8,128)(2,1)} %get-tuple-element.27.refs_2_) | copy-start | bytes 13762564
  117.3 11.4 %slice-start = ((s8[4587520]{0:T(1024)(128)(4,1)}), s8[4194304]{0:T(1024)(128)(4,1)S(1)}, s32[]{:S(2)}) async-start(s8[4587520]{0:T(1024)(128)(4,1)} %bitcast.5), calls=%async_computation | async-start | bytes 8388608
  117.3 11.4 %slice-start.1 = ((s8[4587520]{0:T(1024)(128)(4,1)}), s8[393216]{0:T(1024)(128)(4,1)S(1)}, s32[]{:S(2)}) async-start(s8[4587520]{0:T(1024)(128)(4,1)} %bitcast.5), calls=%async_computation.1 | async-start | bytes 786432
  126.6 1.0 copy-start.3
  127.7 1.0 copy-start.5
  128.7 1.3 copy-start.4
  130.0 1.3 copy-start.6
  140.0 1.3 copy-start.8
  141.2 12.5 %collective-permute-start.13 = (bf16[2,240,512]{2,1,0:T(8,128)(2,1)S(1)}, bf16[2,240,512]{2,1,0:T(8,128)(2,1)S(1)}, u32[]{:S(2)}, u32[]{:S(2)}) collective-permute-start(bf16[2,240,512]{2,1,0:T(8,128)(2,1)S(1)} %get-tuple-element.41), channel_id=1, source_target_pairs={{0,2},{2,4},{4,6},{1,3},{3,5},{5,7},{8,10},{10,12},{12,14},{9,11},... | collective-permute-start | bytes 1474568 | tf_op jit(solution)/shard_map/ppermute | solution.py:428
  144.4 10.1 %collective-permute-start.14 = (bf16[2,240,512]{2,1,0:T(8,128)(2,1)S(1)}, bf16[2,240,512]{2,1,0:T(8,128)(2,1)S(1)}, u32[]{:S(2)}, u32[]{:S(2)}) collective-permute-start(bf16[2,240,512]{2,1,0:T(8,128)(2,1)S(1)} %get-tuple-element.42), channel_id=1, source_target_pairs={{2,0},{4,2},{6,4},{3,1},{5,3},{7,5},{10,8},{12,10},{14,12},{11,9},... | collective-permute-start | bytes 1474568 | tf_op jit(solution)/shard_map/ppermute | solution.py:429
  145.7 6.7 %collective-permute-start.17 = (bf16[4,192,256]{2,1,0:T(8,128)(2,1)S(1)}, bf16[4,192,256]{2,1,0:T(8,128)(2,1)S(1)}, u32[]{:S(2)}, u32[]{:S(2)}) collective-permute-start(bf16[4,192,256]{2,1,0:T(8,128)(2,1)S(1)} %collective-permute-done.16.refs_2_), channel_id=1, source_target_pairs={{0,8},{8,16},{16,24},{24,0},{1,25},{9,1},{17,9},{25,17},{2,10},{10... | collective-permute-start | bytes 1179656 | tf_op jit(solution)/shard_map/ppermute | solution.py:402
  145.8 7.9 %collective-permute-start.20 = (bf16[4,192,256]{2,1,0:T(8,128)(2,1)}, bf16[4,192,256]{2,1,0:T(8,128)(2,1)S(1)}, u32[]{:S(2)}, u32[]{:S(2)}) collective-permute-start(bf16[4,192,256]{2,1,0:T(8,128)(2,1)} %collective-permute-done.19.refs_6_), channel_id=1, source_target_pairs={{0,32},{32,64},{64,96},{96,0},{1,97},{33,1},{65,33},{97,65},{2,34}... | collective-permute-start | bytes 1179656 | tf_op jit(solution)/shard_map/ppermute | solution.py:402
  153.7 0.8 copy-start.14
  153.7 0.9 copy-start.12
  154.5 0.8 copy-start.13
  173.9 14.5 %copy-start.2 = (f32[2,2,12,20,1024]{4,3,2,1,0:T(8,128)S(1)}, f32[2,2,12,20,1024]{4,3,2,1,0:T(8,128)}, u32[]{:S(2)}) copy-start(f32[2,2,12,20,1024]{4,3,2,1,0:T(8,128)} %get-tuple-element.45.mine) | copy-start | bytes 11796484
  177.7 10.6 %copy-start.1 = (bf16[2,2,12,20,1024]{4,3,2,1,0:T(8,128)(2,1)S(1)}, bf16[2,2,12,20,1024]{4,3,2,1,0:T(8,128)(2,1)}, u32[]{:S(2)}) copy-start(bf16[2,2,12,20,1024]{4,3,2,1,0:T(8,128)(2,1)} %copy.17.own.video) | copy-start | bytes 5898244
  177.7 10.0 %collective-permute-start.21 = (bf16[2,2,12,20,1024]{4,1,3,2,0:T(2,128)(2,1)S(1)}, bf16[2,2,12,20,1024]{4,1,3,2,0:T(2,128)(2,1)S(1)}, u32[]{:S(2)}, u32[]{:S(2)}) collective-permute-start(bf16[2,2,12,20,1024]{4,1,3,2,0:T(2,128)(2,1)S(1)} %copy.16), channel_id=1, source_target_pairs={{0,1},{1,0},{2,3},{3,2},{4,5},{5,4},{6,7},{7,6},{8,9},{9,8},{10,11... | collective-permute-start | bytes 5898248 | tf_op jit(solution)/shard_map/ppermute | solution.py:432

commit v2 on v0

v2 whole, which is shorter than its diff:
```python
import functools

import jax
import jax.numpy as jnp
from jax import lax
from jax.experimental import pallas as pl
from jax.experimental.pallas import tpu as pltpu
from jax.sharding import Mesh
from jax.sharding import PartitionSpec as P

EPSILON = 1e-06
F32, BF16 = jnp.float32, jnp.bfloat16
MIB = 2**20

ROWS, COLS, SLOTS = 12, 20, 8
LINE = COLS * SLOTS
POINTS = ROWS * LINE


def silu(v):
    return v / (1.0 + jnp.exp(-v))


def specs(*kinds):
    places = {"s": pltpu.SMEM, "v": pltpu.VMEM, "h": pltpu.HBM}
    return [pl.BlockSpec(memory_space=places[kind]) for kind in kinds]


def params(mib):
    return pltpu.CompilerParams(vmem_limit_bytes=mib * MIB)


def cost(flops, bytes_accessed):
    return pl.CostEstimate(flops=flops, bytes_accessed=bytes_accessed, transcendentals=0)


def pack_kernel(where, spatial, temporal, unit_a, unit_b):
    core = where[3]
    source = lax.broadcasted_iota(jnp.int32, (256, 128), 0)
    target = lax.broadcasted_iota(jnp.int32, (256, 128), 1)
    wanted = (target >> 5) * 64 + (target & 31) + core * 32
    pick = jnp.where(source == wanted, 1.0, 0.0).astype(BF16)
    for part in range(4):
        unit = (unit_a, unit_b)[part // 2]
        columns = spatial[:, :, part * 256 : (part + 1) * 256].reshape(576, 256)
        kept = jnp.dot(columns, pick, preferred_element_type=F32).astype(BF16)
        unit[0:576, (part % 2) * 128 : (part % 2 + 1) * 128] = kept
    for tap in range(3):
        rows = temporal[tap, pl.ds(pl.multiple_of(core * 32, 32), 32), :]
        for part in range(4):
            unit = (unit_a, unit_b)[part // 2]
            start = 576 + (part % 2) * 96 + tap * 32
            unit[start : start + 32, :] = rows[:, part * 256 : (part + 1) * 256]


def pack(where, spatial, temporal):
    unit = jax.ShapeDtypeStruct((768, 256), BF16)
    return pl.pallas_call(
        pack_kernel,
        out_shape=(unit, unit),
        in_specs=specs("s", "v", "v"),
        out_specs=specs("v", "v"),
        compiler_params=params(16),
        cost_estimate=cost(10**9, 3 * 10**6),
    )(where, spatial, temporal)


def norm_kernel(video, gain, active, flat, lines, plain):
    scale = gain[...]
    for i in range(ROWS):
        values = video[0, 0, i].astype(F32)
        mean = jnp.mean(values * values, axis=-1, keepdims=True)
        lines[i * COLS : (i + 1) * COLS, :] = silu(values * lax.rsqrt(mean + EPSILON) * scale)
        plain[i * COLS : (i + 1) * COLS, :] = values
    active[0] = lines[...].astype(BF16)
    flat[0] = plain[...].astype(BF16)


def norm(video, gain):
    return pl.pallas_call(
        norm_kernel,
        grid=(4,),
        out_shape=(jax.ShapeDtypeStruct((4, ROWS * COLS, 1024), BF16),) * 2,
        in_specs=[
            pl.BlockSpec((1, 1, ROWS, COLS, 1024), lambda i: (i // 2, i % 2, 0, 0, 0)),
            pl.BlockSpec((1, 1024), lambda i: (0, 0)),
        ],
        out_specs=(pl.BlockSpec((1, ROWS * COLS, 1024), lambda i: (i, 0, 0)),) * 2,
        scratch_shapes=[pltpu.VMEM((ROWS * COLS, 1024), F32)] * 2,
        compiler_params=params(24),
        cost_estimate=cost(2 * 10**9, 20 * 10**6),
    )(video, gain)


def spread_kernel(where, own, other, wide_a, wide_b, active):
    core = where[3]
    for relative, source in ((0, own), (1, other)):
        owner = core if relative == 0 else 1 - core
        for index in range(2):
            for frame in range(2):
                slot = (2 * owner + frame) * 2 + index
                for part in range(8):
                    values = source[index * 2 + frame, :, part * 128 : (part + 1) * 128]
                    active[part, pl.ds(slot, ROWS * COLS, stride=SLOTS), :] = values.astype(F32)

    low = lax.broadcasted_iota(jnp.int32, (LINE, 128), 1) < 64
    edge = jnp.zeros((SLOTS, 256), F32)

    def put(wide, block, i, value):
        wide[block, i + 1] = jnp.concatenate([edge, value, edge], axis=0).astype(BF16)

    def line(i, carry):
        lines = [active[part, pl.ds(i * LINE, LINE), :] for part in range(8)]
        for y in range(4):
            put(wide_b, y, i, jnp.concatenate([lines[2 * y], lines[2 * y + 1]], axis=1))
        turned = [pltpu.roll(value, 64, 1) for value in lines]
        for z in range(4):
            halves = []
            for y in (0, 2):
                first, second = y * 2 + z // 2, (y + 1) * 2 + z // 2
                if z % 2 == 0:
                    halves.append(jnp.where(low, lines[first], turned[second]))
                else:
                    halves.append(jnp.where(low, turned[first], lines[second]))
            put(wide_a, z, i, jnp.concatenate(halves, axis=1))
        return carry

    for block in range(4):
        for i in (0, ROWS + 1):
            for ref in (wide_a, wide_b):
                ref[block, i] = jnp.zeros(ref.shape[2:], BF16)
    lax.fori_loop(0, ROWS, line, 0)


def spread(where, own, other):
    wide = jax.ShapeDtypeStruct((4, ROWS + 2, LINE + 16, 256), BF16)
    return pl.pallas_call(
        spread_kernel,
        out_shape=(wide, wide),
        in_specs=specs("s", "v", "v"),
        out_specs=specs("v", "v"),
        scratch_shapes=[pltpu.VMEM((8, POINTS, 128), F32)],
        compiler_params=params(24),
        cost_estimate=cost(2 * 10**9, 25 * 10**6),
    )(where, own, other)


def pick_kernel(where, *refs):
    core = where[3]
    for index in range(2):
        for side in range(2):

            @pl.when(core == side)
            def _(source=refs[index * 2 + side], target=refs[4 + index]):
                target[...] = source[...]


def pick(where, *units):
    unit = jax.ShapeDtypeStruct((768, 256), BF16)
    return pl.pallas_call(
        pick_kernel,
        out_shape=(unit, unit),
        in_specs=specs(*"svvvv"),
        out_specs=specs(*"vv"),
        compiler_params=params(8),
        cost_estimate=cost(0, 2 * 10**6),
    )(where, *units)


def stack_kernel(*refs):
    units, wholes = refs[:8], refs[8:]
    for index in range(8):
        wholes[index // 4][index % 4] = units[index][...]


def stack(units):
    whole = jax.ShapeDtypeStruct((4, 768, 256), BF16)
    return pl.pallas_call(
        stack_kernel,
        out_shape=(whole, whole),
        in_specs=specs(*"vvvvvvvv"),
        out_specs=specs(*"vv"),
        compiler_params=params(12),
        cost_estimate=cost(0, 6 * 10**6),
    )(*units)


def divide_kernel(where, *refs):
    core = where[3]
    for index in range(2):
        for side in range(2):

            @pl.when(core == side)
            def _(source=refs[index * 2 + side], spatial=refs[4 + index], temporal=refs[6 + index]):
                for slot in range(4):
                    spatial[slot] = source[slot, 0:576, :]
                    temporal[slot] = source[slot, 576:768, :]


def divide(where, *wholes):
    spatial = jax.ShapeDtypeStruct((4, 576, 256), BF16)
    temporal = jax.ShapeDtypeStruct((4, 192, 256), BF16)
    return pl.pallas_call(
        divide_kernel,
        out_shape=(spatial, spatial, temporal, temporal),
        in_specs=specs(*"svvvv"),
        out_specs=specs(*"vvvv"),
        compiler_params=params(16),
        cost_estimate=cost(0, 6 * 10**6),
    )(where, *wholes)


def conv_kernel(step, colours, *refs):
    first, last = step == 0, step == 2
    count = len(colours)
    where, refs = refs[0], refs[1:]
    wide, refs = refs[:count], refs[count:]
    pieces, refs = refs[:count], refs[count:]
    if not first:
        sums, refs = refs[:count], refs[count:]
    if last:
        bias, refs = refs[0], refs[1:]
        if colours[0] > 0:
            earlier, refs = refs[:2], refs[2:]
        hidden, lower, upper, kernel, sides = refs
        if colours[0] > 0:
            for ref, source in zip((lower, upper), earlier):
                ref[0] = source[0]
    else:
        out, kernel = refs[:count], refs[count]
    y, z = where[0], where[1]
    mine = (z, y)
    across = (y, z)
    lines = 6
    for number, colour in enumerate(colours):
        block = (mine[colour] - step + 4) & 3
        for slot in range(4):
            place = (across[colour] - slot + 4) & 3
            for tap in range(9):
                kernel[number, pl.ds(pl.multiple_of(tap * 256 + place * 64, 64), 64), :] = pieces[number][
                    slot, tap * 64 : (tap + 1) * 64, :
                ]

        def part(group, carry, number=number, colour=colour, block=block):
            i = group * lines
            total = None
            for tap in range(9):
                dy, dx = tap // 3, tap % 3
                window = wide[number][block, pl.ds(i + dy, lines), dx * 8 : dx * 8 + LINE, :]
                product = jnp.dot(
                    window.reshape(lines * LINE, 256),
                    kernel[number, tap * 256 : (tap + 1) * 256, :],
                    preferred_element_type=F32,
                )
                total = product if total is None else total + product
            rows = pl.ds(pl.multiple_of(i * LINE, lines * LINE), lines * LINE)
            if not first:
                total = total + sums[number][rows, :]
            if last:
                total = silu(total + bias[:, colour * 256 : (colour + 1) * 256])
                hidden[rows, :] = total.astype(BF16)
                for half in range(2):
                    sides[half, rows, :] = total[:, half * 128 : (half + 1) * 128]
            else:
                out[number][rows, :] = total
            return carry

        lax.fori_loop(0, ROWS // lines, part, 0)
        if last:
            for half in range(2):
                columns = slice(half * 128, (half + 1) * 128)
                for index in range(2):
                    for ref, slot in ((lower, index), (upper, 6 + index)):
                        values = sides[half, pl.ds(slot, ROWS * COLS, stride=SLOTS), :]
                        ref[colour, index, :, columns] = values.astype(BF16)


def conv(step, colours, where, active, spatial, sums=None, bias=None, sides=()):
    count = len(colours)
    operands = [where, *active, *spatial]
    kinds = "s" + "vv" * count
    scratch = [pltpu.VMEM((count, 2304, 256), BF16)]
    aliases = {}
    if step > 0:
        if step != 2:
            aliases = {len(operands) + number: number for number in range(count)}
        operands += sums
        kinds += "v" * count
    if step == 2:
        operands.append(bias)
        kinds += "v"
        operands += sides
        kinds += "v" * len(sides)
        side = jax.ShapeDtypeStruct((2, 2, ROWS * COLS, 256), BF16)
        out_shape = (jax.ShapeDtypeStruct((POINTS, 256), BF16), side, side)
        out_specs = specs(*"vvv")
        scratch += [pltpu.VMEM((2, POINTS, 128), F32)]
    else:
        total = jax.ShapeDtypeStruct((POINTS, 256), F32)
        out_shape, out_specs = (total,) * count, specs(*"v" * count)
    return pl.pallas_call(
        functools.partial(conv_kernel, step, colours),
        out_shape=out_shape,
        in_specs=specs(*kinds),
        out_specs=out_specs,
        scratch_shapes=scratch,
        input_output_aliases=aliases,
        compiler_params=params(16),
        cost_estimate=cost(4 * 10**9 * count, 12 * 10**6 * count),
    )(*operands)


def shift_kernel(hidden_a, hidden_b, earlier, later):
    slot = lax.broadcasted_iota(jnp.int32, (LINE, 128), 0) & 7
    for part in range(4):
        source, columns = (hidden_a, hidden_b)[part // 2], slice(part % 2 * 128, (part % 2 + 1) * 128)

        def move(i, carry, source=source, columns=columns, part=part):
            rows = pl.ds(pl.multiple_of(i * LINE, LINE), LINE)
            values = source[rows, columns].astype(F32)
            target = slice(part * 128, (part + 1) * 128)
            earlier[rows, target] = jnp.where(slot >= 2, pltpu.roll(values, 2, 0), 0.0).astype(BF16)
            later[rows, target] = jnp.where(slot < 6, pltpu.roll(values, LINE - 2, 0), 0.0).astype(BF16)
            return carry

        lax.fori_loop(0, ROWS, move, 0)


def shift(hidden):
    moved = jax.ShapeDtypeStruct((POINTS, 512), BF16)
    return pl.pallas_call(
        shift_kernel,
        out_shape=(moved, moved),
        in_specs=specs("v", "v"),
        out_specs=specs("v", "v"),
        compiler_params=params(16),
        cost_estimate=cost(10**9, 6 * 10**6),
    )(*hidden)


def place_weights(where, blocks, steps, first_row, targets):
    y, z = where[0], where[1]
    for number, ref in enumerate(blocks):
        colour, step = number % 2, steps[number // 2]
        for unit in range(4):
            fixed, moving = (unit, step) if colour == 0 else (step, unit)
            row, column = (y - fixed + 4) & 3, (z - moving + 4) & 3
            place = pl.ds(pl.multiple_of((row * 4 + column) * 32, 32), 32)
            for half in range(2):
                columns = slice((colour * 2 + half) * 256, (colour * 2 + half + 1) * 256)
                start = first_row + half * 96
                for tap, target in enumerate(targets):
                    target[place, columns] = ref[unit, start + tap * 32 : start + tap * 32 + 32, :]


def ready_kernel(where, *refs):
    blocks, weights = refs[:6], refs[6]
    place_weights(where, blocks, (0, 1, 3), 576, [weights.at[tap] for tap in range(3)])


def ready(where, blocks):
    return pl.pallas_call(
        ready_kernel,
        out_shape=jax.ShapeDtypeStruct((3, 512, 1024), BF16),
        in_specs=specs(*"svvvvvv"),
        out_specs=pl.BlockSpec(memory_space=pltpu.VMEM),
        compiler_params=params(18),
        cost_estimate=cost(0, 5 * 10**6),
    )(where, *blocks)


def centre_kernel(where, hidden_a, hidden_b, earlier, later, weights, block_a, block_b, *refs):
    calm_theirs, calm_mine, rough_theirs, rough_mine, edge, middle, total = refs
    core = where[3]
    edge[0], middle[...], edge[1] = weights[0], weights[1], weights[2]
    place_weights(where, (block_a, block_b), (2,), 0, (edge.at[0], middle, edge.at[1]))
    for part in range(4):
        columns = slice(part * 256, (part + 1) * 256)
        for group in range(2):
            rows = slice(group * 960, (group + 1) * 960)
            value = jnp.dot(hidden_a[rows, :], middle[0:256, columns], preferred_element_type=F32)
            value = value + jnp.dot(hidden_b[rows, :], middle[256:512, columns], preferred_element_type=F32)
            value = value + jnp.dot(earlier[rows, :], edge[0, :, columns], preferred_element_type=F32)
            value = value + jnp.dot(later[rows, :], edge[1, :, columns], preferred_element_type=F32)
            for half in range(2):
                total[part * 2 + half, rows, :] = value[:, half * 128 : (half + 1) * 128]
        for index in range(2):
            for target, owner, frame in (
                (calm_theirs, 1 - core, core),
                (rough_theirs, 1 - core, 1 - core),
                (calm_mine, core, 1 - core),
                (rough_mine, core, core),
            ):
                start = (2 * owner + frame) * 2 + index
                for half in (part * 2, part * 2 + 1):
                    values = total[half, pl.ds(start, ROWS * COLS, stride=SLOTS), :]
                    target[index, :, half * 128 : (half + 1) * 128] = values.astype(target.dtype)


PAIR = (2, ROWS * COLS, 1024)


def centre(where, hidden, moved, weights, blocks):
    wide, narrow = jax.ShapeDtypeStruct(PAIR, F32), jax.ShapeDtypeStruct(PAIR, BF16)
    return pl.pallas_call(
        centre_kernel,
        out_shape=(narrow, wide, wide, wide, jax.ShapeDtypeStruct((2, 512, 1024), BF16)),
        in_specs=specs(*"svvvvvvv"),
        out_specs=specs(*"vvvvv"),
        scratch_shapes=[pltpu.VMEM((512, 1024), BF16), pltpu.VMEM((8, POINTS, 128), F32)],
        compiler_params=params(32),
        cost_estimate=cost(10**10, 12 * 10**6),
    )(where, *hidden, *moved, weights, *blocks)


def edge_kernel(own, where, before, behind, weights, calm, result):
    core = where[3]
    for side, halo in enumerate((before, behind)):

        @pl.when(core == side if own else core != side)
        def _(side=side, halo=halo):
            for index in range(2):
                value = jnp.dot(halo[0, index], weights[side, 0:256, :], preferred_element_type=F32)
                value = value + jnp.dot(halo[1, index], weights[side, 256:512, :], preferred_element_type=F32)
                result[index] = (calm[index] + value).astype(result.dtype)


def edges(own, where, before, behind, weights, calm):
    return pl.pallas_call(
        functools.partial(edge_kernel, own),
        out_shape=jax.ShapeDtypeStruct(PAIR, F32 if own else BF16),
        in_specs=specs(*"svvvv"),
        out_specs=pl.BlockSpec(memory_space=pltpu.VMEM),
        compiler_params=params(24),
        cost_estimate=cost(3 * 10**9, 6 * 10**6),
    )(where, before, behind, weights, calm)


def finish_kernel(where, video, calm_mine, calm_received, rough_mine, rough_received, result, lines):
    core, index = where[3], pl.program_id(0)
    for part in range(8):
        columns = slice(part * 128, (part + 1) * 128)
        for frame, mine, received in (
            (core, rough_mine, rough_received),
            (1 - core, calm_mine, calm_received),
        ):
            value = video[2 * index + frame, :, columns].astype(F32) + (
                mine[index, :, columns] + received[index, :, columns].astype(F32)
            )
            lines[part, pl.ds(frame, ROWS * COLS, stride=2), :] = value
        for i in range(ROWS):
            value = lines[part, i * 2 * COLS : (i + 1) * 2 * COLS, :]
            result[0, i, :, :, columns] = value.astype(BF16).reshape(COLS, 2, 128)


def finish(where, video, *parts):
    shown = pl.pallas_call(
        finish_kernel,
        grid=(2,),
        out_shape=jax.ShapeDtypeStruct((2, ROWS, COLS, 2, 1024), BF16),
        in_specs=specs(*"svvvvv"),
        out_specs=pl.BlockSpec((1, ROWS, COLS, 2, 1024), lambda i: (i, 0, 0, 0, 0)),
        scratch_shapes=[pltpu.VMEM((8, 2 * ROWS * COLS, 128), F32)],
        compiler_params=params(24),
        cost_estimate=cost(3 * 10**6, 10 * 10**6),
    )(where, video, *parts)
    return shown.transpose(0, 3, 1, 2, 4)


def ring(value, axis):
    count = lax.axis_size(axis)
    pairs = [(i * 2, (i + 1) % count * 2) for i in range(count)]
    pairs += [(i * 2 + 1, (i - 1) % count * 2 + 1) for i in range(count)]
    return lax.ppermute(value, (axis, "core"), pairs)


def after(value, *others):
    return lax.optimization_barrier((value, *others))[0]


def step_to(value, axis, distance):
    count = lax.axis_size(axis)
    return lax.ppermute(value, axis, [(i, (i + distance) % count) for i in range(count)])


def shards(video, norm_gain, spatial_weight, spatial_bias, temporal_weight):
    where = jnp.stack([lax.axis_index(axis) for axis in ("y", "z", "x", "core")]).astype(jnp.int32)
    swap = [(0, 1), (1, 0)]
    bias = spatial_bias.reshape(16, 2, 32)[:, where[3], :].reshape(1, 512)
    unit_a, unit_b = pack(where, spatial_weight, temporal_weight)

    a1, b1 = step_to(unit_a, "y", 1), step_to(unit_b, "z", 1)
    a3, b3 = step_to(unit_a, "y", -1), step_to(unit_b, "z", -1)
    own, flat = norm(after(video, unit_a, unit_b, bias), norm_gain.reshape(1, 1024))
    other = lax.ppermute(after(own, a1, b1, a3, b3), "core", swap)
    a2, b2 = pick(where, after(a1, own, flat), a3, b1, b3)
    a2, b2 = ring(a2, "y"), ring(b2, "z")
    whole_a, whole_b = stack((unit_a, a1, a2, a3, unit_b, b1, b2, b3))

    both = (0, 1)
    whole_1 = step_to(whole_a, "z", 1), step_to(whole_b, "y", 1)
    whole_3 = step_to(whole_a, "z", -1), step_to(whole_b, "y", -1)
    active = spread(where, after(own, whole_a), other)
    sums = conv(0, both, where, active, (whole_a, whole_b))
    sa, sb, ta, tb = divide(where, after(whole_1[0], sums[0]), whole_3[0], whole_1[1], whole_3[1])
    sa, sb = ring(sa, "z"), ring(sb, "y")
    sums = conv(1, both, where, active, whole_1, sums)
    sums = conv(3, both, where, active, whole_3, sums)
    weights = ready(where, (whole_a, whole_b, *whole_1, *whole_3))
    ta, tb = ring(after(ta, sums[0]), "z"), ring(after(tb, sums[0]), "y")
    sa, sb = after(sa, sums[0], weights), after(sb, sums[0], weights)
    hidden_a, *sides = conv(2, (0,), where, active[:1], (sa,), sums[:1], bias)
    hidden_b, lower, upper = conv(2, (1,), where, active[1:], (sb,), sums[1:], bias, sides)
    count = lax.axis_size("x")
    before = lax.ppermute(upper, "x", [(i, i + 1) for i in range(count - 1)])
    behind = lax.ppermute(lower, "x", [(i + 1, i) for i in range(count - 1)])
    hidden = hidden_a, hidden_b
    moved = shift(hidden)
    calm_theirs, calm_mine, rough_theirs, rough_mine, weights = centre(where, hidden, moved, weights, (ta, tb))
    calm_received = lax.ppermute(calm_theirs, "core", swap)
    before = after(before, weights)
    sent = edges(False, where, before, behind, weights, rough_theirs)
    rough_received = lax.ppermute(sent, "core", swap)
    rough_mine = edges(True, where, before, behind, weights, after(rough_mine, sent))
    return finish(where, flat, calm_mine, calm_received, rough_mine, rough_received)


def solution(mesh):
    parts = Mesh(mesh.devices.reshape(4, 4, 4, 2), ("y", "z", "x", "core"))
    dp, frame = ("y", "z"), ("x", "core")
    in_specs = (
        P(dp, frame, None, None, None),
        P(),
        P(None, dp, None),
        P(),
        P(None, dp, None),
    )
    out_specs = P(dp, frame, None, None, None)
    return jax.shard_map(shards, mesh=parts, in_specs=in_specs, out_specs=out_specs, check_vma=False)
```

time: 243 us -> 124 us (0.51)
  waiting for transfers between devices: 118 us -> 35.4 us
  Pallas kernels: 0 us -> 53.1 us
  matrix products: 42.1 us -> 0 us
  local copies, waits for them, and re-layouts: 38.5 us -> 4.68 us
  starting transfers between devices: 5.58 us -> 29.8 us
  other arithmetic: 22.6 us -> 0.08 us
  between operations: 13.8 us -> 0.24 us
    all_gather x2 -> x0, waiting for transfers between devices: 105 us -> none  [the longest x1 105 us: shards(): piece = lax.all_gather(spatial_weight, 'dp', axis=1, tiled=True)]
    pallas_call x0 -> x17, Pallas kernels: none -> 53.1 us  [the longest x5 25.2 us: conv(): pl.pallas_call(functools.partial(conv_kernel, step, colours), out_shape=o...]
    conv_general_dilated x2 -> x0, matrix products: 42.1 us -> none  [the longest x1 28.2 us: spatial_conv(): lax.conv_general_dilated(inputs, kernel, (1, 1), ((1, 1), (1, 1)), dimens...]
    ppermute x2 -> x19, starting transfers between devices: 5.53 us -> 29.8 us  [the longest x8 11.6 us: step_to(): lax.ppermute(value, axis, [(i, (i + distance) % count) for i in range(cou...]
    ppermute x2 -> x19, waiting for transfers between devices: 12 us -> 35.4 us  [the longest x8 27.8 us: step_to(): lax.ppermute(value, axis, [(i, (i + distance) % count) for i in range(cou...]
    convert_element_type x5 -> x0, local copies, waits for them, and re-layouts: 14 us -> none  [the longest x4 11.1 us: shards(): hidden = jax.nn.silu(spatial + spatial_bias).astype(jnp.bfloat16)]
    reshape x3 -> x1, local copies, waits for them, and re-layouts: 9.91 us -> 0.08 us  [shards(): bias = spatial_bias.reshape(16, 2, 32)[:, where[3], :].reshape(1, 512)]
    convert_element_type x2 -> x0, other arithmetic: 8.76 us -> none  [the longest x1 5.21 us: shards(): active = jax.nn.silu(scaled).astype(jnp.bfloat16)]
  transfers between devices with their start and end apart: 4 -> 19, of which waited for: 3 -> 7; matrix products, arithmetic and copies ran while one was open for 34% -> 2% of each run, Pallas kernels for 0% -> 38%
where the time goes in v2:
time: 124 us; the launch traced here: 123 us
  Pallas kernels  53.1 us (43%)
  waiting for transfers between devices  35.4 us (29%)
  starting transfers between devices  29.8 us (24%)
  local copies, waits for them, and re-layouts  4.68 us (4%)
    ppermute x8, waiting for transfers between devices, step_to(): lax.ppermute(value, axis, [(i, (i + distance) % count) for i in range(cou...  27.8 us
    pallas_call x5, Pallas kernels, conv(): pl.pallas_call(functools.partial(conv_kernel, step, colours), out_shape=o...  25.2 us
    ppermute x8, starting transfers between devices, step_to(): lax.ppermute(value, axis, [(i, (i + distance) % count) for i in range(cou...  11.6 us
    pallas_call x1, Pallas kernels, centre(): pl.pallas_call(centre_kernel, out_shape=(narrow, wide, wide, wide, jax.Sh...  9.03 us
    ppermute x6, starting transfers between devices, ring(): return lax.ppermute(value, (axis, 'core'), pairs)  7.94 us
    ppermute x6, waiting for transfers between devices, ring(): return lax.ppermute(value, (axis, 'core'), pairs)  6.63 us
    pallas_call x1, Pallas kernels, spread(): pl.pallas_call(spread_kernel, out_shape=(wide, wide), in_specs=specs('s',...  4.83 us
    pallas_call x1, Pallas kernels, finish(): pl.pallas_call(finish_kernel, grid=(2,), out_shape=jax.ShapeDtypeStruct((...  4.02 us
  transfers between devices with their start and end apart: 19, of which 7 were waited for; matrix products, arithmetic and copies ran while one was open for 2% of the time, Pallas kernels for 38%

profile of v2, /device:TPU:1, one launch (start us, length us, event | category | flops | bytes accessed | tf_op | source)
XLA Modules:
  0.0 123.3 jit_solution(17032672204123314407)
XLA Ops:
  0.0 0.0 copy-start.3
  0.0 0.1 pad_add_fusion.where.refs_0_
  0.1 1.3 %copy-done = bf16[9,64,1024]{2,1,0:T(8,128)(2,1)S(1)} copy-done((bf16[9,64,1024]{2,1,0:T(8,128)(2,1)S(1)}, bf16[9,64,1024]{2,1,0:T(8,128)(2,1)}, u32[]{:S(2)}) %copy-start) | copy-done | bytes 1179672
  1.4 1.0 copy-done.1
  2.3 1.0 shard_map.55
  3.4 3.6 %collective-permute-start.1 = (bf16[768,256]{1,0:T(8,128)(2,1)S(1)}, bf16[768,256]{1,0:T(8,128)(2,1)S(1)}, u32[]{:S(2)}, u32[]{:S(2)}) collective-permute-start(bf16[768,256]{1,0:T(8,128)(2,1)S(1)} %get-tuple-element.49.refs_0_), channel_id=1, source_target_pairs={{0,96},{32,0},{64,32},{96,64},{1,97},{33,1},{65,33},{97,65},{2,98}... | collective-permute-start | bytes 1179656 | tf_op jit(solution)/shard_map/ppermute | solution.py:483
  7.0 0.0 collective-permute-start
  7.0 3.8 %collective-permute-start.3 = (bf16[768,256]{1,0:T(8,128)(2,1)S(1)}, bf16[768,256]{1,0:T(8,128)(2,1)S(1)}, u32[]{:S(2)}, u32[]{:S(2)}) collective-permute-start(bf16[768,256]{1,0:T(8,128)(2,1)S(1)} %get-tuple-element.50.refs_4_), channel_id=1, source_target_pairs={{0,24},{8,0},{16,8},{24,16},{1,25},{9,1},{17,9},{25,17},{2,26},{10... | collective-permute-start | bytes 1179656 | tf_op jit(solution)/shard_map/ppermute | solution.py:483
  10.8 0.0 collective-permute-start.2
  10.8 0.0 copy-done.3
  10.8 0.1 reshape.6
  10.9 0.1 reshape_squeeze.3.refs_4_
  11.0 2.2 %copy.11.video = bf16[2,2,12,20,1024]{4,3,2,1,0:T(8,128)(2,1)S(1)} copy(bf16[2,2,12,20,1024]{4,1,3,2,0:T(2,128)(2,1)} %param.5) | data formatting | bytes 3932160 | tf_op jit(solution)/shard_map/optimization_barrier | solution.py:478
  13.2 0.0 copy-done.2
  13.2 2.6 %shard_map.56 = (bf16[4,240,1024]{2,1,0:T(8,128)(2,1)S(1)}, bf16[4,240,1024]{2,1,0:T(8,128)(2,1)S(1)}) custom-call(bf16[2,2,12,20,1024]{4,3,2,1,0:T(8,128)(2,1)S(1)} %copy.11.video, f32[1,1024]{1,0:T(1,128)S(1)} %bitcast.6), custom_call_target="tpu_custom_call" | custom-call | flops 2000000000 | bytes 20000000 | tf_op jit(solution)/shard_map/pallas_call | solution.py:80
  15.8 0.0 collective-permute-done.1.refs_1_.refs_3_
  15.8 2.1 %collective-permute-done.refs_0_.refs_1_ = bf16[768,256]{1,0:T(8,128)(2,1)S(1)} collective-permute-done((bf16[768,256]{1,0:T(8,128)(2,1)S(1)}, bf16[768,256]{1,0:T(8,128)(2,1)S(1)}, u32[]{:S(2)}, u32[]{:S(2)}) %collective-permute-start) | collective-permute-done | bytes 393248 | tf_op jit(solution)/shard_map/ppermute | solution.py:483
  17.9 0.3 collective-permute-done.3.refs_3_.refs_7_
  18.2 3.1 %collective-permute-done.2.refs_2_.refs_5_ = bf16[768,256]{1,0:T(8,128)(2,1)S(1)} collective-permute-done((bf16[768,256]{1,0:T(8,128)(2,1)S(1)}, bf16[768,256]{1,0:T(8,128)(2,1)S(1)}, u32[]{:S(2)}, u32[]{:S(2)}) %collective-permute-start.2) | collective-permute-done | bytes 393248 | tf_op jit(solution)/shard_map/ppermute | solution.py:483
  21.4 2.2 %collective-permute-start.6 = (bf16[4,240,1024]{2,1,0:T(8,128)(2,1)S(1)}, bf16[4,240,1024]{2,1,0:T(8,128)(2,1)S(1)}, u32[]{:S(2)}, u32[]{:S(2)}) collective-permute-start(bf16[4,240,1024]{2,1,0:T(8,128)(2,1)S(1)} %get-tuple-element.59.own), channel_id=1, source_target_pairs={{0,1},{1,0},{2,3},{3,2},{4,5},{5,4},{6,7},{7,6},{8,9},{9,8},{10,11... | collective-permute-start | bytes 5898248 | tf_op jit(solution)/shard_map/ppermute | solution.py:495
  23.5 0.6 shard_map.57
  24.1 2.7 %collective-permute-start.4 = (bf16[768,256]{1,0:T(8,128)(2,1)S(1)}, bf16[768,256]{1,0:T(8,128)(2,1)S(1)}, u32[]{:S(2)}, u32[]{:S(2)}) collective-permute-start(bf16[768,256]{1,0:T(8,128)(2,1)S(1)} %get-tuple-element.55), channel_id=1, source_target_pairs={{0,32},{32,64},{64,96},{96,0},{1,97},{33,1},{65,33},{97,65},{2,34}... | collective-permute-start | bytes 1179656 | tf_op jit(solution)/shard_map/ppermute | solution.py:474
  26.9 0.0 collective-permute-start.5
  26.9 4.7 %collective-permute-done.4.refs_2_ = bf16[768,256]{1,0:T(8,128)(2,1)S(1)} collective-permute-done((bf16[768,256]{1,0:T(8,128)(2,1)S(1)}, bf16[768,256]{1,0:T(8,128)(2,1)S(1)}, u32[]{:S(2)}, u32[]{:S(2)}) %collective-permute-start.4) | collective-permute-done | bytes 393248 | tf_op jit(solution)/shard_map/ppermute | solution.py:474
  31.6 1.9 %collective-permute-done.5.refs_6_ = bf16[768,256]{1,0:T(8,128)(2,1)S(1)} collective-permute-done((bf16[768,256]{1,0:T(8,128)(2,1)S(1)}, bf16[768,256]{1,0:T(8,128)(2,1)S(1)}, u32[]{:S(2)}, u32[]{:S(2)}) %collective-permute-start.5) | collective-permute-done | bytes 393248 | tf_op jit(solution)/shard_map/ppermute | solution.py:474
  33.5 0.2 shard_map.58
  33.7 0.1 collective-permute-start.7
  33.8 1.6 %collective-permute-start.10 = (bf16[4,768,256]{2,1,0:T(8,128)(2,1)S(1)}, bf16[4,768,256]{2,1,0:T(8,128)(2,1)S(1)}, u32[]{:S(2)}, u32[]{:S(2)}) collective-permute-start(bf16[4,768,256]{2,1,0:T(8,128)(2,1)S(1)} %get-tuple-element.62.refs_4_.refs_1_), channel_id=1, source_target_pairs={{0,96},{32,0},{64,32},{96,64},{1,97},{33,1},{65,33},{97,65},{2,98}... | collective-permute-start | bytes 4718600 | tf_op jit(solution)/shard_map/ppermute | solution.py:483
  35.4 0.0 collective-permute-start.9
  35.4 2.6 %collective-permute-start.8 = (bf16[4,768,256]{2,1,0:T(8,128)(2,1)S(1)}, bf16[4,768,256]{2,1,0:T(8,128)(2,1)S(1)}, u32[]{:S(2)}, u32[]{:S(2)}) collective-permute-start(bf16[4,768,256]{2,1,0:T(8,128)(2,1)S(1)} %get-tuple-element.57.refs_3_.refs_0_), channel_id=1, source_target_pairs={{0,24},{8,0},{16,8},{24,16},{1,25},{9,1},{17,9},{25,17},{2,26},{10... | collective-permute-start | bytes 4718600 | tf_op jit(solution)/shard_map/ppermute | solution.py:483
  38.0 0.0 collective-permute-done.6.other
  38.0 4.8 %shard_map.59 = (bf16[4,14,176,256]{3,2,1,0:T(8,128)(2,1)S(1)}, bf16[4,14,176,256]{3,2,1,0:T(8,128)(2,1)S(1)}) custom-call(s32[4]{0:T(128)S(1)} %pad_add_fusion.where.refs_0_, bf16[4,240,1024]{2,1,0:T(8,128)(2,1)S(1)} %get-tuple-element.59.own, bf16[4,240,1024]{2,1,0:T(8,128)(2,1)S(1)} %collective-permute-done.6.other), custom_call_target="tpu_custom_call" | custom-call | flops 2000000000 | bytes 25000000 | tf_op jit(solution)/shard_map/pallas_call | solution.py:137
  42.8 5.9 %shard_map.60 = (f32[1920,256]{1,0:T(8,128)S(1)}, f32[1920,256]{1,0:T(8,128)S(1)}) custom-call(s32[4]{0:T(128)S(1)} %pad_add_fusion.where.refs_0_, bf16[4,14,176,256]{3,2,1,0:T(8,128)(2,1)S(1)} %get-tuple-element.60.refs_1_, bf16[4,14,176,256]{3,2,1,0:T(8,128)(2,1)S(1)} %get-tuple-element.61.refs_2_.refs_1_, ...), custom_call_target="tpu_custom_call" | custom-call | flops 8000000000 | bytes 24000000 | tf_op jit(solution)/shard_map/pallas_call | solution.py:301
  48.8 22.3 %collective-permute-done.7.refs_0_.refs_3_.refs_2_ = bf16[4,768,256]{2,1,0:T(8,128)(2,1)S(1)} collective-permute-done((bf16[4,768,256]{2,1,0:T(8,128)(2,1)S(1)}, bf16[4,768,256]{2,1,0:T(8,128)(2,1)S(1)}, u32[]{:S(2)}, u32[]{:S(2)}) %collective-permute-start.7) | collective-permute-done | bytes 1572896 | tf_op jit(solution)/shard_map/ppermute | solution.py:483
  71.0 0.0 collective-permute-done.10.refs_3_.refs_4_.refs_5_
  71.0 0.0 collective-permute-done.9.refs_2_.refs_4_.refs_3_
  71.0 0.0 collective-permute-done.8.refs_1_.refs_3_.refs_4_
  71.0 0.8 shard_map.61
  71.8 2.4 %collective-permute-start.11 = (bf16[4,576,256]{2,1,0:T(8,128)(2,1)S(1)}, bf16[4,576,256]{2,1,0:T(8,128)(2,1)S(1)}, u32[]{:S(2)}, u32[]{:S(2)}) collective-permute-start(bf16[4,576,256]{2,1,0:T(8,128)(2,1)S(1)} %get-tuple-element.65), channel_id=1, source_target_pairs={{0,8},{8,16},{16,24},{24,0},{1,25},{9,1},{17,9},{25,17},{2,10},{10... | collective-permute-start | bytes 3538952 | tf_op jit(solution)/shard_map/ppermute | solution.py:474
  74.2 2.4 %collective-permute-start.12 = (bf16[4,576,256]{2,1,0:T(8,128)(2,1)S(1)}, bf16[4,576,256]{2,1,0:T(8,128)(2,1)S(1)}, u32[]{:S(2)}, u32[]{:S(2)}) collective-permute-start(bf16[4,576,256]{2,1,0:T(8,128)(2,1)S(1)} %get-tuple-element.72), channel_id=1, source_target_pairs={{0,32},{32,64},{64,96},{96,0},{1,97},{33,1},{65,33},{97,65},{2,34}... | collective-permute-start | bytes 3538952 | tf_op jit(solution)/shard_map/ppermute | solution.py:474
  76.6 6.0 %shard_map.62 = (f32[1920,256]{1,0:T(8,128)S(1)}, f32[1920,256]{1,0:T(8,128)S(1)}) custom-call(s32[4]{0:T(128)S(1)} %pad_add_fusion.where.refs_0_, bf16[4,14,176,256]{3,2,1,0:T(8,128)(2,1)S(1)} %get-tuple-element.60.refs_1_, bf16[4,14,176,256]{3,2,1,0:T(8,128)(2,1)S(1)} %get-tuple-element.61.refs_2_.refs_1_, ...), custom_call_target="tpu_custom_call", output_to_operand_aliasing={{0}: (5, {}), {1}: (6, {})} | custom-call | flops 8000000000 | bytes 24000000 | tf_op jit(solution)/shard_map/pallas_call | solution.py:301
  82.6 6.0 %shard_map.63 = (f32[1920,256]{1,0:T(8,128)S(1)}, f32[1920,256]{1,0:T(8,128)S(1)}) custom-call(s32[4]{0:T(128)S(1)} %pad_add_fusion.where.refs_0_, bf16[4,14,176,256]{3,2,1,0:T(8,128)(2,1)S(1)} %get-tuple-element.60.refs_1_, bf16[4,14,176,256]{3,2,1,0:T(8,128)(2,1)S(1)} %get-tuple-element.61.refs_2_.refs_1_, ...), custom_call_target="tpu_custom_call", output_to_operand_aliasing={{0}: (5, {}), {1}: (6, {})} | custom-call | flops 8000000000 | bytes 24000000 | tf_op jit(solution)/shard_map/pallas_call | solution.py:301
  88.6 0.1 collective-permute-start.14
  88.7 0.3 collective-permute-start.13
  89.0 0.8 shard_map.64.weights
  89.8 0.0 collective-permute-done.11.refs_2_
  89.8 3.6 %shard_map.65 = (bf16[1920,256]{1,0:T(8,128)(2,1)S(1)}, bf16[2,2,240,256]{3,2,1,0:T(8,128)(2,1)S(1)}, bf16[2,2,240,256]{3,2,1,0:T(8,128)(2,1)S(1)}) custom-call(s32[4]{0:T(128)S(1)} %pad_add_fusion.where.refs_0_, bf16[4,14,176,256]{3,2,1,0:T(8,128)(2,1)S(1)} %get-tuple-element.60.refs_1_, bf16[4,576,256]{2,1,0:T(8,128)(2,1)S(1)} %collective-permute-done.11.refs_2_, ...), custom_call_target="tpu_custom_call" | custom-call | flops 4000000000 | bytes 12000000 | tf_op jit(solution)/shard_map/pallas_call | solution.py:301
  93.4 0.0 collective-permute-done.12.refs_2_
  93.5 3.7 %shard_map.66 = (bf16[1920,256]{1,0:T(8,128)(2,1)S(1)}, bf16[2,2,240,256]{3,2,1,0:T(8,128)(2,1)S(1)}, bf16[2,2,240,256]{3,2,1,0:T(8,128)(2,1)S(1)}) custom-call(s32[4]{0:T(128)S(1)} %pad_add_fusion.where.refs_0_, bf16[4,14,176,256]{3,2,1,0:T(8,128)(2,1)S(1)} %get-tuple-element.61.refs_2_.refs_1_, bf16[4,576,256]{2,1,0:T(8,128)(2,1)S(1)} %collective-permute-done.12.refs_2_, ...), custom_call_target="tpu_custom_call" | custom-call | flops 4000000000 | bytes 12000000 | tf_op jit(solution)/shard_map/pallas_call | solution.py:301
  97.1 3.1 %collective-permute-start.16 = (bf16[2,2,240,256]{3,2,1,0:T(8,128)(2,1)S(1)}, bf16[2,2,240,256]{3,2,1,0:T(8,128)(2,1)S(1)}, u32[]{:S(2)}, u32[]{:S(2)}) collective-permute-start(bf16[2,2,240,256]{3,2,1,0:T(8,128)(2,1)S(1)} %get-tuple-element.86), channel_id=1, source_target_pairs={{0,2},{2,4},{4,6},{1,3},{3,5},{5,7},{8,10},{10,12},{12,14},{9,11},... | collective-permute-start | bytes 1474568 | tf_op jit(solution)/shard_map/ppermute | solution.py:515
  100.3 1.5 %collective-permute-start.17 = (bf16[2,2,240,256]{3,2,1,0:T(8,128)(2,1)S(1)}, bf16[2,2,240,256]{3,2,1,0:T(8,128)(2,1)S(1)}, u32[]{:S(2)}, u32[]{:S(2)}) collective-permute-start(bf16[2,2,240,256]{3,2,1,0:T(8,128)(2,1)S(1)} %get-tuple-element.89), channel_id=1, source_target_pairs={{2,0},{4,2},{6,4},{3,1},{5,3},{7,5},{10,8},{12,10},{14,12},{11,9},... | collective-permute-start | bytes 1474568 | tf_op jit(solution)/shard_map/ppermute | solution.py:516
  101.8 1.6 %shard_map.67 = (bf16[1920,512]{1,0:T(8,128)(2,1)S(1)}, bf16[1920,512]{1,0:T(8,128)(2,1)S(1)}) custom-call(bf16[1920,256]{1,0:T(8,128)(2,1)S(1)} %get-tuple-element.71.hidden_a, bf16[1920,256]{1,0:T(8,128)(2,1)S(1)} %get-tuple-element.77.hidden_b), custom_call_target="tpu_custom_call" | custom-call | flops 1000000000 | bytes 6000000 | tf_op jit(solution)/shard_map/pallas_call | solution.py:331
  103.4 0.0 collective-permute-done.14.block_b
  103.4 0.0 collective-permute-done.13.block_a
  103.4 9.0 %shard_map.68 = (bf16[2,240,1024]{2,1,0:T(8,128)(2,1)S(1)}, f32[2,240,1024]{2,1,0:T(8,128)S(1)}, f32[2,240,1024]{2,1,0:T(8,128)S(1)}, f32[2,240,1024]{2,1,0:T(8,128)S(1)}, bf16[2,512,1024]{2,1,0:T(8,128)(2,1)S(1)}) custom-call(s32[4]{0:T(128)S(1)} %pad_add_fusion.where.refs_0_, bf16[1920,256]{1,0:T(8,128)(2,1)S(1)} %get-tuple-element.71.hidden_a, ...), custom_call_target="tpu_custom_call" | custom-call | flops 10000000000 | bytes 12000000 | tf_op jit(solution)/shard_map/pallas_call | solution.py:405
  112.5 2.2 %collective-permute-start.15 = (bf16[2,240,1024]{2,1,0:T(8,128)(2,1)S(1)}, bf16[2,240,1024]{2,1,0:T(8,128)(2,1)S(1)}, u32[]{:S(2)}, u32[]{:S(2)}) collective-permute-start(bf16[2,240,1024]{2,1,0:T(8,128)(2,1)S(1)} %get-tuple-element.85), channel_id=1, source_target_pairs={{0,1},{1,0},{2,3},{3,2},{4,5},{5,4},{6,7},{7,6},{8,9},{9,8},{10,11... | collective-permute-start | bytes 2949128 | tf_op jit(solution)/shard_map/ppermute | solution.py:520
  114.6 0.0 collective-permute-done.16.before
  114.6 0.0 collective-permute-done.17.behind
  114.6 1.2 shard_map.69
  115.9 1.3 %collective-permute-start.18 = (bf16[2,240,1024]{2,1,0:T(8,128)(2,1)S(1)}, bf16[2,240,1024]{2,1,0:T(8,128)(2,1)S(1)}, u32[]{:S(2)}, u32[]{:S(2)}) collective-permute-start(bf16[2,240,1024]{2,1,0:T(8,128)(2,1)S(1)} %shard_map.69), channel_id=1, source_target_pairs={{0,1},{1,0},{2,3},{3,2},{4,5},{5,4},{6,7},{7,6},{8,9},{9,8},{10,11... | collective-permute-start | bytes 2949128 | tf_op jit(solution)/shard_map/ppermute | solution.py:523
  117.1 1.2 %shard_map.70.rough_mine = f32[2,240,1024]{2,1,0:T(8,128)S(1)} custom-call(s32[4]{0:T(128)S(1)} %pad_add_fusion.where.refs_0_, bf16[2,2,240,256]{3,2,1,0:T(8,128)(2,1)S(1)} %collective-permute-done.16.before, bf16[2,2,240,256]{3,2,1,0:T(8,128)(2,1)S(1)} %collective-permute-done.17.behind, bf16[2,512,1024]{2,1,0:T(8,128)(2,1)S(1)} %get-tuple-element.87.weights, ...), custom_call_target="tpu_custom_call" | custom-call | flops 3000000000 | bytes 6000000 | tf_op jit(solution)/shard_map/pallas_call | solution.py:429
  118.4 0.0 collective-permute-done.15.calm_received
  118.4 0.9 collective-permute-done.18.rough_received
  119.3 4.0 %shard_map.71 = bf16[2,12,20,2,1024]{4,3,2,1,0:T(2,128)(2,1)} custom-call(s32[4]{0:T(128)S(1)} %pad_add_fusion.where.refs_0_, bf16[4,240,1024]{2,1,0:T(8,128)(2,1)S(1)} %get-tuple-element.52.video, f32[2,240,1024]{2,1,0:T(8,128)S(1)} %get-tuple-element.84.calm_mine, bf16[2,240,1024]{2,1,0:T(8,128)(2,1)S(1)} %collective-permute-done.15.calm_received, ...), custom_call_target="tpu_custom_call" | custom-call | flops 3000000 | bytes 10000000 | tf_op jit(solution)/shard_map/pallas_call | solution.py:457
  (4 shorter events, 0.0 us)
Async XLA Ops:
  0.0 10.8 %copy-start.3 = (f32[1024]{0:T(1024)S(1)}, f32[1024]{0:T(1024)}, u32[]{:S(2)}) copy-start(f32[1024]{0:T(1024)} %param.8) | copy-start | bytes 12292
  0.1 1.3 %copy-start = (bf16[9,64,1024]{2,1,0:T(8,128)(2,1)S(1)}, bf16[9,64,1024]{2,1,0:T(8,128)(2,1)}, u32[]{:S(2)}) copy-start(bf16[9,64,1024]{2,1,0:T(8,128)(2,1)} %spatial.1) | copy-start | bytes 3538948
  1.4 1.0 copy-start.1
  3.4 12.4 %collective-permute-start.1 = (bf16[768,256]{1,0:T(8,128)(2,1)S(1)}, bf16[768,256]{1,0:T(8,128)(2,1)S(1)}, u32[]{:S(2)}, u32[]{:S(2)}) collective-permute-start(bf16[768,256]{1,0:T(8,128)(2,1)S(1)} %get-tuple-element.49.refs_0_), channel_id=1, source_target_pairs={{0,96},{32,0},{64,32},{96,64},{1,97},{33,1},{65,33},{97,65},{2,98}... | collective-permute-start | bytes 1179656 | tf_op jit(solution)/shard_map/ppermute | solution.py:483
  7.0 10.9 %collective-permute-start = (bf16[768,256]{1,0:T(8,128)(2,1)S(1)}, bf16[768,256]{1,0:T(8,128)(2,1)S(1)}, u32[]{:S(2)}, u32[]{:S(2)}) collective-permute-start(bf16[768,256]{1,0:T(8,128)(2,1)S(1)} %get-tuple-element.49.refs_0_), channel_id=1, source_target_pairs={{0,32},{32,64},{64,96},{96,0},{1,33},{33,65},{65,97},{97,1},{2,34}... | collective-permute-start | bytes 1179656 | tf_op jit(solution)/shard_map/ppermute | solution.py:483
  7.0 11.2 %collective-permute-start.3 = (bf16[768,256]{1,0:T(8,128)(2,1)S(1)}, bf16[768,256]{1,0:T(8,128)(2,1)S(1)}, u32[]{:S(2)}, u32[]{:S(2)}) collective-permute-start(bf16[768,256]{1,0:T(8,128)(2,1)S(1)} %get-tuple-element.50.refs_4_), channel_id=1, source_target_pairs={{0,24},{8,0},{16,8},{24,16},{1,25},{9,1},{17,9},{25,17},{2,26},{10... | collective-permute-start | bytes 1179656 | tf_op jit(solution)/shard_map/ppermute | solution.py:483
  10.8 10.6 %collective-permute-start.2 = (bf16[768,256]{1,0:T(8,128)(2,1)S(1)}, bf16[768,256]{1,0:T(8,128)(2,1)S(1)}, u32[]{:S(2)}, u32[]{:S(2)}) collective-permute-start(bf16[768,256]{1,0:T(8,128)(2,1)S(1)} %get-tuple-element.50.refs_4_), channel_id=1, source_target_pairs={{0,8},{8,16},{16,24},{24,0},{1,9},{9,17},{17,25},{25,1},{2,10},{10... | collective-permute-start | bytes 1179656 | tf_op jit(solution)/shard_map/ppermute | solution.py:483
  11.0 2.2 %copy-start.2 = (f32[1024]{0:T(1024)S(1)}, f32[1024]{0:T(1024)}, u32[]{:S(2)}) copy-start(f32[1024]{0:T(1024)} %param.6) | copy-start | bytes 12292
  21.4 16.6 %collective-permute-start.6 = (bf16[4,240,1024]{2,1,0:T(8,128)(2,1)S(1)}, bf16[4,240,1024]{2,1,0:T(8,128)(2,1)S(1)}, u32[]{:S(2)}, u32[]{:S(2)}) collective-permute-start(bf16[4,240,1024]{2,1,0:T(8,128)(2,1)S(1)} %get-tuple-element.59.own), channel_id=1, source_target_pairs={{0,1},{1,0},{2,3},{3,2},{4,5},{5,4},{6,7},{7,6},{8,9},{9,8},{10,11... | collective-permute-start | bytes 5898248 | tf_op jit(solution)/shard_map/ppermute | solution.py:495
  24.1 7.5 %collective-permute-start.4 = (bf16[768,256]{1,0:T(8,128)(2,1)S(1)}, bf16[768,256]{1,0:T(8,128)(2,1)S(1)}, u32[]{:S(2)}, u32[]{:S(2)}) collective-permute-start(bf16[768,256]{1,0:T(8,128)(2,1)S(1)} %get-tuple-element.55), channel_id=1, source_target_pairs={{0,32},{32,64},{64,96},{96,0},{1,97},{33,1},{65,33},{97,65},{2,34}... | collective-permute-start | bytes 1179656 | tf_op jit(solution)/shard_map/ppermute | solution.py:474
  26.9 6.6 %collective-permute-start.5 = (bf16[768,256]{1,0:T(8,128)(2,1)S(1)}, bf16[768,256]{1,0:T(8,128)(2,1)S(1)}, u32[]{:S(2)}, u32[]{:S(2)}) collective-permute-start(bf16[768,256]{1,0:T(8,128)(2,1)S(1)} %get-tuple-element.56), channel_id=1, source_target_pairs={{0,8},{8,16},{16,24},{24,0},{1,25},{9,1},{17,9},{25,17},{2,10},{10... | collective-permute-start | bytes 1179656 | tf_op jit(solution)/shard_map/ppermute | solution.py:474
  33.7 37.3 %collective-permute-start.7 = (bf16[4,768,256]{2,1,0:T(8,128)(2,1)S(1)}, bf16[4,768,256]{2,1,0:T(8,128)(2,1)S(1)}, u32[]{:S(2)}, u32[]{:S(2)}) collective-permute-start(bf16[4,768,256]{2,1,0:T(8,128)(2,1)S(1)} %get-tuple-element.57.refs_3_.refs_0_), channel_id=1, source_target_pairs={{0,8},{8,16},{16,24},{24,0},{1,9},{9,17},{17,25},{25,1},{2,10},{10... | collective-permute-start | bytes 4718600 | tf_op jit(solution)/shard_map/ppermute | solution.py:483
  33.8 37.2 %collective-permute-start.10 = (bf16[4,768,256]{2,1,0:T(8,128)(2,1)S(1)}, bf16[4,768,256]{2,1,0:T(8,128)(2,1)S(1)}, u32[]{:S(2)}, u32[]{:S(2)}) collective-permute-start(bf16[4,768,256]{2,1,0:T(8,128)(2,1)S(1)} %get-tuple-element.62.refs_4_.refs_1_), channel_id=1, source_target_pairs={{0,96},{32,0},{64,32},{96,64},{1,97},{33,1},{65,33},{97,65},{2,98}... | collective-permute-start | bytes 4718600 | tf_op jit(solution)/shard_map/ppermute | solution.py:483
  35.4 35.7 %collective-permute-start.9 = (bf16[4,768,256]{2,1,0:T(8,128)(2,1)S(1)}, bf16[4,768,256]{2,1,0:T(8,128)(2,1)S(1)}, u32[]{:S(2)}, u32[]{:S(2)}) collective-permute-start(bf16[4,768,256]{2,1,0:T(8,128)(2,1)S(1)} %get-tuple-element.62.refs_4_.refs_1_), channel_id=1, source_target_pairs={{0,32},{32,64},{64,96},{96,0},{1,33},{33,65},{65,97},{97,1},{2,34}... | collective-permute-start | bytes 4718600 | tf_op jit(solution)/shard_map/ppermute | solution.py:483
  35.4 35.7 %collective-permute-start.8 = (bf16[4,768,256]{2,1,0:T(8,128)(2,1)S(1)}, bf16[4,768,256]{2,1,0:T(8,128)(2,1)S(1)}, u32[]{:S(2)}, u32[]{:S(2)}) collective-permute-start(bf16[4,768,256]{2,1,0:T(8,128)(2,1)S(1)} %get-tuple-element.57.refs_3_.refs_0_), channel_id=1, source_target_pairs={{0,24},{8,0},{16,8},{24,16},{1,25},{9,1},{17,9},{25,17},{2,26},{10... | collective-permute-start | bytes 4718600 | tf_op jit(solution)/shard_map/ppermute | solution.py:483
  71.8 18.0 %collective-permute-start.11 = (bf16[4,576,256]{2,1,0:T(8,128)(2,1)S(1)}, bf16[4,576,256]{2,1,0:T(8,128)(2,1)S(1)}, u32[]{:S(2)}, u32[]{:S(2)}) collective-permute-start(bf16[4,576,256]{2,1,0:T(8,128)(2,1)S(1)} %get-tuple-element.65), channel_id=1, source_target_pairs={{0,8},{8,16},{16,24},{24,0},{1,25},{9,1},{17,9},{25,17},{2,10},{10... | collective-permute-start | bytes 3538952 | tf_op jit(solution)/shard_map/ppermute | solution.py:474
  74.2 19.3 %collective-permute-start.12 = (bf16[4,576,256]{2,1,0:T(8,128)(2,1)S(1)}, bf16[4,576,256]{2,1,0:T(8,128)(2,1)S(1)}, u32[]{:S(2)}, u32[]{:S(2)}) collective-permute-start(bf16[4,576,256]{2,1,0:T(8,128)(2,1)S(1)} %get-tuple-element.72), channel_id=1, source_target_pairs={{0,32},{32,64},{64,96},{96,0},{1,97},{33,1},{65,33},{97,65},{2,34}... | collective-permute-start | bytes 3538952 | tf_op jit(solution)/shard_map/ppermute | solution.py:474
  88.6 14.8 %collective-permute-start.14 = (bf16[4,192,256]{2,1,0:T(8,128)(2,1)S(1)}, bf16[4,192,256]{2,1,0:T(8,128)(2,1)S(1)}, u32[]{:S(2)}, u32[]{:S(2)}) collective-permute-start(bf16[4,192,256]{2,1,0:T(8,128)(2,1)S(1)} %get-tuple-element.83), channel_id=1, source_target_pairs={{0,32},{32,64},{64,96},{96,0},{1,97},{33,1},{65,33},{97,65},{2,34}... | collective-permute-start | bytes 1179656 | tf_op jit(solution)/shard_map/ppermute | solution.py:474
  88.7 14.7 %collective-permute-start.13 = (bf16[4,192,256]{2,1,0:T(8,128)(2,1)S(1)}, bf16[4,192,256]{2,1,0:T(8,128)(2,1)S(1)}, u32[]{:S(2)}, u32[]{:S(2)}) collective-permute-start(bf16[4,192,256]{2,1,0:T(8,128)(2,1)S(1)} %get-tuple-element.81), channel_id=1, source_target_pairs={{0,8},{8,16},{16,24},{24,0},{1,25},{9,1},{17,9},{25,17},{2,10},{10... | collective-permute-start | bytes 1179656 | tf_op jit(solution)/shard_map/ppermute | solution.py:474
  97.1 17.5 %collective-permute-start.16 = (bf16[2,2,240,256]{3,2,1,0:T(8,128)(2,1)S(1)}, bf16[2,2,240,256]{3,2,1,0:T(8,128)(2,1)S(1)}, u32[]{:S(2)}, u32[]{:S(2)}) collective-permute-start(bf16[2,2,240,256]{3,2,1,0:T(8,128)(2,1)S(1)} %get-tuple-element.86), channel_id=1, source_target_pairs={{0,2},{2,4},{4,6},{1,3},{3,5},{5,7},{8,10},{10,12},{12,14},{9,11},... | collective-permute-start | bytes 1474568 | tf_op jit(solution)/shard_map/ppermute | solution.py:515
  100.3 14.4 %collective-permute-start.17 = (bf16[2,2,240,256]{3,2,1,0:T(8,128)(2,1)S(1)}, bf16[2,2,240,256]{3,2,1,0:T(8,128)(2,1)S(1)}, u32[]{:S(2)}, u32[]{:S(2)}) collective-permute-start(bf16[2,2,240,256]{3,2,1,0:T(8,128)(2,1)S(1)} %get-tuple-element.89), channel_id=1, source_target_pairs={{2,0},{4,2},{6,4},{3,1},{5,3},{7,5},{10,8},{12,10},{14,12},{11,9},... | collective-permute-start | bytes 1474568 | tf_op jit(solution)/shard_map/ppermute | solution.py:516
  112.5 5.9 %collective-permute-start.15 = (bf16[2,240,1024]{2,1,0:T(8,128)(2,1)S(1)}, bf16[2,240,1024]{2,1,0:T(8,128)(2,1)S(1)}, u32[]{:S(2)}, u32[]{:S(2)}) collective-permute-start(bf16[2,240,1024]{2,1,0:T(8,128)(2,1)S(1)} %get-tuple-element.85), channel_id=1, source_target_pairs={{0,1},{1,0},{2,3},{3,2},{4,5},{5,4},{6,7},{7,6},{8,9},{9,8},{10,11... | collective-permute-start | bytes 2949128 | tf_op jit(solution)/shard_map/ppermute | solution.py:520
  115.9 3.4 %collective-permute-start.18 = (bf16[2,240,1024]{2,1,0:T(8,128)(2,1)S(1)}, bf16[2,240,1024]{2,1,0:T(8,128)(2,1)S(1)}, u32[]{:S(2)}, u32[]{:S(2)}) collective-permute-start(bf16[2,240,1024]{2,1,0:T(8,128)(2,1)S(1)} %shard_map.69), channel_id=1, source_target_pairs={{0,1},{1,0},{2,3},{3,2},{4,5},{5,4},{6,7},{7,6},{8,9},{9,8},{10,11... | collective-permute-start | bytes 2949128 | tf_op jit(solution)/shard_map/ppermute | solution.py:523

commit v3 on v2

--- a/solution.py
+++ b/solution.py
@@ -34,19 +34,28 @@
     return pl.CostEstimate(flops=flops, bytes_accessed=bytes_accessed, transcendentals=0)
 
 
-def pack_kernel(where, spatial, temporal, unit_a, unit_b):
+def pack_kernel(where, spatial_hbm, temporal_hbm, unit_a, unit_b, spatial, temporal, sem):
     core = where[3]
+    half = pl.ds(pl.multiple_of(core * 32, 32), 32)
+    copies = [
+        pltpu.make_async_copy(spatial_hbm, spatial, sem.at[0]),
+        pltpu.make_async_copy(temporal_hbm.at[:, half, :], temporal, sem.at[1]),
+    ]
+    for copy in copies:
+        copy.start()
     source = lax.broadcasted_iota(jnp.int32, (256, 128), 0)
     target = lax.broadcasted_iota(jnp.int32, (256, 128), 1)
     wanted = (target >> 5) * 64 + (target & 31) + core * 32
     pick = jnp.where(source == wanted, 1.0, 0.0).astype(BF16)
+    for copy in copies:
+        copy.wait()
     for part in range(4):
         unit = (unit_a, unit_b)[part // 2]
         columns = spatial[:, :, part * 256 : (part + 1) * 256].reshape(576, 256)
         kept = jnp.dot(columns, pick, preferred_element_type=F32).astype(BF16)
         unit[0:576, (part % 2) * 128 : (part % 2 + 1) * 128] = kept
     for tap in range(3):
-        rows = temporal[tap, pl.ds(pl.multiple_of(core * 32, 32), 32), :]
+        rows = temporal[tap]
         for part in range(4):
             unit = (unit_a, unit_b)[part // 2]
             start = 576 + (part % 2) * 96 + tap * 32
@@ -58,8 +67,13 @@
     return pl.pallas_call(
         pack_kernel,
         out_shape=(unit, unit),
-        in_specs=specs("s", "v", "v"),
+        in_specs=specs("s", "h", "h"),
         out_specs=specs("v", "v"),
+        scratch_shapes=[
+            pltpu.VMEM((9, 64, 1024), BF16),
+            pltpu.VMEM((3, 32, 1024), BF16),
+            pltpu.SemaphoreType.DMA((2,)),
+        ],
         compiler_params=params(16),
         cost_estimate=cost(10**9, 3 * 10**6),
     )(where, spatial, temporal)
@@ -145,28 +159,6 @@
     )(where, own, other)
 
 
-def pick_kernel(where, *refs):
-    core = where[3]
-    for index in range(2):
-        for side in range(2):
-
-            @pl.when(core == side)
-            def _(source=refs[index * 2 + side], target=refs[4 + index]):
-                target[...] = source[...]
-
-
-def pick(where, *units):
-    unit = jax.ShapeDtypeStruct((768, 256), BF16)
-    return pl.pallas_call(
-        pick_kernel,
-        out_shape=(unit, unit),
-        in_specs=specs(*"svvvv"),
-        out_specs=specs(*"vv"),
-        compiler_params=params(8),
-        cost_estimate=cost(0, 2 * 10**6),
-    )(where, *units)
-
-
 def stack_kernel(*refs):
     units, wholes = refs[:8], refs[8:]
     for index in range(8):
@@ -185,29 +177,24 @@
     )(*units)
 
 
-def divide_kernel(where, *refs):
-    core = where[3]
-    for index in range(2):
-        for side in range(2):
-
-            @pl.when(core == side)
-            def _(source=refs[index * 2 + side], spatial=refs[4 + index], temporal=refs[6 + index]):
-                for slot in range(4):
-                    spatial[slot] = source[slot, 0:576, :]
-                    temporal[slot] = source[slot, 576:768, :]
-
-
-def divide(where, *wholes):
+def divide_kernel(whole_a, whole_b, spatial_a, spatial_b, temporal_a, temporal_b):
+    for whole, spatial, temporal in ((whole_a, spatial_a, temporal_a), (whole_b, spatial_b, temporal_b)):
+        for slot in range(4):
+            spatial[slot] = whole[slot, 0:576, :]
+            temporal[slot] = whole[slot, 576:768, :]
+
+
+def divide(*wholes):
     spatial = jax.ShapeDtypeStruct((4, 576, 256), BF16)
     temporal = jax.ShapeDtypeStruct((4, 192, 256), BF16)
     return pl.pallas_call(
         divide_kernel,
         out_shape=(spatial, spatial, temporal, temporal),
-        in_specs=specs(*"svvvv"),
+        in_specs=specs(*"vv"),
         out_specs=specs(*"vvvv"),
-        compiler_params=params(16),
+        compiler_params=params(10),
         cost_estimate=cost(0, 6 * 10**6),
-    )(where, *wholes)
+    )(*wholes)
 
 
 def conv_kernel(step, colours, *refs):
@@ -229,13 +216,14 @@
     else:
         out, kernel = refs[:count], refs[count]
     y, z = where[0], where[1]
+    turn = 2 * where[3] - 1
     mine = (z, y)
     across = (y, z)
     lines = 6
     for number, colour in enumerate(colours):
-        block = (mine[colour] - step + 4) & 3
+        block = (mine[colour] + turn * step + 4) & 3
         for slot in range(4):
-            place = (across[colour] - slot + 4) & 3
+            place = (across[colour] + turn * slot + 4) & 3
             for tap in range(9):
                 kernel[number, pl.ds(pl.multiple_of(tap * 256 + place * 64, 64), 64), :] = pieces[number][
                     slot, tap * 64 : (tap + 1) * 64, :
@@ -340,11 +328,12 @@
 
 def place_weights(where, blocks, steps, first_row, targets):
     y, z = where[0], where[1]
+    turn = 2 * where[3] - 1
     for number, ref in enumerate(blocks):
         colour, step = number % 2, steps[number // 2]
         for unit in range(4):
             fixed, moving = (unit, step) if colour == 0 else (step, unit)
-            row, column = (y - fixed + 4) & 3, (z - moving + 4) & 3
+            row, column = (y + turn * fixed + 4) & 3, (z + turn * moving + 4) & 3
             place = pl.ds(pl.multiple_of((row * 4 + column) * 32, 32), 32)
             for half in range(2):
                 columns = slice((colour * 2 + half) * 256, (colour * 2 + half + 1) * 256)
@@ -467,20 +456,15 @@
     return shown.transpose(0, 3, 1, 2, 4)
 
 
-def ring(value, axis):
+def ring(value, axis, way=1):
     count = lax.axis_size(axis)
-    pairs = [(i * 2, (i + 1) % count * 2) for i in range(count)]
-    pairs += [(i * 2 + 1, (i - 1) % count * 2 + 1) for i in range(count)]
+    pairs = [(i * 2, (i + way) % count * 2) for i in range(count)]
+    pairs += [(i * 2 + 1, (i - way) % count * 2 + 1) for i in range(count)]
     return lax.ppermute(value, (axis, "core"), pairs)
 
 
 def after(value, *others):
     return lax.optimization_barrier((value, *others))[0]
-
-
-def step_to(value, axis, distance):
-    count = lax.axis_size(axis)
-    return lax.ppermute(value, axis, [(i, (i + distance) % count) for i in range(count)])
 
 
 def shards(video, norm_gain, spatial_weight, spatial_bias, temporal_weight):
@@ -489,25 +473,24 @@
     bias = spatial_bias.reshape(16, 2, 32)[:, where[3], :].reshape(1, 512)
     unit_a, unit_b = pack(where, spatial_weight, temporal_weight)
 
-    a1, b1 = step_to(unit_a, "y", 1), step_to(unit_b, "z", 1)
-    a3, b3 = step_to(unit_a, "y", -1), step_to(unit_b, "z", -1)
-    own, flat = norm(after(video, unit_a, unit_b, bias), norm_gain.reshape(1, 1024))
-    other = lax.ppermute(after(own, a1, b1, a3, b3), "core", swap)
-    a2, b2 = pick(where, after(a1, own, flat), a3, b1, b3)
-    a2, b2 = ring(a2, "y"), ring(b2, "z")
-    whole_a, whole_b = stack((unit_a, a1, a2, a3, unit_b, b1, b2, b3))
+    a1, b1 = ring(unit_a, "y"), ring(unit_b, "z")
+    a3, b3 = ring(unit_a, "y", -1), ring(unit_b, "z", -1)
+    a2, b2 = ring(a1, "y"), ring(b1, "z")
+    own, flat = norm(after(video, a1, b1, bias), norm_gain.reshape(1, 1024))
+    other = lax.ppermute(after(own, a2, b2, a3, b3), "core", swap)
+    whole_a, whole_b = stack((unit_a, a1, after(a2, own), a3, unit_b, b1, b2, b3))
 
     both = (0, 1)
-    whole_1 = step_to(whole_a, "z", 1), step_to(whole_b, "y", 1)
-    whole_3 = step_to(whole_a, "z", -1), step_to(whole_b, "y", -1)
+    whole_1 = ring(whole_a, "z"), ring(whole_b, "y")
     active = spread(where, after(own, whole_a), other)
+    whole_3 = ring(after(whole_a, active[0]), "z", -1), ring(after(whole_b, active[0]), "y", -1)
     sums = conv(0, both, where, active, (whole_a, whole_b))
-    sa, sb, ta, tb = divide(where, after(whole_1[0], sums[0]), whole_3[0], whole_1[1], whole_3[1])
+    sa, sb, ta, tb = divide(after(whole_1[0], sums[0]), whole_1[1])
     sa, sb = ring(sa, "z"), ring(sb, "y")
     sums = conv(1, both, where, active, whole_1, sums)
+    ta, tb = ring(after(ta, *whole_3), "z"), ring(after(tb, *whole_3), "y")
     sums = conv(3, both, where, active, whole_3, sums)
     weights = ready(where, (whole_a, whole_b, *whole_1, *whole_3))
-    ta, tb = ring(after(ta, sums[0]), "z"), ring(after(tb, sums[0]), "y")
     sa, sb = after(sa, sums[0], weights), after(sb, sums[0], weights)
     hidden_a, *sides = conv(2, (0,), where, active[:1], (sa,), sums[:1], bias)
     hidden_b, lower, upper = conv(2, (1,), where, active[1:], (sb,), sums[1:], bias, sides)

time: 124 us -> 113 us (0.911)
  waiting for transfers between devices: 35.4 us -> 22.1 us
  starting transfers between devices: 29.8 us -> 33.3 us
    ppermute x9 -> x1, waiting for transfers between devices: 27.8 us -> 0.63 us  [shards(): other = lax.ppermute(after(own, a2, b2, a3, b3), 'core', swap)]
    ppermute x6 -> x14, starting transfers between devices: 7.94 us -> 23.8 us  [ring(): return lax.ppermute(value, (axis, 'core'), pairs)]
    ppermute x6 -> x14, waiting for transfers between devices: 6.63 us -> 20.6 us  [ring(): return lax.ppermute(value, (axis, 'core'), pairs)]
    ppermute x9 -> x1, starting transfers between devices: 13.8 us -> 1.38 us  [shards(): other = lax.ppermute(after(own, a2, b2, a3, b3), 'core', swap)]
  transfers between devices with their start and end apart: 19 -> 19, of which waited for: 7 -> 7; matrix products, arithmetic and copies ran while one was open for 2% -> 2% of each run, Pallas kernels for 38% -> 42%
where the time goes in v3:
time: 113 us; the launch traced here: 112 us
  Pallas kernels  52 us (46%)
  starting transfers between devices  33.3 us (29%)
  waiting for transfers between devices  22.1 us (20%)
  local copies, waits for them, and re-layouts  4.69 us (4%)
    pallas_call x5, Pallas kernels, conv(): pl.pallas_call(functools.partial(conv_kernel, step, colours), out_shape=o...  25 us
    ppermute x14, starting transfers between devices, ring(): return lax.ppermute(value, (axis, 'core'), pairs)  23.8 us
    ppermute x14, waiting for transfers between devices, ring(): return lax.ppermute(value, (axis, 'core'), pairs)  20.6 us
    pallas_call x1, Pallas kernels, centre(): pl.pallas_call(centre_kernel, out_shape=(narrow, wide, wide, wide, jax.Sh...  9.03 us
    pallas_call x1, Pallas kernels, spread(): pl.pallas_call(spread_kernel, out_shape=(wide, wide), in_specs=specs('s',...  4.83 us
    pallas_call x1, Pallas kernels, finish(): pl.pallas_call(finish_kernel, grid=(2,), out_shape=jax.ShapeDtypeStruct((...  3.9 us
    ppermute x1, starting transfers between devices, shards(): before = lax.ppermute(upper, 'x', [(i, i + 1) for i in range(count - 1)])  3.15 us
    pallas_call x1, Pallas kernels, norm(): pl.pallas_call(norm_kernel, grid=(4,), out_shape=(jax.ShapeDtypeStruct((4...  2.58 us
  transfers between devices with their start and end apart: 19, of which 7 were waited for; matrix products, arithmetic and copies ran while one was open for 2% of the time, Pallas kernels for 42%

profile of v3, /device:TPU:1, one launch (start us, length us, event | category | flops | bytes accessed | tf_op | source)
XLA Modules:
  0.0 112.4 jit_solution(8918136731776488526)
XLA Ops:
  0.0 0.1 pad_add_fusion.where.refs_0_
  0.1 1.3 %copy-done = bf16[9,64,1024]{2,1,0:T(8,128)(2,1)S(1)} copy-done((bf16[9,64,1024]{2,1,0:T(8,128)(2,1)S(1)}, bf16[9,64,1024]{2,1,0:T(8,128)(2,1)}, u32[]{:S(2)}) %copy-start) | copy-done | bytes 1179672
  1.4 1.0 copy-done.1
  2.3 1.4 %shard_map.55 = (bf16[768,256]{1,0:T(8,128)(2,1)S(1)}, bf16[768,256]{1,0:T(8,128)(2,1)S(1)}) custom-call(s32[4]{0:T(128)S(1)} %pad_add_fusion.where.refs_0_, bf16[9,64,1024]{2,1,0:T(8,128)(2,1)S(1)} %copy-done, bf16[3,64,1024]{2,1,0:T(8,128)(2,1)S(1)} %copy-done.1), custom_call_target="tpu_custom_call" | custom-call | flops 1000000000 | bytes 3000000 | tf_op jit(solution)/shard_map/pallas_call | solution.py:67
  3.7 3.6 %collective-permute-start = (bf16[768,256]{1,0:T(8,128)(2,1)S(1)}, bf16[768,256]{1,0:T(8,128)(2,1)S(1)}, u32[]{:S(2)}, u32[]{:S(2)}) collective-permute-start(bf16[768,256]{1,0:T(8,128)(2,1)S(1)} %get-tuple-element.49.refs_0_), channel_id=1, source_target_pairs={{0,32},{32,64},{64,96},{96,0},{1,97},{33,1},{65,33},{97,65},{2,34}... | collective-permute-start | bytes 1179656 | tf_op jit(solution)/shard_map/ppermute | solution.py:463
  7.4 3.8 %collective-permute-start.1 = (bf16[768,256]{1,0:T(8,128)(2,1)S(1)}, bf16[768,256]{1,0:T(8,128)(2,1)S(1)}, u32[]{:S(2)}, u32[]{:S(2)}) collective-permute-start(bf16[768,256]{1,0:T(8,128)(2,1)S(1)} %get-tuple-element.50.refs_4_), channel_id=1, source_target_pairs={{0,8},{8,16},{16,24},{24,0},{1,25},{9,1},{17,9},{25,17},{2,10},{10... | collective-permute-start | bytes 1179656 | tf_op jit(solution)/shard_map/ppermute | solution.py:463
  11.1 0.0 collective-permute-start.3
  11.1 0.0 collective-permute-start.5
  11.1 1.8 %collective-permute-done.refs_1_ = bf16[768,256]{1,0:T(8,128)(2,1)S(1)} collective-permute-done((bf16[768,256]{1,0:T(8,128)(2,1)S(1)}, bf16[768,256]{1,0:T(8,128)(2,1)S(1)}, u32[]{:S(2)}, u32[]{:S(2)}) %collective-permute-start) | collective-permute-done | bytes 393248 | tf_op jit(solution)/shard_map/ppermute | solution.py:463
  13.0 3.4 %collective-permute-start.2 = (bf16[768,256]{1,0:T(8,128)(2,1)S(1)}, bf16[768,256]{1,0:T(8,128)(2,1)S(1)}, u32[]{:S(2)}, u32[]{:S(2)}) collective-permute-start(bf16[768,256]{1,0:T(8,128)(2,1)S(1)} %collective-permute-done.refs_1_), channel_id=1, source_target_pairs={{0,32},{32,64},{64,96},{96,0},{1,97},{33,1},{65,33},{97,65},{2,34}... | collective-permute-start | bytes 1179656 | tf_op jit(solution)/shard_map/ppermute | solution.py:463
  16.4 2.0 %collective-permute-done.1.refs_5_ = bf16[768,256]{1,0:T(8,128)(2,1)S(1)} collective-permute-done((bf16[768,256]{1,0:T(8,128)(2,1)S(1)}, bf16[768,256]{1,0:T(8,128)(2,1)S(1)}, u32[]{:S(2)}, u32[]{:S(2)}) %collective-permute-start.1) | collective-permute-done | bytes 393248 | tf_op jit(solution)/shard_map/ppermute | solution.py:463
  18.3 3.7 %collective-permute-start.4 = (bf16[768,256]{1,0:T(8,128)(2,1)S(1)}, bf16[768,256]{1,0:T(8,128)(2,1)S(1)}, u32[]{:S(2)}, u32[]{:S(2)}) collective-permute-start(bf16[768,256]{1,0:T(8,128)(2,1)S(1)} %collective-permute-done.1.refs_5_), channel_id=1, source_target_pairs={{0,8},{8,16},{16,24},{24,0},{1,25},{9,1},{17,9},{25,17},{2,10},{10... | collective-permute-start | bytes 1179656 | tf_op jit(solution)/shard_map/ppermute | solution.py:463
  22.1 0.0 copy-done.5
  22.1 0.1 reshape.6
  22.2 0.1 reshape_squeeze.3.refs_4_
  22.3 2.2 %copy.11.video = bf16[2,2,12,20,1024]{4,3,2,1,0:T(8,128)(2,1)S(1)} copy(bf16[2,2,12,20,1024]{4,1,3,2,0:T(2,128)(2,1)} %param.5) | data formatting | bytes 3932160 | tf_op jit(solution)/shard_map/optimization_barrier | solution.py:467
  24.5 0.0 copy-done.2
  24.5 2.6 %shard_map.56 = (bf16[4,240,1024]{2,1,0:T(8,128)(2,1)S(1)}, bf16[4,240,1024]{2,1,0:T(8,128)(2,1)S(1)}) custom-call(bf16[2,2,12,20,1024]{4,3,2,1,0:T(8,128)(2,1)S(1)} %copy.11.video, f32[1,1024]{1,0:T(1,128)S(1)} %bitcast.6), custom_call_target="tpu_custom_call" | custom-call | flops 2000000000 | bytes 20000000 | tf_op jit(solution)/shard_map/pallas_call | solution.py:94
  27.1 0.0 collective-permute-done.3.refs_3_
  27.1 0.0 collective-permute-done.5.refs_7_
  27.1 0.0 collective-permute-done.2.refs_2_
  27.1 0.0 collective-permute-done.4.refs_6_
  27.1 1.4 %collective-permute-start.6 = (bf16[4,240,1024]{2,1,0:T(8,128)(2,1)S(1)}, bf16[4,240,1024]{2,1,0:T(8,128)(2,1)S(1)}, u32[]{:S(2)}, u32[]{:S(2)}) collective-permute-start(bf16[4,240,1024]{2,1,0:T(8,128)(2,1)S(1)} %get-tuple-element.57.own), channel_id=1, source_target_pairs={{0,1},{1,0},{2,3},{3,2},{4,5},{5,4},{6,7},{7,6},{8,9},{9,8},{10,11... | collective-permute-start | bytes 5898248 | tf_op jit(solution)/shard_map/ppermute | solution.py:480
  28.5 0.2 shard_map.57
  28.7 1.8 %collective-permute-start.7 = (bf16[4,768,256]{2,1,0:T(8,128)(2,1)S(1)}, bf16[4,768,256]{2,1,0:T(8,128)(2,1)S(1)}, u32[]{:S(2)}, u32[]{:S(2)}) collective-permute-start(bf16[4,768,256]{2,1,0:T(8,128)(2,1)S(1)} %get-tuple-element.64.refs_3_.refs_0_), channel_id=1, source_target_pairs={{0,8},{8,16},{16,24},{24,0},{1,25},{9,1},{17,9},{25,17},{2,10},{10... | collective-permute-start | bytes 4718600 | tf_op jit(solution)/shard_map/ppermute | solution.py:463
  30.5 1.0 collective-permute-start.8
  31.5 0.6 collective-permute-done.6.other
  32.1 4.8 %shard_map.58 = (bf16[4,14,176,256]{3,2,1,0:T(8,128)(2,1)S(1)}, bf16[4,14,176,256]{3,2,1,0:T(8,128)(2,1)S(1)}) custom-call(s32[4]{0:T(128)S(1)} %pad_add_fusion.where.refs_0_, bf16[4,240,1024]{2,1,0:T(8,128)(2,1)S(1)} %get-tuple-element.57.own, bf16[4,240,1024]{2,1,0:T(8,128)(2,1)S(1)} %collective-permute-done.6.other), custom_call_target="tpu_custom_call" | custom-call | flops 2000000000 | bytes 25000000 | tf_op jit(solution)/shard_map/pallas_call | solution.py:151
  36.9 0.0 copy-start.3
  37.0 0.1 collective-permute-start.10
  37.0 1.0 collective-permute-start.11
  38.0 5.9 %shard_map.59 = (f32[1920,256]{1,0:T(8,128)S(1)}, f32[1920,256]{1,0:T(8,128)S(1)}) custom-call(s32[4]{0:T(128)S(1)} %pad_add_fusion.where.refs_0_, bf16[4,14,176,256]{3,2,1,0:T(8,128)(2,1)S(1)} %get-tuple-element.58.refs_1_, bf16[4,14,176,256]{3,2,1,0:T(8,128)(2,1)S(1)} %get-tuple-element.59.refs_2_.refs_1_, ...), custom_call_target="tpu_custom_call" | custom-call | flops 8000000000 | bytes 24000000 | tf_op jit(solution)/shard_map/pallas_call | solution.py:289
  43.9 12.1 %collective-permute-done.7.whole_a.refs_3_.refs_2_ = bf16[4,768,256]{2,1,0:T(8,128)(2,1)S(1)} collective-permute-done((bf16[4,768,256]{2,1,0:T(8,128)(2,1)S(1)}, bf16[4,768,256]{2,1,0:T(8,128)(2,1)S(1)}, u32[]{:S(2)}, u32[]{:S(2)}) %collective-permute-start.7) | collective-permute-done | bytes 1572896 | tf_op jit(solution)/shard_map/ppermute | solution.py:463
  56.1 1.5 %collective-permute-done.8.whole_b.refs_4_.refs_3_ = bf16[4,768,256]{2,1,0:T(8,128)(2,1)S(1)} collective-permute-done((bf16[4,768,256]{2,1,0:T(8,128)(2,1)S(1)}, bf16[4,768,256]{2,1,0:T(8,128)(2,1)S(1)}, u32[]{:S(2)}, u32[]{:S(2)}) %collective-permute-start.8) | collective-permute-done | bytes 1572896 | tf_op jit(solution)/shard_map/ppermute | solution.py:463
  57.5 0.2 shard_map.60
  57.7 1.6 %collective-permute-start.9 = (bf16[4,576,256]{2,1,0:T(8,128)(2,1)S(1)}, bf16[4,576,256]{2,1,0:T(8,128)(2,1)S(1)}, u32[]{:S(2)}, u32[]{:S(2)}) collective-permute-start(bf16[4,576,256]{2,1,0:T(8,128)(2,1)S(1)} %get-tuple-element.63), channel_id=1, source_target_pairs={{0,8},{8,16},{16,24},{24,0},{1,25},{9,1},{17,9},{25,17},{2,10},{10... | collective-permute-start | bytes 3538952 | tf_op jit(solution)/shard_map/ppermute | solution.py:463
  59.3 1.0 collective-permute-start.12
  60.2 0.0 copy-done.3
  60.3 5.9 %shard_map.61 = (f32[1920,256]{1,0:T(8,128)S(1)}, f32[1920,256]{1,0:T(8,128)S(1)}) custom-call(s32[4]{0:T(128)S(1)} %pad_add_fusion.where.refs_0_, bf16[4,14,176,256]{3,2,1,0:T(8,128)(2,1)S(1)} %get-tuple-element.58.refs_1_, bf16[4,14,176,256]{3,2,1,0:T(8,128)(2,1)S(1)} %get-tuple-element.59.refs_2_.refs_1_, ...), custom_call_target="tpu_custom_call", output_to_operand_aliasing={{0}: (5, {}), {1}: (6, {})} | custom-call | flops 8000000000 | bytes 24000000 | tf_op jit(solution)/shard_map/pallas_call | solution.py:289
  66.2 3.1 %collective-permute-done.10.refs_3_.refs_4_ = bf16[4,768,256]{2,1,0:T(8,128)(2,1)S(1)} collective-permute-done((bf16[4,768,256]{2,1,0:T(8,128)(2,1)S(1)}, bf16[4,768,256]{2,1,0:T(8,128)(2,1)S(1)}, u32[]{:S(2)}, u32[]{:S(2)}) %collective-permute-start.10) | collective-permute-done | bytes 1572896 | tf_op jit(solution)/shard_map/ppermute | solution.py:463
  69.3 0.0 collective-permute-done.11.refs_4_.refs_5_
  69.3 1.3 %collective-permute-start.14 = (bf16[4,192,256]{2,1,0:T(8,128)(2,1)S(1)}, bf16[4,192,256]{2,1,0:T(8,128)(2,1)S(1)}, u32[]{:S(2)}, u32[]{:S(2)}) collective-permute-start(bf16[4,192,256]{2,1,0:T(8,128)(2,1)S(1)} %get-tuple-element.83), channel_id=1, source_target_pairs={{0,32},{32,64},{64,96},{96,0},{1,97},{33,1},{65,33},{97,65},{2,34}... | collective-permute-start | bytes 1179656 | tf_op jit(solution)/shard_map/ppermute | solution.py:463
  70.6 1.7 %collective-permute-start.13 = (bf16[4,192,256]{2,1,0:T(8,128)(2,1)S(1)}, bf16[4,192,256]{2,1,0:T(8,128)(2,1)S(1)}, u32[]{:S(2)}, u32[]{:S(2)}) collective-permute-start(bf16[4,192,256]{2,1,0:T(8,128)(2,1)S(1)} %get-tuple-element.81), channel_id=1, source_target_pairs={{0,8},{8,16},{16,24},{24,0},{1,25},{9,1},{17,9},{25,17},{2,10},{10... | collective-permute-start | bytes 1179656 | tf_op jit(solution)/shard_map/ppermute | solution.py:463
  72.3 0.8 shard_map.63.weights
  73.1 5.9 %shard_map.62 = (f32[1920,256]{1,0:T(8,128)S(1)}, f32[1920,256]{1,0:T(8,128)S(1)}) custom-call(s32[4]{0:T(128)S(1)} %pad_add_fusion.where.refs_0_, bf16[4,14,176,256]{3,2,1,0:T(8,128)(2,1)S(1)} %bitcast.8, bf16[4,14,176,256]{3,2,1,0:T(8,128)(2,1)S(1)} %get-tuple-element.59.refs_2_.refs_1_, ...), custom_call_target="tpu_custom_call", output_to_operand_aliasing={{0}: (5, {}), {1}: (6, {})} | custom-call | flops 8000000000 | bytes 24000000 | tf_op jit(solution)/shard_map/pallas_call | solution.py:289
  79.1 0.0 collective-permute-done.9.refs_2_
  79.1 3.6 %shard_map.64 = (bf16[1920,256]{1,0:T(8,128)(2,1)S(1)}, bf16[2,2,240,256]{3,2,1,0:T(8,128)(2,1)S(1)}, bf16[2,2,240,256]{3,2,1,0:T(8,128)(2,1)S(1)}) custom-call(s32[4]{0:T(128)S(1)} %pad_add_fusion.where.refs_0_, bf16[4,14,176,256]{3,2,1,0:T(8,128)(2,1)S(1)} %copy-done.4, bf16[4,576,256]{2,1,0:T(8,128)(2,1)S(1)} %collective-permute-done.9.refs_2_, ...), custom_call_target="tpu_custom_call" | custom-call | flops 4000000000 | bytes 12000000 | tf_op jit(solution)/shard_map/pallas_call | solution.py:289
  82.7 0.0 collective-permute-done.12.refs_2_
  82.7 3.6 %shard_map.65 = (bf16[1920,256]{1,0:T(8,128)(2,1)S(1)}, bf16[2,2,240,256]{3,2,1,0:T(8,128)(2,1)S(1)}, bf16[2,2,240,256]{3,2,1,0:T(8,128)(2,1)S(1)}) custom-call(s32[4]{0:T(128)S(1)} %pad_add_fusion.where.refs_0_, bf16[4,14,176,256]{3,2,1,0:T(8,128)(2,1)S(1)} %get-tuple-element.59.refs_2_.refs_1_, bf16[4,576,256]{2,1,0:T(8,128)(2,1)S(1)} %collective-permute-done.12.refs_2_, ...), custom_call_target="tpu_custom_call" | custom-call | flops 4000000000 | bytes 12000000 | tf_op jit(solution)/shard_map/pallas_call | solution.py:289
  86.3 3.2 %collective-permute-start.16 = (bf16[2,2,240,256]{3,2,1,0:T(8,128)(2,1)S(1)}, bf16[2,2,240,256]{3,2,1,0:T(8,128)(2,1)S(1)}, u32[]{:S(2)}, u32[]{:S(2)}) collective-permute-start(bf16[2,2,240,256]{3,2,1,0:T(8,128)(2,1)S(1)} %get-tuple-element.86), channel_id=1, source_target_pairs={{0,2},{2,4},{4,6},{1,3},{3,5},{5,7},{8,10},{10,12},{12,14},{9,11},... | collective-permute-start | bytes 1474568 | tf_op jit(solution)/shard_map/ppermute | solution.py:498
  89.5 1.5 %collective-permute-start.17 = (bf16[2,2,240,256]{3,2,1,0:T(8,128)(2,1)S(1)}, bf16[2,2,240,256]{3,2,1,0:T(8,128)(2,1)S(1)}, u32[]{:S(2)}, u32[]{:S(2)}) collective-permute-start(bf16[2,2,240,256]{3,2,1,0:T(8,128)(2,1)S(1)} %get-tuple-element.89), channel_id=1, source_target_pairs={{2,0},{4,2},{6,4},{3,1},{5,3},{7,5},{10,8},{12,10},{14,12},{11,9},... | collective-permute-start | bytes 1474568 | tf_op jit(solution)/shard_map/ppermute | solution.py:499
  91.0 1.6 %shard_map.66 = (bf16[1920,512]{1,0:T(8,128)(2,1)S(1)}, bf16[1920,512]{1,0:T(8,128)(2,1)S(1)}) custom-call(bf16[1920,256]{1,0:T(8,128)(2,1)S(1)} %get-tuple-element.71.hidden_a, bf16[1920,256]{1,0:T(8,128)(2,1)S(1)} %get-tuple-element.77.hidden_b), custom_call_target="tpu_custom_call" | custom-call | flops 1000000000 | bytes 6000000 | tf_op jit(solution)/shard_map/pallas_call | solution.py:319
  92.6 0.0 collective-permute-done.14.block_b
  92.6 0.0 collective-permute-done.13.block_a
  92.6 9.0 %shard_map.67 = (bf16[2,240,1024]{2,1,0:T(8,128)(2,1)S(1)}, f32[2,240,1024]{2,1,0:T(8,128)S(1)}, f32[2,240,1024]{2,1,0:T(8,128)S(1)}, f32[2,240,1024]{2,1,0:T(8,128)S(1)}, bf16[2,512,1024]{2,1,0:T(8,128)(2,1)S(1)}) custom-call(s32[4]{0:T(128)S(1)} %pad_add_fusion.where.refs_0_, bf16[1920,256]{1,0:T(8,128)(2,1)S(1)} %get-tuple-element.71.hidden_a, ...), custom_call_target="tpu_custom_call" | custom-call | flops 10000000000 | bytes 12000000 | tf_op jit(solution)/shard_map/pallas_call | solution.py:394
  101.7 1.8 %collective-permute-start.15 = (bf16[2,240,1024]{2,1,0:T(8,128)(2,1)S(1)}, bf16[2,240,1024]{2,1,0:T(8,128)(2,1)S(1)}, u32[]{:S(2)}, u32[]{:S(2)}) collective-permute-start(bf16[2,240,1024]{2,1,0:T(8,128)(2,1)S(1)} %get-tuple-element.85), channel_id=1, source_target_pairs={{0,1},{1,0},{2,3},{3,2},{4,5},{5,4},{6,7},{7,6},{8,9},{9,8},{10,11... | collective-permute-start | bytes 2949128 | tf_op jit(solution)/shard_map/ppermute | solution.py:503
  103.5 0.0 collective-permute-done.16.before
  103.5 0.0 collective-permute-done.17.behind
  103.5 1.2 %shard_map.68 = bf16[2,240,1024]{2,1,0:T(8,128)(2,1)S(1)} custom-call(s32[4]{0:T(128)S(1)} %pad_add_fusion.where.refs_0_, bf16[2,2,240,256]{3,2,1,0:T(8,128)(2,1)S(1)} %collective-permute-done.16.before, bf16[2,2,240,256]{3,2,1,0:T(8,128)(2,1)S(1)} %collective-permute-done.17.behind, bf16[2,512,1024]{2,1,0:T(8,128)(2,1)S(1)} %get-tuple-element.87.weights, ...), custom_call_target="tpu_custom_call" | custom-call | flops 3000000000 | bytes 6000000 | tf_op jit(solution)/shard_map/pallas_call | solution.py:418
  104.7 1.6 %collective-permute-start.18 = (bf16[2,240,1024]{2,1,0:T(8,128)(2,1)S(1)}, bf16[2,240,1024]{2,1,0:T(8,128)(2,1)S(1)}, u32[]{:S(2)}, u32[]{:S(2)}) collective-permute-start(bf16[2,240,1024]{2,1,0:T(8,128)(2,1)S(1)} %shard_map.68), channel_id=1, source_target_pairs={{0,1},{1,0},{2,3},{3,2},{4,5},{5,4},{6,7},{7,6},{8,9},{9,8},{10,11... | collective-permute-start | bytes 2949128 | tf_op jit(solution)/shard_map/ppermute | solution.py:506
  106.3 1.2 %shard_map.69.rough_mine = f32[2,240,1024]{2,1,0:T(8,128)S(1)} custom-call(s32[4]{0:T(128)S(1)} %pad_add_fusion.where.refs_0_, bf16[2,2,240,256]{3,2,1,0:T(8,128)(2,1)S(1)} %collective-permute-done.16.before, bf16[2,2,240,256]{3,2,1,0:T(8,128)(2,1)S(1)} %collective-permute-done.17.behind, bf16[2,512,1024]{2,1,0:T(8,128)(2,1)S(1)} %get-tuple-element.87.weights, ...), custom_call_target="tpu_custom_call" | custom-call | flops 3000000000 | bytes 6000000 | tf_op jit(solution)/shard_map/pallas_call | solution.py:418
  107.6 0.0 collective-permute-done.15.calm_received
  107.6 1.0 collective-permute-done.18.rough_received
  108.5 3.9 %shard_map.70 = bf16[2,12,20,2,1024]{4,3,2,1,0:T(2,128)(2,1)} custom-call(s32[4]{0:T(128)S(1)} %pad_add_fusion.where.refs_0_, bf16[4,240,1024]{2,1,0:T(8,128)(2,1)S(1)} %get-tuple-element.52.video, f32[2,240,1024]{2,1,0:T(8,128)S(1)} %get-tuple-element.84.calm_mine, bf16[2,240,1024]{2,1,0:T(8,128)(2,1)S(1)} %collective-permute-done.15.calm_received, ...), custom_call_target="tpu_custom_call" | custom-call | flops 3000000 | bytes 10000000 | tf_op jit(solution)/shard_map/pallas_call | solution.py:446
  (12 shorter events, 0.1 us)
Async XLA Ops:
  0.0 22.1 %copy-start.5 = (f32[1024]{0:T(1024)S(1)}, f32[1024]{0:T(1024)}, u32[]{:S(2)}) copy-start(f32[1024]{0:T(1024)} %param.8) | copy-start | bytes 12292
  0.1 1.3 %copy-start = (bf16[9,64,1024]{2,1,0:T(8,128)(2,1)S(1)}, bf16[9,64,1024]{2,1,0:T(8,128)(2,1)}, u32[]{:S(2)}) copy-start(bf16[9,64,1024]{2,1,0:T(8,128)(2,1)} %spatial_hbm.1) | copy-start | bytes 3538948
  1.4 1.0 copy-start.1
  3.7 9.2 %collective-permute-start = (bf16[768,256]{1,0:T(8,128)(2,1)S(1)}, bf16[768,256]{1,0:T(8,128)(2,1)S(1)}, u32[]{:S(2)}, u32[]{:S(2)}) collective-permute-start(bf16[768,256]{1,0:T(8,128)(2,1)S(1)} %get-tuple-element.49.refs_0_), channel_id=1, source_target_pairs={{0,32},{32,64},{64,96},{96,0},{1,97},{33,1},{65,33},{97,65},{2,34}... | collective-permute-start | bytes 1179656 | tf_op jit(solution)/shard_map/ppermute | solution.py:463
  7.4 11.0 %collective-permute-start.1 = (bf16[768,256]{1,0:T(8,128)(2,1)S(1)}, bf16[768,256]{1,0:T(8,128)(2,1)S(1)}, u32[]{:S(2)}, u32[]{:S(2)}) collective-permute-start(bf16[768,256]{1,0:T(8,128)(2,1)S(1)} %get-tuple-element.50.refs_4_), channel_id=1, source_target_pairs={{0,8},{8,16},{16,24},{24,0},{1,25},{9,1},{17,9},{25,17},{2,10},{10... | collective-permute-start | bytes 1179656 | tf_op jit(solution)/shard_map/ppermute | solution.py:463
  11.1 16.0 %collective-permute-start.3 = (bf16[768,256]{1,0:T(8,128)(2,1)S(1)}, bf16[768,256]{1,0:T(8,128)(2,1)S(1)}, u32[]{:S(2)}, u32[]{:S(2)}) collective-permute-start(bf16[768,256]{1,0:T(8,128)(2,1)S(1)} %get-tuple-element.49.refs_0_), channel_id=1, source_target_pairs={{0,96},{32,0},{64,32},{96,64},{1,33},{33,65},{65,97},{97,1},{2,98}... | collective-permute-start | bytes 1179656 | tf_op jit(solution)/shard_map/ppermute | solution.py:463
  11.1 16.0 %collective-permute-start.5 = (bf16[768,256]{1,0:T(8,128)(2,1)S(1)}, bf16[768,256]{1,0:T(8,128)(2,1)S(1)}, u32[]{:S(2)}, u32[]{:S(2)}) collective-permute-start(bf16[768,256]{1,0:T(8,128)(2,1)S(1)} %get-tuple-element.50.refs_4_), channel_id=1, source_target_pairs={{0,24},{8,0},{16,8},{24,16},{1,9},{9,17},{17,25},{25,1},{2,26},{10... | collective-permute-start | bytes 1179656 | tf_op jit(solution)/shard_map/ppermute | solution.py:463
  13.0 14.2 %collective-permute-start.2 = (bf16[768,256]{1,0:T(8,128)(2,1)S(1)}, bf16[768,256]{1,0:T(8,128)(2,1)S(1)}, u32[]{:S(2)}, u32[]{:S(2)}) collective-permute-start(bf16[768,256]{1,0:T(8,128)(2,1)S(1)} %collective-permute-done.refs_1_), channel_id=1, source_target_pairs={{0,32},{32,64},{64,96},{96,0},{1,97},{33,1},{65,33},{97,65},{2,34}... | collective-permute-start | bytes 1179656 | tf_op jit(solution)/shard_map/ppermute | solution.py:463
  18.3 8.8 %collective-permute-start.4 = (bf16[768,256]{1,0:T(8,128)(2,1)S(1)}, bf16[768,256]{1,0:T(8,128)(2,1)S(1)}, u32[]{:S(2)}, u32[]{:S(2)}) collective-permute-start(bf16[768,256]{1,0:T(8,128)(2,1)S(1)} %collective-permute-done.1.refs_5_), channel_id=1, source_target_pairs={{0,8},{8,16},{16,24},{24,0},{1,25},{9,1},{17,9},{25,17},{2,10},{10... | collective-permute-start | bytes 1179656 | tf_op jit(solution)/shard_map/ppermute | solution.py:463
  22.3 2.2 %copy-start.2 = (f32[1024]{0:T(1024)S(1)}, f32[1024]{0:T(1024)}, u32[]{:S(2)}) copy-start(f32[1024]{0:T(1024)} %param.6) | copy-start | bytes 12292
  27.1 5.0 %collective-permute-start.6 = (bf16[4,240,1024]{2,1,0:T(8,128)(2,1)S(1)}, bf16[4,240,1024]{2,1,0:T(8,128)(2,1)S(1)}, u32[]{:S(2)}, u32[]{:S(2)}) collective-permute-start(bf16[4,240,1024]{2,1,0:T(8,128)(2,1)S(1)} %get-tuple-element.57.own), channel_id=1, source_target_pairs={{0,1},{1,0},{2,3},{3,2},{4,5},{5,4},{6,7},{7,6},{8,9},{9,8},{10,11... | collective-permute-start | bytes 5898248 | tf_op jit(solution)/shard_map/ppermute | solution.py:480
  28.7 27.3 %collective-permute-start.7 = (bf16[4,768,256]{2,1,0:T(8,128)(2,1)S(1)}, bf16[4,768,256]{2,1,0:T(8,128)(2,1)S(1)}, u32[]{:S(2)}, u32[]{:S(2)}) collective-permute-start(bf16[4,768,256]{2,1,0:T(8,128)(2,1)S(1)} %get-tuple-element.64.refs_3_.refs_0_), channel_id=1, source_target_pairs={{0,8},{8,16},{16,24},{24,0},{1,25},{9,1},{17,9},{25,17},{2,10},{10... | collective-permute-start | bytes 4718600 | tf_op jit(solution)/shard_map/ppermute | solution.py:463
  30.5 27.0 %collective-permute-start.8 = (bf16[4,768,256]{2,1,0:T(8,128)(2,1)S(1)}, bf16[4,768,256]{2,1,0:T(8,128)(2,1)S(1)}, u32[]{:S(2)}, u32[]{:S(2)}) collective-permute-start(bf16[4,768,256]{2,1,0:T(8,128)(2,1)S(1)} %get-tuple-element.65.refs_4_.refs_1_), channel_id=1, source_target_pairs={{0,32},{32,64},{64,96},{96,0},{1,97},{33,1},{65,33},{97,65},{2,34}... | collective-permute-start | bytes 4718600 | tf_op jit(solution)/shard_map/ppermute | solution.py:463
  36.9 23.3 %copy-start.3 = (bf16[4,14,176,256]{3,2,1,0:T(8,128)(2,1)}, bf16[4,14,176,256]{3,2,1,0:T(8,128)(2,1)S(1)}, u32[]{:S(2)}) copy-start(bf16[4,14,176,256]{3,2,1,0:T(8,128)(2,1)S(1)} %get-tuple-element.58.refs_1_) | copy-start | bytes 15138820
  37.0 32.4 %collective-permute-start.10 = (bf16[4,768,256]{2,1,0:T(8,128)(2,1)S(1)}, bf16[4,768,256]{2,1,0:T(8,128)(2,1)S(1)}, u32[]{:S(2)}, u32[]{:S(2)}) collective-permute-start(bf16[4,768,256]{2,1,0:T(8,128)(2,1)S(1)} %get-tuple-element.64.refs_3_.refs_0_), channel_id=1, source_target_pairs={{0,24},{8,0},{16,8},{24,16},{1,9},{9,17},{17,25},{25,1},{2,26},{10... | collective-permute-start | bytes 4718600 | tf_op jit(solution)/shard_map/ppermute | solution.py:463
  37.0 32.3 %collective-permute-start.11 = (bf16[4,768,256]{2,1,0:T(8,128)(2,1)S(1)}, bf16[4,768,256]{2,1,0:T(8,128)(2,1)S(1)}, u32[]{:S(2)}, u32[]{:S(2)}) collective-permute-start(bf16[4,768,256]{2,1,0:T(8,128)(2,1)S(1)} %get-tuple-element.65.refs_4_.refs_1_), channel_id=1, source_target_pairs={{0,96},{32,0},{64,32},{96,64},{1,33},{33,65},{65,97},{97,1},{2,98}... | collective-permute-start | bytes 4718600 | tf_op jit(solution)/shard_map/ppermute | solution.py:463
  57.7 21.3 %collective-permute-start.9 = (bf16[4,576,256]{2,1,0:T(8,128)(2,1)S(1)}, bf16[4,576,256]{2,1,0:T(8,128)(2,1)S(1)}, u32[]{:S(2)}, u32[]{:S(2)}) collective-permute-start(bf16[4,576,256]{2,1,0:T(8,128)(2,1)S(1)} %get-tuple-element.63), channel_id=1, source_target_pairs={{0,8},{8,16},{16,24},{24,0},{1,25},{9,1},{17,9},{25,17},{2,10},{10... | collective-permute-start | bytes 3538952 | tf_op jit(solution)/shard_map/ppermute | solution.py:463
  59.3 23.4 %collective-permute-start.12 = (bf16[4,576,256]{2,1,0:T(8,128)(2,1)S(1)}, bf16[4,576,256]{2,1,0:T(8,128)(2,1)S(1)}, u32[]{:S(2)}, u32[]{:S(2)}) collective-permute-start(bf16[4,576,256]{2,1,0:T(8,128)(2,1)S(1)} %get-tuple-element.72), channel_id=1, source_target_pairs={{0,32},{32,64},{64,96},{96,0},{1,97},{33,1},{65,33},{97,65},{2,34}... | collective-permute-start | bytes 3538952 | tf_op jit(solution)/shard_map/ppermute | solution.py:463
  69.3 3.8 %slice-start = ((s8[5046272]{0:T(1024)(128)(4,1)}), s8[4194304]{0:T(1024)(128)(4,1)S(1)}, s32[]{:S(2)}) async-start(s8[5046272]{0:T(1024)(128)(4,1)} %bitcast.7), calls=%async_computation | async-start | bytes 8388608
  69.3 3.8 %slice-start.1 = ((s8[5046272]{0:T(1024)(128)(4,1)}), s8[851968]{0:T(1024)(128)(4,1)S(1)}, s32[]{:S(2)}) async-start(s8[5046272]{0:T(1024)(128)(4,1)} %bitcast.7), calls=%async_computation.1 | async-start | bytes 1703936
  69.3 23.3 %collective-permute-start.14 = (bf16[4,192,256]{2,1,0:T(8,128)(2,1)S(1)}, bf16[4,192,256]{2,1,0:T(8,128)(2,1)S(1)}, u32[]{:S(2)}, u32[]{:S(2)}) collective-permute-start(bf16[4,192,256]{2,1,0:T(8,128)(2,1)S(1)} %get-tuple-element.83), channel_id=1, source_target_pairs={{0,32},{32,64},{64,96},{96,0},{1,97},{33,1},{65,33},{97,65},{2,34}... | collective-permute-start | bytes 1179656 | tf_op jit(solution)/shard_map/ppermute | solution.py:463
  70.6 22.0 %collective-permute-start.13 = (bf16[4,192,256]{2,1,0:T(8,128)(2,1)S(1)}, bf16[4,192,256]{2,1,0:T(8,128)(2,1)S(1)}, u32[]{:S(2)}, u32[]{:S(2)}) collective-permute-start(bf16[4,192,256]{2,1,0:T(8,128)(2,1)S(1)} %get-tuple-element.81), channel_id=1, source_target_pairs={{0,8},{8,16},{16,24},{24,0},{1,25},{9,1},{17,9},{25,17},{2,10},{10... | collective-permute-start | bytes 1179656 | tf_op jit(solution)/shard_map/ppermute | solution.py:463
  73.1 6.0 %copy-start.4 = (bf16[4,14,176,256]{3,2,1,0:T(8,128)(2,1)S(1)}, bf16[4,14,176,256]{3,2,1,0:T(8,128)(2,1)}, u32[]{:S(2)}) copy-start(bf16[4,14,176,256]{3,2,1,0:T(8,128)(2,1)} %copy-done.3) | copy-start | bytes 15138820
  86.3 17.2 %collective-permute-start.16 = (bf16[2,2,240,256]{3,2,1,0:T(8,128)(2,1)S(1)}, bf16[2,2,240,256]{3,2,1,0:T(8,128)(2,1)S(1)}, u32[]{:S(2)}, u32[]{:S(2)}) collective-permute-start(bf16[2,2,240,256]{3,2,1,0:T(8,128)(2,1)S(1)} %get-tuple-element.86), channel_id=1, source_target_pairs={{0,2},{2,4},{4,6},{1,3},{3,5},{5,7},{8,10},{10,12},{12,14},{9,11},... | collective-permute-start | bytes 1474568 | tf_op jit(solution)/shard_map/ppermute | solution.py:498
  89.5 14.0 %collective-permute-start.17 = (bf16[2,2,240,256]{3,2,1,0:T(8,128)(2,1)S(1)}, bf16[2,2,240,256]{3,2,1,0:T(8,128)(2,1)S(1)}, u32[]{:S(2)}, u32[]{:S(2)}) collective-permute-start(bf16[2,2,240,256]{3,2,1,0:T(8,128)(2,1)S(1)} %get-tuple-element.89), channel_id=1, source_target_pairs={{2,0},{4,2},{6,4},{3,1},{5,3},{7,5},{10,8},{12,10},{14,12},{11,9},... | collective-permute-start | bytes 1474568 | tf_op jit(solution)/shard_map/ppermute | solution.py:499
  101.7 5.9 %collective-permute-start.15 = (bf16[2,240,1024]{2,1,0:T(8,128)(2,1)S(1)}, bf16[2,240,1024]{2,1,0:T(8,128)(2,1)S(1)}, u32[]{:S(2)}, u32[]{:S(2)}) collective-permute-start(bf16[2,240,1024]{2,1,0:T(8,128)(2,1)S(1)} %get-tuple-element.85), channel_id=1, source_target_pairs={{0,1},{1,0},{2,3},{3,2},{4,5},{5,4},{6,7},{7,6},{8,9},{9,8},{10,11... | collective-permute-start | bytes 2949128 | tf_op jit(solution)/shard_map/ppermute | solution.py:503
  104.7 3.8 %collective-permute-start.18 = (bf16[2,240,1024]{2,1,0:T(8,128)(2,1)S(1)}, bf16[2,240,1024]{2,1,0:T(8,128)(2,1)S(1)}, u32[]{:S(2)}, u32[]{:S(2)}) collective-permute-start(bf16[2,240,1024]{2,1,0:T(8,128)(2,1)S(1)} %shard_map.68), channel_id=1, source_target_pairs={{0,1},{1,0},{2,3},{3,2},{4,5},{5,4},{6,7},{7,6},{8,9},{9,8},{10,11... | collective-permute-start | bytes 2949128 | tf_op jit(solution)/shard_map/ppermute | solution.py:506

commit v4 on v3

--- a/solution.py
+++ b/solution.py
@@ -34,28 +34,19 @@
     return pl.CostEstimate(flops=flops, bytes_accessed=bytes_accessed, transcendentals=0)
 
 
-def pack_kernel(where, spatial_hbm, temporal_hbm, unit_a, unit_b, spatial, temporal, sem):
+def pack_kernel(where, spatial, temporal, unit_a, unit_b):
     core = where[3]
-    half = pl.ds(pl.multiple_of(core * 32, 32), 32)
-    copies = [
-        pltpu.make_async_copy(spatial_hbm, spatial, sem.at[0]),
-        pltpu.make_async_copy(temporal_hbm.at[:, half, :], temporal, sem.at[1]),
-    ]
-    for copy in copies:
-        copy.start()
     source = lax.broadcasted_iota(jnp.int32, (256, 128), 0)
     target = lax.broadcasted_iota(jnp.int32, (256, 128), 1)
     wanted = (target >> 5) * 64 + (target & 31) + core * 32
     pick = jnp.where(source == wanted, 1.0, 0.0).astype(BF16)
-    for copy in copies:
-        copy.wait()
     for part in range(4):
         unit = (unit_a, unit_b)[part // 2]
         columns = spatial[:, :, part * 256 : (part + 1) * 256].reshape(576, 256)
         kept = jnp.dot(columns, pick, preferred_element_type=F32).astype(BF16)
         unit[0:576, (part % 2) * 128 : (part % 2 + 1) * 128] = kept
     for tap in range(3):
-        rows = temporal[tap]
+        rows = temporal[tap, pl.ds(pl.multiple_of(core * 32, 32), 32), :]
         for part in range(4):
             unit = (unit_a, unit_b)[part // 2]
             start = 576 + (part % 2) * 96 + tap * 32
@@ -67,13 +58,8 @@
     return pl.pallas_call(
         pack_kernel,
         out_shape=(unit, unit),
-        in_specs=specs("s", "h", "h"),
+        in_specs=specs("s", "v", "v"),
         out_specs=specs("v", "v"),
-        scratch_shapes=[
-            pltpu.VMEM((9, 64, 1024), BF16),
-            pltpu.VMEM((3, 32, 1024), BF16),
-            pltpu.SemaphoreType.DMA((2,)),
-        ],
         compiler_params=params(16),
         cost_estimate=cost(10**9, 3 * 10**6),
     )(where, spatial, temporal)
@@ -326,11 +312,12 @@
     )(*hidden)
 
 
-def place_weights(where, blocks, steps, first_row, targets):
+def place_weights(where, blocks, targets):
     y, z = where[0], where[1]
     turn = 2 * where[3] - 1
     for number, ref in enumerate(blocks):
-        colour, step = number % 2, steps[number // 2]
+        colour, step = number % 2, number // 2
+        first_row = 0 if step == 2 else 576
         for unit in range(4):
             fixed, moving = (unit, step) if colour == 0 else (step, unit)
             row, column = (y + turn * fixed + 4) & 3, (z + turn * moving + 4) & 3
@@ -342,27 +329,10 @@
                     target[place, columns] = ref[unit, start + tap * 32 : start + tap * 32 + 32, :]
 
 
-def ready_kernel(where, *refs):
-    blocks, weights = refs[:6], refs[6]
-    place_weights(where, blocks, (0, 1, 3), 576, [weights.at[tap] for tap in range(3)])
-
-
-def ready(where, blocks):
-    return pl.pallas_call(
-        ready_kernel,
-        out_shape=jax.ShapeDtypeStruct((3, 512, 1024), BF16),
-        in_specs=specs(*"svvvvvv"),
-        out_specs=pl.BlockSpec(memory_space=pltpu.VMEM),
-        compiler_params=params(18),
-        cost_estimate=cost(0, 5 * 10**6),
-    )(where, *blocks)
-
-
-def centre_kernel(where, hidden_a, hidden_b, earlier, later, weights, block_a, block_b, *refs):
-    calm_theirs, calm_mine, rough_theirs, rough_mine, edge, middle, total = refs
+def centre_kernel(where, hidden_a, hidden_b, earlier, later, *refs):
+    blocks, (calm_theirs, calm_mine, rough_theirs, rough_mine, edge, middle, total) = refs[:8], refs[8:]
     core = where[3]
-    edge[0], middle[...], edge[1] = weights[0], weights[1], weights[2]
-    place_weights(where, (block_a, block_b), (2,), 0, (edge.at[0], middle, edge.at[1]))
+    place_weights(where, blocks, (edge.at[0], middle, edge.at[1]))
     for part in range(4):
         columns = slice(part * 256, (part + 1) * 256)
         for group in range(2):
@@ -389,17 +359,17 @@
 PAIR = (2, ROWS * COLS, 1024)
 
 
-def centre(where, hidden, moved, weights, blocks):
+def centre(where, hidden, moved, blocks):
     wide, narrow = jax.ShapeDtypeStruct(PAIR, F32), jax.ShapeDtypeStruct(PAIR, BF16)
     return pl.pallas_call(
         centre_kernel,
         out_shape=(narrow, wide, wide, wide, jax.ShapeDtypeStruct((2, 512, 1024), BF16)),
-        in_specs=specs(*"svvvvvvv"),
+        in_specs=specs(*"svvvv", *"vvvvvvvv"),
         out_specs=specs(*"vvvvv"),
         scratch_shapes=[pltpu.VMEM((512, 1024), BF16), pltpu.VMEM((8, POINTS, 128), F32)],
-        compiler_params=params(32),
+        compiler_params=params(20),
         cost_estimate=cost(10**10, 12 * 10**6),
-    )(where, *hidden, *moved, weights, *blocks)
+    )(where, *hidden, *moved, *blocks)
 
 
 def edge_kernel(own, where, before, behind, weights, calm, result):
@@ -488,10 +458,11 @@
     sa, sb, ta, tb = divide(after(whole_1[0], sums[0]), whole_1[1])
     sa, sb = ring(sa, "z"), ring(sb, "y")
     sums = conv(1, both, where, active, whole_1, sums)
-    ta, tb = ring(after(ta, *whole_3), "z"), ring(after(tb, *whole_3), "y")
-    sums = conv(3, both, where, active, whole_3, sums)
-    weights = ready(where, (whole_a, whole_b, *whole_1, *whole_3))
-    sa, sb = after(sa, sums[0], weights), after(sb, sums[0], weights)
+    (sum_a,) = conv(3, (0,), where, active[:1], whole_3[:1], sums[:1])
+    ta, tb = ring(after(ta, *whole_3, sum_a), "z"), ring(after(tb, *whole_3, sum_a), "y")
+    (sum_b,) = conv(3, (1,), where, active[1:], whole_3[1:], sums[1:])
+    sums = [sum_a, sum_b]
+    sa, sb = after(sa, *sums), after(sb, *sums)
     hidden_a, *sides = conv(2, (0,), where, active[:1], (sa,), sums[:1], bias)
     hidden_b, lower, upper = conv(2, (1,), where, active[1:], (sb,), sums[1:], bias, sides)
     count = lax.axis_size("x")
@@ -499,7 +470,9 @@
     behind = lax.ppermute(lower, "x", [(i + 1, i) for i in range(count - 1)])
     hidden = hidden_a, hidden_b
     moved = shift(hidden)
-    calm_theirs, calm_mine, rough_theirs, rough_mine, weights = centre(where, hidden, moved, weights, (ta, tb))
+    calm_theirs, calm_mine, rough_theirs, rough_mine, weights = centre(
+        where, hidden, moved, (whole_a, whole_b, *whole_1, ta, tb, *whole_3)
+    )
     calm_received = lax.ppermute(calm_theirs, "core", swap)
     before = after(before, weights)
     sent = edges(False, where, before, behind, weights, rough_theirs)

time: 113 us -> 111 us (0.982)
  starting transfers between devices: 33.3 us -> 31.9 us
    ppermute x14, starting transfers between devices: 23.8 us -> 22.5 us  [ring(): return lax.ppermute(value, (axis, 'core'), pairs)]
    pallas_call x5 -> x6, Pallas kernels: 25 us -> 25.7 us  [conv(): pl.pallas_call(functools.partial(conv_kernel, step, colours), out_shape=o...]
    unnamed x16 -> x12, local copies, waits for them, and re-layouts: 2.29 us -> 2.28 us
  transfers between devices with their start and end apart: 19 -> 19, of which waited for: 7 -> 8; matrix products, arithmetic and copies ran while one was open for 2% -> 2% of each run, Pallas kernels for 42% -> 42%
where the time goes in v4:
time: 111 us
  Pallas kernels  51.7 us (47%)
  starting transfers between devices  31.9 us (29%)
  waiting for transfers between devices  22.3 us (20%)
  local copies, waits for them, and re-layouts  4.69 us (4%)
    pallas_call x6, Pallas kernels, conv(): pl.pallas_call(functools.partial(conv_kernel, step, colours), out_shape=o...  25.7 us
    ppermute x14, starting transfers between devices, ring(): return lax.ppermute(value, (axis, 'core'), pairs)  22.5 us
    ppermute x14, waiting for transfers between devices, ring(): return lax.ppermute(value, (axis, 'core'), pairs)  20.8 us
    pallas_call x1, Pallas kernels, centre(): pl.pallas_call(centre_kernel, out_shape=(narrow, wide, wide, wide, jax.Sh...  9.09 us
    pallas_call x1, Pallas kernels, spread(): pl.pallas_call(spread_kernel, out_shape=(wide, wide), in_specs=specs('s',...  4.83 us
    pallas_call x1, Pallas kernels, finish(): pl.pallas_call(finish_kernel, grid=(2,), out_shape=jax.ShapeDtypeStruct((...  4.02 us
    ppermute x1, starting transfers between devices, shards(): before = lax.ppermute(upper, 'x', [(i, i + 1) for i in range(count - 1)])  3.15 us
    pallas_call x1, Pallas kernels, norm(): pl.pallas_call(norm_kernel, grid=(4,), out_shape=(jax.ShapeDtypeStruct((4...  2.58 us
  transfers between devices with their start and end apart: 19, of which 8 were waited for; matrix products, arithmetic and copies ran while one was open for 2% of the time, Pallas kernels for 42%

profile of v4, /device:TPU:1, one launch (start us, length us, event | category | flops | bytes accessed | tf_op | source)
XLA Modules:
  0.0 111.0 jit_solution(14789147265862598857)
XLA Ops:
  0.0 0.1 pad_add_fusion.where.refs_0_
  0.1 1.3 %copy-done = bf16[9,64,1024]{2,1,0:T(8,128)(2,1)S(1)} copy-done((bf16[9,64,1024]{2,1,0:T(8,128)(2,1)S(1)}, bf16[9,64,1024]{2,1,0:T(8,128)(2,1)}, u32[]{:S(2)}) %copy-start) | copy-done | bytes 1179672
  1.4 1.0 copy-done.1
  2.3 1.0 shard_map.55
  3.4 3.6 %collective-permute-start = (bf16[768,256]{1,0:T(8,128)(2,1)S(1)}, bf16[768,256]{1,0:T(8,128)(2,1)S(1)}, u32[]{:S(2)}, u32[]{:S(2)}) collective-permute-start(bf16[768,256]{1,0:T(8,128)(2,1)S(1)} %get-tuple-element.47.refs_0_), channel_id=1, source_target_pairs={{0,32},{32,64},{64,96},{96,0},{1,97},{33,1},{65,33},{97,65},{2,34}... | collective-permute-start | bytes 1179656 | tf_op jit(solution)/shard_map/ppermute | solution.py:433
  7.0 3.8 %collective-permute-start.1 = (bf16[768,256]{1,0:T(8,128)(2,1)S(1)}, bf16[768,256]{1,0:T(8,128)(2,1)S(1)}, u32[]{:S(2)}, u32[]{:S(2)}) collective-permute-start(bf16[768,256]{1,0:T(8,128)(2,1)S(1)} %get-tuple-element.48.refs_4_), channel_id=1, source_target_pairs={{0,8},{8,16},{16,24},{24,0},{1,25},{9,1},{17,9},{25,17},{2,10},{10... | collective-permute-start | bytes 1179656 | tf_op jit(solution)/shard_map/ppermute | solution.py:433
  10.8 0.0 collective-permute-start.3
  10.8 0.0 collective-permute-start.5
  10.8 1.8 %collective-permute-done.refs_1_ = bf16[768,256]{1,0:T(8,128)(2,1)S(1)} collective-permute-done((bf16[768,256]{1,0:T(8,128)(2,1)S(1)}, bf16[768,256]{1,0:T(8,128)(2,1)S(1)}, u32[]{:S(2)}, u32[]{:S(2)}) %collective-permute-start) | collective-permute-done | bytes 393248 | tf_op jit(solution)/shard_map/ppermute | solution.py:433
  12.6 3.4 %collective-permute-start.2 = (bf16[768,256]{1,0:T(8,128)(2,1)S(1)}, bf16[768,256]{1,0:T(8,128)(2,1)S(1)}, u32[]{:S(2)}, u32[]{:S(2)}) collective-permute-start(bf16[768,256]{1,0:T(8,128)(2,1)S(1)} %collective-permute-done.refs_1_), channel_id=1, source_target_pairs={{0,32},{32,64},{64,96},{96,0},{1,97},{33,1},{65,33},{97,65},{2,34}... | collective-permute-start | bytes 1179656 | tf_op jit(solution)/shard_map/ppermute | solution.py:433
  16.0 2.0 %collective-permute-done.1.refs_5_ = bf16[768,256]{1,0:T(8,128)(2,1)S(1)} collective-permute-done((bf16[768,256]{1,0:T(8,128)(2,1)S(1)}, bf16[768,256]{1,0:T(8,128)(2,1)S(1)}, u32[]{:S(2)}, u32[]{:S(2)}) %collective-permute-start.1) | collective-permute-done | bytes 393248 | tf_op jit(solution)/shard_map/ppermute | solution.py:433
  18.0 3.7 %collective-permute-start.4 = (bf16[768,256]{1,0:T(8,128)(2,1)S(1)}, bf16[768,256]{1,0:T(8,128)(2,1)S(1)}, u32[]{:S(2)}, u32[]{:S(2)}) collective-permute-start(bf16[768,256]{1,0:T(8,128)(2,1)S(1)} %collective-permute-done.1.refs_5_), channel_id=1, source_target_pairs={{0,8},{8,16},{16,24},{24,0},{1,25},{9,1},{17,9},{25,17},{2,10},{10... | collective-permute-start | bytes 1179656 | tf_op jit(solution)/shard_map/ppermute | solution.py:433
  21.7 0.0 copy-done.5
  21.7 0.1 reshape.6
  21.8 0.1 reshape_squeeze.3.refs_4_
  21.9 2.2 %copy.11.video = bf16[2,2,12,20,1024]{4,3,2,1,0:T(8,128)(2,1)S(1)} copy(bf16[2,2,12,20,1024]{4,1,3,2,0:T(2,128)(2,1)} %param.5) | data formatting | bytes 3932160 | tf_op jit(solution)/shard_map/optimization_barrier | solution.py:437
  24.1 0.0 copy-done.2
  24.1 2.6 %shard_map.56 = (bf16[4,240,1024]{2,1,0:T(8,128)(2,1)S(1)}, bf16[4,240,1024]{2,1,0:T(8,128)(2,1)S(1)}) custom-call(bf16[2,2,12,20,1024]{4,3,2,1,0:T(8,128)(2,1)S(1)} %copy.11.video, f32[1,1024]{1,0:T(1,128)S(1)} %bitcast.6), custom_call_target="tpu_custom_call" | custom-call | flops 2000000000 | bytes 20000000 | tf_op jit(solution)/shard_map/pallas_call | solution.py:80
  26.7 0.0 collective-permute-done.3.refs_3_
  26.7 0.0 collective-permute-done.5.refs_7_
  26.7 0.0 collective-permute-done.2.refs_2_
  26.8 0.0 collective-permute-done.4.refs_6_
  26.8 1.4 %collective-permute-start.6 = (bf16[4,240,1024]{2,1,0:T(8,128)(2,1)S(1)}, bf16[4,240,1024]{2,1,0:T(8,128)(2,1)S(1)}, u32[]{:S(2)}, u32[]{:S(2)}) collective-permute-start(bf16[4,240,1024]{2,1,0:T(8,128)(2,1)S(1)} %get-tuple-element.55.own), channel_id=1, source_target_pairs={{0,1},{1,0},{2,3},{3,2},{4,5},{5,4},{6,7},{7,6},{8,9},{9,8},{10,11... | collective-permute-start | bytes 5898248 | tf_op jit(solution)/shard_map/ppermute | solution.py:450
  28.2 0.2 shard_map.57
  28.4 1.8 %collective-permute-start.7 = (bf16[4,768,256]{2,1,0:T(8,128)(2,1)S(1)}, bf16[4,768,256]{2,1,0:T(8,128)(2,1)S(1)}, u32[]{:S(2)}, u32[]{:S(2)}) collective-permute-start(bf16[4,768,256]{2,1,0:T(8,128)(2,1)S(1)} %get-tuple-element.62.refs_3_.refs_0_), channel_id=1, source_target_pairs={{0,8},{8,16},{16,24},{24,0},{1,25},{9,1},{17,9},{25,17},{2,10},{10... | collective-permute-start | bytes 4718600 | tf_op jit(solution)/shard_map/ppermute | solution.py:433
  30.2 1.0 collective-permute-start.8
  31.1 0.6 collective-permute-done.6.other
  31.8 4.8 %shard_map.58 = (bf16[4,14,176,256]{3,2,1,0:T(8,128)(2,1)S(1)}, bf16[4,14,176,256]{3,2,1,0:T(8,128)(2,1)S(1)}) custom-call(s32[4]{0:T(128)S(1)} %pad_add_fusion.where.refs_0_, bf16[4,240,1024]{2,1,0:T(8,128)(2,1)S(1)} %get-tuple-element.55.own, bf16[4,240,1024]{2,1,0:T(8,128)(2,1)S(1)} %collective-permute-done.6.other), custom_call_target="tpu_custom_call" | custom-call | flops 2000000000 | bytes 25000000 | tf_op jit(solution)/shard_map/pallas_call | solution.py:137
  36.6 0.0 copy-start.3
  36.6 0.1 collective-permute-start.10
  36.7 1.0 collective-permute-start.11
  37.6 5.9 %shard_map.59 = (f32[1920,256]{1,0:T(8,128)S(1)}, f32[1920,256]{1,0:T(8,128)S(1)}) custom-call(s32[4]{0:T(128)S(1)} %pad_add_fusion.where.refs_0_, bf16[4,14,176,256]{3,2,1,0:T(8,128)(2,1)S(1)} %get-tuple-element.56.refs_1_, bf16[4,14,176,256]{3,2,1,0:T(8,128)(2,1)S(1)} %get-tuple-element.57.refs_2_.refs_1_, ...), custom_call_target="tpu_custom_call" | custom-call | flops 8000000000 | bytes 24000000 | tf_op jit(solution)/shard_map/pallas_call | solution.py:275
  43.6 12.1 %collective-permute-done.7.whole_a.refs_3_.refs_2_ = bf16[4,768,256]{2,1,0:T(8,128)(2,1)S(1)} collective-permute-done((bf16[4,768,256]{2,1,0:T(8,128)(2,1)S(1)}, bf16[4,768,256]{2,1,0:T(8,128)(2,1)S(1)}, u32[]{:S(2)}, u32[]{:S(2)}) %collective-permute-start.7) | collective-permute-done | bytes 1572896 | tf_op jit(solution)/shard_map/ppermute | solution.py:433
  55.7 1.5 %collective-permute-done.8.whole_b.refs_4_.refs_3_ = bf16[4,768,256]{2,1,0:T(8,128)(2,1)S(1)} collective-permute-done((bf16[4,768,256]{2,1,0:T(8,128)(2,1)S(1)}, bf16[4,768,256]{2,1,0:T(8,128)(2,1)S(1)}, u32[]{:S(2)}, u32[]{:S(2)}) %collective-permute-start.8) | collective-permute-done | bytes 1572896 | tf_op jit(solution)/shard_map/ppermute | solution.py:433
  57.2 0.2 shard_map.60
  57.4 1.6 %collective-permute-start.9 = (bf16[4,576,256]{2,1,0:T(8,128)(2,1)S(1)}, bf16[4,576,256]{2,1,0:T(8,128)(2,1)S(1)}, u32[]{:S(2)}, u32[]{:S(2)}) collective-permute-start(bf16[4,576,256]{2,1,0:T(8,128)(2,1)S(1)} %get-tuple-element.61), channel_id=1, source_target_pairs={{0,8},{8,16},{16,24},{24,0},{1,25},{9,1},{17,9},{25,17},{2,10},{10... | collective-permute-start | bytes 3538952 | tf_op jit(solution)/shard_map/ppermute | solution.py:433
  58.9 1.0 collective-permute-start.12
  59.9 6.0 %shard_map.61 = (f32[1920,256]{1,0:T(8,128)S(1)}, f32[1920,256]{1,0:T(8,128)S(1)}) custom-call(s32[4]{0:T(128)S(1)} %pad_add_fusion.where.refs_0_, bf16[4,14,176,256]{3,2,1,0:T(8,128)(2,1)S(1)} %get-tuple-element.56.refs_1_, bf16[4,14,176,256]{3,2,1,0:T(8,128)(2,1)S(1)} %get-tuple-element.57.refs_2_.refs_1_, ...), custom_call_target="tpu_custom_call", output_to_operand_aliasing={{0}: (5, {}), {1}: (6, {})} | custom-call | flops 8000000000 | bytes 24000000 | tf_op jit(solution)/shard_map/pallas_call | solution.py:275
  65.9 3.1 %collective-permute-done.10.refs_2_.refs_6_ = bf16[4,768,256]{2,1,0:T(8,128)(2,1)S(1)} collective-permute-done((bf16[4,768,256]{2,1,0:T(8,128)(2,1)S(1)}, bf16[4,768,256]{2,1,0:T(8,128)(2,1)S(1)}, u32[]{:S(2)}, u32[]{:S(2)}) %collective-permute-start.10) | collective-permute-done | bytes 1572896 | tf_op jit(solution)/shard_map/ppermute | solution.py:433
  69.0 3.3 %shard_map.62.refs_3_ = f32[1920,256]{1,0:T(8,128)S(1)} custom-call(s32[4]{0:T(128)S(1)} %pad_add_fusion.where.refs_0_, bf16[4,14,176,256]{3,2,1,0:T(8,128)(2,1)S(1)} %get-tuple-element.56.refs_1_, bf16[4,768,256]{2,1,0:T(8,128)(2,1)S(1)} %collective-permute-done.10.refs_2_.refs_6_, ...), custom_call_target="tpu_custom_call", output_to_operand_aliasing={{}: (3, {})} | custom-call | flops 4000000000 | bytes 12000000 | tf_op jit(solution)/shard_map/pallas_call | solution.py:275
  72.2 0.0 collective-permute-done.11.refs_2_.refs_7_
  72.3 1.3 %collective-permute-start.14 = (bf16[4,192,256]{2,1,0:T(8,128)(2,1)S(1)}, bf16[4,192,256]{2,1,0:T(8,128)(2,1)S(1)}, u32[]{:S(2)}, u32[]{:S(2)}) collective-permute-start(bf16[4,192,256]{2,1,0:T(8,128)(2,1)S(1)} %get-tuple-element.79), channel_id=1, source_target_pairs={{0,32},{32,64},{64,96},{96,0},{1,97},{33,1},{65,33},{97,65},{2,34}... | collective-permute-start | bytes 1179656 | tf_op jit(solution)/shard_map/ppermute | solution.py:433
  73.6 0.4 collective-permute-start.13
  73.9 3.3 %shard_map.63.refs_3_ = f32[1920,256]{1,0:T(8,128)S(1)} custom-call(s32[4]{0:T(128)S(1)} %pad_add_fusion.where.refs_0_, bf16[4,14,176,256]{3,2,1,0:T(8,128)(2,1)S(1)} %get-tuple-element.57.refs_2_.refs_1_, bf16[4,768,256]{2,1,0:T(8,128)(2,1)S(1)} %collective-permute-done.11.refs_2_.refs_7_, ...), custom_call_target="tpu_custom_call", output_to_operand_aliasing={{}: (3, {})} | custom-call | flops 4000000000 | bytes 12000000 | tf_op jit(solution)/shard_map/pallas_call | solution.py:275
  77.2 0.3 collective-permute-done.9.refs_2_
  77.5 0.0 copy-done.4
  77.5 3.6 %shard_map.64 = (bf16[1920,256]{1,0:T(8,128)(2,1)S(1)}, bf16[2,2,240,256]{3,2,1,0:T(8,128)(2,1)S(1)}, bf16[2,2,240,256]{3,2,1,0:T(8,128)(2,1)S(1)}) custom-call(s32[4]{0:T(128)S(1)} %pad_add_fusion.where.refs_0_, bf16[4,14,176,256]{3,2,1,0:T(8,128)(2,1)S(1)} %copy-done.4, bf16[4,576,256]{2,1,0:T(8,128)(2,1)S(1)} %collective-permute-done.9.refs_2_, ...), custom_call_target="tpu_custom_call" | custom-call | flops 4000000000 | bytes 12000000 | tf_op jit(solution)/shard_map/pallas_call | solution.py:275
  81.1 0.0 collective-permute-done.12.refs_2_
  81.1 3.7 %shard_map.65 = (bf16[1920,256]{1,0:T(8,128)(2,1)S(1)}, bf16[2,2,240,256]{3,2,1,0:T(8,128)(2,1)S(1)}, bf16[2,2,240,256]{3,2,1,0:T(8,128)(2,1)S(1)}) custom-call(s32[4]{0:T(128)S(1)} %pad_add_fusion.where.refs_0_, bf16[4,14,176,256]{3,2,1,0:T(8,128)(2,1)S(1)} %get-tuple-element.57.refs_2_.refs_1_, bf16[4,576,256]{2,1,0:T(8,128)(2,1)S(1)} %collective-permute-done.12.refs_2_, ...), custom_call_target="tpu_custom_call" | custom-call | flops 4000000000 | bytes 12000000 | tf_op jit(solution)/shard_map/pallas_call | solution.py:275
  84.8 3.2 %collective-permute-start.16 = (bf16[2,2,240,256]{3,2,1,0:T(8,128)(2,1)S(1)}, bf16[2,2,240,256]{3,2,1,0:T(8,128)(2,1)S(1)}, u32[]{:S(2)}, u32[]{:S(2)}) collective-permute-start(bf16[2,2,240,256]{3,2,1,0:T(8,128)(2,1)S(1)} %get-tuple-element.82), channel_id=1, source_target_pairs={{0,2},{2,4},{4,6},{1,3},{3,5},{5,7},{8,10},{10,12},{12,14},{9,11},... | collective-permute-start | bytes 1474568 | tf_op jit(solution)/shard_map/ppermute | solution.py:469
  87.9 1.5 %collective-permute-start.17 = (bf16[2,2,240,256]{3,2,1,0:T(8,128)(2,1)S(1)}, bf16[2,2,240,256]{3,2,1,0:T(8,128)(2,1)S(1)}, u32[]{:S(2)}, u32[]{:S(2)}) collective-permute-start(bf16[2,2,240,256]{3,2,1,0:T(8,128)(2,1)S(1)} %get-tuple-element.85), channel_id=1, source_target_pairs={{2,0},{4,2},{6,4},{3,1},{5,3},{7,5},{10,8},{12,10},{14,12},{11,9},... | collective-permute-start | bytes 1474568 | tf_op jit(solution)/shard_map/ppermute | solution.py:470
  89.5 1.6 %shard_map.66 = (bf16[1920,512]{1,0:T(8,128)(2,1)S(1)}, bf16[1920,512]{1,0:T(8,128)(2,1)S(1)}) custom-call(bf16[1920,256]{1,0:T(8,128)(2,1)S(1)} %get-tuple-element.68.hidden_a, bf16[1920,256]{1,0:T(8,128)(2,1)S(1)} %get-tuple-element.73.hidden_b), custom_call_target="tpu_custom_call" | custom-call | flops 1000000000 | bytes 6000000 | tf_op jit(solution)/shard_map/pallas_call | solution.py:305
  91.1 0.0 collective-permute-done.14.refs_5_
  91.1 0.0 collective-permute-done.13.refs_4_
  91.1 9.1 %shard_map.67 = (bf16[2,240,1024]{2,1,0:T(8,128)(2,1)S(1)}, f32[2,240,1024]{2,1,0:T(8,128)S(1)}, f32[2,240,1024]{2,1,0:T(8,128)S(1)}, f32[2,240,1024]{2,1,0:T(8,128)S(1)}, bf16[2,512,1024]{2,1,0:T(8,128)(2,1)S(1)}) custom-call(s32[4]{0:T(128)S(1)} %pad_add_fusion.where.refs_0_, bf16[1920,256]{1,0:T(8,128)(2,1)S(1)} %get-tuple-element.68.hidden_a, ...), custom_call_target="tpu_custom_call" | custom-call | flops 10000000000 | bytes 12000000 | tf_op jit(solution)/shard_map/pallas_call | solution.py:364
  100.2 2.4 %collective-permute-start.15 = (bf16[2,240,1024]{2,1,0:T(8,128)(2,1)S(1)}, bf16[2,240,1024]{2,1,0:T(8,128)(2,1)S(1)}, u32[]{:S(2)}, u32[]{:S(2)}) collective-permute-start(bf16[2,240,1024]{2,1,0:T(8,128)(2,1)S(1)} %get-tuple-element.81), channel_id=1, source_target_pairs={{0,1},{1,0},{2,3},{3,2},{4,5},{5,4},{6,7},{7,6},{8,9},{9,8},{10,11... | collective-permute-start | bytes 2949128 | tf_op jit(solution)/shard_map/ppermute | solution.py:476
  102.6 0.0 collective-permute-done.16.before
  102.6 0.0 collective-permute-done.17.behind
  102.6 1.2 %shard_map.68 = bf16[2,240,1024]{2,1,0:T(8,128)(2,1)S(1)} custom-call(s32[4]{0:T(128)S(1)} %pad_add_fusion.where.refs_0_, bf16[2,2,240,256]{3,2,1,0:T(8,128)(2,1)S(1)} %collective-permute-done.16.before, bf16[2,2,240,256]{3,2,1,0:T(8,128)(2,1)S(1)} %collective-permute-done.17.behind, bf16[2,512,1024]{2,1,0:T(8,128)(2,1)S(1)} %get-tuple-element.83.weights, ...), custom_call_target="tpu_custom_call" | custom-call | flops 3000000000 | bytes 6000000 | tf_op jit(solution)/shard_map/pallas_call | solution.py:388
  103.8 1.0 collective-permute-start.18
  104.8 1.2 %shard_map.69.rough_mine = f32[2,240,1024]{2,1,0:T(8,128)S(1)} custom-call(s32[4]{0:T(128)S(1)} %pad_add_fusion.where.refs_0_, bf16[2,2,240,256]{3,2,1,0:T(8,128)(2,1)S(1)} %collective-permute-done.16.before, bf16[2,2,240,256]{3,2,1,0:T(8,128)(2,1)S(1)} %collective-permute-done.17.behind, bf16[2,512,1024]{2,1,0:T(8,128)(2,1)S(1)} %get-tuple-element.83.weights, ...), custom_call_target="tpu_custom_call" | custom-call | flops 3000000000 | bytes 6000000 | tf_op jit(solution)/shard_map/pallas_call | solution.py:388
  106.0 0.0 collective-permute-done.15.calm_received
  106.0 1.0 collective-permute-done.18.rough_received
  107.0 4.0 %shard_map.70 = bf16[2,12,20,2,1024]{4,3,2,1,0:T(2,128)(2,1)} custom-call(s32[4]{0:T(128)S(1)} %pad_add_fusion.where.refs_0_, bf16[4,240,1024]{2,1,0:T(8,128)(2,1)S(1)} %get-tuple-element.50.video, f32[2,240,1024]{2,1,0:T(8,128)S(1)} %get-tuple-element.80.calm_mine, bf16[2,240,1024]{2,1,0:T(8,128)(2,1)S(1)} %collective-permute-done.15.calm_received, ...), custom_call_target="tpu_custom_call" | custom-call | flops 3000000 | bytes 10000000 | tf_op jit(solution)/shard_map/pallas_call | solution.py:416
  (7 shorter events, 0.0 us)
Async XLA Ops:
  0.0 21.7 %copy-start.5 = (f32[1024]{0:T(1024)S(1)}, f32[1024]{0:T(1024)}, u32[]{:S(2)}) copy-start(f32[1024]{0:T(1024)} %param.8) | copy-start | bytes 12292
  0.1 1.3 %copy-start = (bf16[9,64,1024]{2,1,0:T(8,128)(2,1)S(1)}, bf16[9,64,1024]{2,1,0:T(8,128)(2,1)}, u32[]{:S(2)}) copy-start(bf16[9,64,1024]{2,1,0:T(8,128)(2,1)} %spatial.1) | copy-start | bytes 3538948
  1.4 1.0 copy-start.1
  3.4 9.2 %collective-permute-start = (bf16[768,256]{1,0:T(8,128)(2,1)S(1)}, bf16[768,256]{1,0:T(8,128)(2,1)S(1)}, u32[]{:S(2)}, u32[]{:S(2)}) collective-permute-start(bf16[768,256]{1,0:T(8,128)(2,1)S(1)} %get-tuple-element.47.refs_0_), channel_id=1, source_target_pairs={{0,32},{32,64},{64,96},{96,0},{1,97},{33,1},{65,33},{97,65},{2,34}... | collective-permute-start | bytes 1179656 | tf_op jit(solution)/shard_map/ppermute | solution.py:433
  7.0 11.0 %collective-permute-start.1 = (bf16[768,256]{1,0:T(8,128)(2,1)S(1)}, bf16[768,256]{1,0:T(8,128)(2,1)S(1)}, u32[]{:S(2)}, u32[]{:S(2)}) collective-permute-start(bf16[768,256]{1,0:T(8,128)(2,1)S(1)} %get-tuple-element.48.refs_4_), channel_id=1, source_target_pairs={{0,8},{8,16},{16,24},{24,0},{1,25},{9,1},{17,9},{25,17},{2,10},{10... | collective-permute-start | bytes 1179656 | tf_op jit(solution)/shard_map/ppermute | solution.py:433
  10.8 16.0 %collective-permute-start.3 = (bf16[768,256]{1,0:T(8,128)(2,1)S(1)}, bf16[768,256]{1,0:T(8,128)(2,1)S(1)}, u32[]{:S(2)}, u32[]{:S(2)}) collective-permute-start(bf16[768,256]{1,0:T(8,128)(2,1)S(1)} %get-tuple-element.47.refs_0_), channel_id=1, source_target_pairs={{0,96},{32,0},{64,32},{96,64},{1,33},{33,65},{65,97},{97,1},{2,98}... | collective-permute-start | bytes 1179656 | tf_op jit(solution)/shard_map/ppermute | solution.py:433
  10.8 16.0 %collective-permute-start.5 = (bf16[768,256]{1,0:T(8,128)(2,1)S(1)}, bf16[768,256]{1,0:T(8,128)(2,1)S(1)}, u32[]{:S(2)}, u32[]{:S(2)}) collective-permute-start(bf16[768,256]{1,0:T(8,128)(2,1)S(1)} %get-tuple-element.48.refs_4_), channel_id=1, source_target_pairs={{0,24},{8,0},{16,8},{24,16},{1,9},{9,17},{17,25},{25,1},{2,26},{10... | collective-permute-start | bytes 1179656 | tf_op jit(solution)/shard_map/ppermute | solution.py:433
  12.6 14.2 %collective-permute-start.2 = (bf16[768,256]{1,0:T(8,128)(2,1)S(1)}, bf16[768,256]{1,0:T(8,128)(2,1)S(1)}, u32[]{:S(2)}, u32[]{:S(2)}) collective-permute-start(bf16[768,256]{1,0:T(8,128)(2,1)S(1)} %collective-permute-done.refs_1_), channel_id=1, source_target_pairs={{0,32},{32,64},{64,96},{96,0},{1,97},{33,1},{65,33},{97,65},{2,34}... | collective-permute-start | bytes 1179656 | tf_op jit(solution)/shard_map/ppermute | solution.py:433
  18.0 8.8 %collective-permute-start.4 = (bf16[768,256]{1,0:T(8,128)(2,1)S(1)}, bf16[768,256]{1,0:T(8,128)(2,1)S(1)}, u32[]{:S(2)}, u32[]{:S(2)}) collective-permute-start(bf16[768,256]{1,0:T(8,128)(2,1)S(1)} %collective-permute-done.1.refs_5_), channel_id=1, source_target_pairs={{0,8},{8,16},{16,24},{24,0},{1,25},{9,1},{17,9},{25,17},{2,10},{10... | collective-permute-start | bytes 1179656 | tf_op jit(solution)/shard_map/ppermute | solution.py:433
  21.9 2.2 %copy-start.2 = (f32[1024]{0:T(1024)S(1)}, f32[1024]{0:T(1024)}, u32[]{:S(2)}) copy-start(f32[1024]{0:T(1024)} %param.6) | copy-start | bytes 12292
  26.8 5.0 %collective-permute-start.6 = (bf16[4,240,1024]{2,1,0:T(8,128)(2,1)S(1)}, bf16[4,240,1024]{2,1,0:T(8,128)(2,1)S(1)}, u32[]{:S(2)}, u32[]{:S(2)}) collective-permute-start(bf16[4,240,1024]{2,1,0:T(8,128)(2,1)S(1)} %get-tuple-element.55.own), channel_id=1, source_target_pairs={{0,1},{1,0},{2,3},{3,2},{4,5},{5,4},{6,7},{7,6},{8,9},{9,8},{10,11... | collective-permute-start | bytes 5898248 | tf_op jit(solution)/shard_map/ppermute | solution.py:450
  28.4 27.3 %collective-permute-start.7 = (bf16[4,768,256]{2,1,0:T(8,128)(2,1)S(1)}, bf16[4,768,256]{2,1,0:T(8,128)(2,1)S(1)}, u32[]{:S(2)}, u32[]{:S(2)}) collective-permute-start(bf16[4,768,256]{2,1,0:T(8,128)(2,1)S(1)} %get-tuple-element.62.refs_3_.refs_0_), channel_id=1, source_target_pairs={{0,8},{8,16},{16,24},{24,0},{1,25},{9,1},{17,9},{25,17},{2,10},{10... | collective-permute-start | bytes 4718600 | tf_op jit(solution)/shard_map/ppermute | solution.py:433
  30.2 27.0 %collective-permute-start.8 = (bf16[4,768,256]{2,1,0:T(8,128)(2,1)S(1)}, bf16[4,768,256]{2,1,0:T(8,128)(2,1)S(1)}, u32[]{:S(2)}, u32[]{:S(2)}) collective-permute-start(bf16[4,768,256]{2,1,0:T(8,128)(2,1)S(1)} %get-tuple-element.65.refs_4_.refs_1_), channel_id=1, source_target_pairs={{0,32},{32,64},{64,96},{96,0},{1,97},{33,1},{65,33},{97,65},{2,34}... | collective-permute-start | bytes 4718600 | tf_op jit(solution)/shard_map/ppermute | solution.py:433
  36.6 32.4 %copy-start.3 = (bf16[4,14,176,256]{3,2,1,0:T(8,128)(2,1)}, bf16[4,14,176,256]{3,2,1,0:T(8,128)(2,1)S(1)}, u32[]{:S(2)}) copy-start(bf16[4,14,176,256]{3,2,1,0:T(8,128)(2,1)S(1)} %get-tuple-element.56.refs_1_) | copy-start | bytes 15138820
  36.6 32.4 %collective-permute-start.10 = (bf16[4,768,256]{2,1,0:T(8,128)(2,1)S(1)}, bf16[4,768,256]{2,1,0:T(8,128)(2,1)S(1)}, u32[]{:S(2)}, u32[]{:S(2)}) collective-permute-start(bf16[4,768,256]{2,1,0:T(8,128)(2,1)S(1)} %get-tuple-element.62.refs_3_.refs_0_), channel_id=1, source_target_pairs={{0,24},{8,0},{16,8},{24,16},{1,9},{9,17},{17,25},{25,1},{2,26},{10... | collective-permute-start | bytes 4718600 | tf_op jit(solution)/shard_map/ppermute | solution.py:433
  36.7 35.6 %collective-permute-start.11 = (bf16[4,768,256]{2,1,0:T(8,128)(2,1)S(1)}, bf16[4,768,256]{2,1,0:T(8,128)(2,1)S(1)}, u32[]{:S(2)}, u32[]{:S(2)}) collective-permute-start(bf16[4,768,256]{2,1,0:T(8,128)(2,1)S(1)} %get-tuple-element.65.refs_4_.refs_1_), channel_id=1, source_target_pairs={{0,96},{32,0},{64,32},{96,64},{1,33},{33,65},{65,97},{97,1},{2,98}... | collective-permute-start | bytes 4718600 | tf_op jit(solution)/shard_map/ppermute | solution.py:433
  57.4 20.1 %collective-permute-start.9 = (bf16[4,576,256]{2,1,0:T(8,128)(2,1)S(1)}, bf16[4,576,256]{2,1,0:T(8,128)(2,1)S(1)}, u32[]{:S(2)}, u32[]{:S(2)}) collective-permute-start(bf16[4,576,256]{2,1,0:T(8,128)(2,1)S(1)} %get-tuple-element.61), channel_id=1, source_target_pairs={{0,8},{8,16},{16,24},{24,0},{1,25},{9,1},{17,9},{25,17},{2,10},{10... | collective-permute-start | bytes 3538952 | tf_op jit(solution)/shard_map/ppermute | solution.py:433
  58.9 22.2 %collective-permute-start.12 = (bf16[4,576,256]{2,1,0:T(8,128)(2,1)S(1)}, bf16[4,576,256]{2,1,0:T(8,128)(2,1)S(1)}, u32[]{:S(2)}, u32[]{:S(2)}) collective-permute-start(bf16[4,576,256]{2,1,0:T(8,128)(2,1)S(1)} %get-tuple-element.69), channel_id=1, source_target_pairs={{0,32},{32,64},{64,96},{96,0},{1,97},{33,1},{65,33},{97,65},{2,34}... | collective-permute-start | bytes 3538952 | tf_op jit(solution)/shard_map/ppermute | solution.py:433
  72.3 18.8 %collective-permute-start.14 = (bf16[4,192,256]{2,1,0:T(8,128)(2,1)S(1)}, bf16[4,192,256]{2,1,0:T(8,128)(2,1)S(1)}, u32[]{:S(2)}, u32[]{:S(2)}) collective-permute-start(bf16[4,192,256]{2,1,0:T(8,128)(2,1)S(1)} %get-tuple-element.79), channel_id=1, source_target_pairs={{0,32},{32,64},{64,96},{96,0},{1,97},{33,1},{65,33},{97,65},{2,34}... | collective-permute-start | bytes 1179656 | tf_op jit(solution)/shard_map/ppermute | solution.py:433
  73.6 17.5 %collective-permute-start.13 = (bf16[4,192,256]{2,1,0:T(8,128)(2,1)S(1)}, bf16[4,192,256]{2,1,0:T(8,128)(2,1)S(1)}, u32[]{:S(2)}, u32[]{:S(2)}) collective-permute-start(bf16[4,192,256]{2,1,0:T(8,128)(2,1)S(1)} %get-tuple-element.77), channel_id=1, source_target_pairs={{0,8},{8,16},{16,24},{24,0},{1,25},{9,1},{17,9},{25,17},{2,10},{10... | collective-permute-start | bytes 1179656 | tf_op jit(solution)/shard_map/ppermute | solution.py:433
  73.9 3.6 %copy-start.4 = (bf16[4,14,176,256]{3,2,1,0:T(8,128)(2,1)S(1)}, bf16[4,14,176,256]{3,2,1,0:T(8,128)(2,1)}, u32[]{:S(2)}) copy-start(bf16[4,14,176,256]{3,2,1,0:T(8,128)(2,1)} %copy-done.3) | copy-start | bytes 15138820
  84.8 17.8 %collective-permute-start.16 = (bf16[2,2,240,256]{3,2,1,0:T(8,128)(2,1)S(1)}, bf16[2,2,240,256]{3,2,1,0:T(8,128)(2,1)S(1)}, u32[]{:S(2)}, u32[]{:S(2)}) collective-permute-start(bf16[2,2,240,256]{3,2,1,0:T(8,128)(2,1)S(1)} %get-tuple-element.82), channel_id=1, source_target_pairs={{0,2},{2,4},{4,6},{1,3},{3,5},{5,7},{8,10},{10,12},{12,14},{9,11},... | collective-permute-start | bytes 1474568 | tf_op jit(solution)/shard_map/ppermute | solution.py:469
  87.9 14.7 %collective-permute-start.17 = (bf16[2,2,240,256]{3,2,1,0:T(8,128)(2,1)S(1)}, bf16[2,2,240,256]{3,2,1,0:T(8,128)(2,1)S(1)}, u32[]{:S(2)}, u32[]{:S(2)}) collective-permute-start(bf16[2,2,240,256]{3,2,1,0:T(8,128)(2,1)S(1)} %get-tuple-element.85), channel_id=1, source_target_pairs={{2,0},{4,2},{6,4},{3,1},{5,3},{7,5},{10,8},{12,10},{14,12},{11,9},... | collective-permute-start | bytes 1474568 | tf_op jit(solution)/shard_map/ppermute | solution.py:470
  100.2 5.8 %collective-permute-start.15 = (bf16[2,240,1024]{2,1,0:T(8,128)(2,1)S(1)}, bf16[2,240,1024]{2,1,0:T(8,128)(2,1)S(1)}, u32[]{:S(2)}, u32[]{:S(2)}) collective-permute-start(bf16[2,240,1024]{2,1,0:T(8,128)(2,1)S(1)} %get-tuple-element.81), channel_id=1, source_target_pairs={{0,1},{1,0},{2,3},{3,2},{4,5},{5,4},{6,7},{7,6},{8,9},{9,8},{10,11... | collective-permute-start | bytes 2949128 | tf_op jit(solution)/shard_map/ppermute | solution.py:476
  103.8 3.1 %collective-permute-start.18 = (bf16[2,240,1024]{2,1,0:T(8,128)(2,1)S(1)}, bf16[2,240,1024]{2,1,0:T(8,128)(2,1)S(1)}, u32[]{:S(2)}, u32[]{:S(2)}) collective-permute-start(bf16[2,240,1024]{2,1,0:T(8,128)(2,1)S(1)} %shard_map.68), channel_id=1, source_target_pairs={{0,1},{1,0},{2,3},{3,2},{4,5},{5,4},{6,7},{7,6},{8,9},{9,8},{10,11... | collective-permute-start | bytes 2949128 | tf_op jit(solution)/shard_map/ppermute | solution.py:479
